TPU v7x, 32 devices: a whole 2x2x4 slice. The times are simulated.
32 devices in a mesh: dp: 8 (over y, x, core), seq: 4 (over z).
Axes of the slice: x: 2, y: 2, z: 4, core: 2. Of those that a mesh axis runs over, the one named last changes fastest.
Arguments:
- tokens: bfloat16 [8, 1024, 1152], P('dp', 'seq'), may hold values from -6 to 6
- segment_ids: int32 [8, 1024], P('dp', 'seq'), may hold values from 0 to 2, as said below
- routes: int32 [8, 1024, 1], P('dp', 'seq'), may hold values from 0 to 3; in each aligned block of 256 rows (0 to 255, 256 to 511, ..., all dimensions but the last counted through in order) at most 128 rows name the same one
- cotangent: bfloat16 [8, 1024, 1152], P('dp', 'seq'), may hold values from -6 to 6
- small_params: bfloat16 [6912], P(('dp', 'seq'))
- w_in: bfloat16 [4608, 1152], P(('dp', 'seq')), may hold values from -0.1875 to 0.1875
- conv_w: bfloat16 [2304, 4], P(('dp', 'seq')), may hold values from -0.5 to 0.5
- conv_b: bfloat16 [2304], P(('dp', 'seq')), may hold values from -0.5 to 0.5
- w_x: bfloat16 [2304, 104], P(('dp', 'seq')), may hold values from -0.125 to 0.125
- w_dt: bfloat16 [2304, 72], P(('dp', 'seq')), may hold values from -0.75 to 0.75
- dt_bias: bfloat16 [2304], P(('dp', 'seq')), may hold values from -9 to -2
- a_log: bfloat16 [2304, 16], P(('dp', 'seq')), may hold values from 0 to 2.796875
- d_skip: bfloat16 [2304], P(('dp', 'seq')), may hold values from 0.5 to 1.5
- w_out: bfloat16 [2304, 1152], P(('dp', 'seq')), may hold values from -0.125 to 0.125
- w_up: bfloat16 [4, 1152, 3072], P(None, None, ('dp', 'seq')), may hold values from -0.1875 to 0.1875
- w_down: bfloat16 [4, 3072, 1152], P(None, ('dp', 'seq')), may hold values from -0.4375 to 0.4375
Outputs:
- mixed_out: bfloat16 [8, 1024, 1152], P('dp', 'seq')
- tokens_grad: bfloat16 [8, 1024, 1152], P('dp', 'seq')
- small_grad: float32 [6912], P(('dp', 'seq'))
- w_in_grad: float32 [4608, 1152], P(('dp', 'seq'))
- conv_w_grad: float32 [2304, 4], P(('dp', 'seq'))
- conv_b_grad: float32 [2304], P(('dp', 'seq'))
- w_x_grad: float32 [2304, 104], P(('dp', 'seq'))
- w_dt_grad: float32 [2304, 72], P(('dp', 'seq'))
- dt_bias_grad: float32 [2304], P(('dp', 'seq'))
- a_log_grad: float32 [2304, 16], P(('dp', 'seq'))
- d_skip_grad: float32 [2304], P(('dp', 'seq'))
- w_out_grad: float32 [2304, 1152], P(('dp', 'seq'))
- w_up_grad: float32 [4, 1152, 3072], P(None, None, ('dp', 'seq'))
- w_down_grad: float32 [4, 3072, 1152], P(None, ('dp', 'seq'))
Inputs may be any that keep to these rules, and one draw needn't show every extreme that they name: `segment_ids`: along a row the ids start at 0, never fall and rise by one at a time. `routes`: no expert is named by more than 128 of the rows of one device.
All inputs are finite; a program needn't handle non-finite values.
Results may differ from a plain program's by a relative error of at most 0.012.
Values may be sent and summed in bfloat16 or wider, within the bound.
A program may use at most 448 MiB of HBM per device.

v0:
```python
import math

import jax
import jax.numpy as jnp
from jax import lax
from jax.sharding import PartitionSpec as P

EPS = 1e-05


def from_behind(value, axis, steps):
    count = lax.axis_size(axis)
    first, last = (max(0, -steps), min(count, count - steps))
    return lax.ppermute(value, axis, [(source, source + steps) for source in range(first, last)])


def prefix(array, axis, combine, identity):
    size, mine = (lax.axis_size(axis), lax.axis_index(axis))
    everything = jax.tree.map(
        lambda part, kind: lax.all_gather(part.astype(kind), axis),
        array,
        (jnp.bfloat16, jnp.bfloat16),
    )
    start = jax.tree.map(
        lambda part, zero: jnp.broadcast_to(jnp.asarray(zero, part.dtype), part.shape),
        array,
        identity,
    )

    def prefix_turn(k, before):
        reached = k < mine
        new = combine(
            before, jax.tree.map(lambda part, own: part[k].astype(own.dtype), everything, array)
        )
        return jax.tree.map(lambda a, b: jnp.where(reached, a, b), new, before)

    return lax.fori_loop(0, size, prefix_turn, start)


def entering(array, axis, combine, identity):
    size, mine = (lax.axis_size(axis), lax.axis_index(axis))
    everything = jax.tree.map(
        lambda part, kind: lax.all_gather(part.astype(kind), axis),
        array,
        jax.tree.map(lambda a: jnp.bfloat16 if a.dtype == jnp.float32 else a.dtype, array),
    )
    start = jax.tree.map(
        lambda part, zero: jnp.broadcast_to(jnp.asarray(zero, part.dtype), part.shape),
        array,
        identity,
    )

    def entering_turn(k, before):
        at = size - 1 - k
        reached = at > mine
        new = combine(
            before, jax.tree.map(lambda part, own: part[at].astype(own.dtype), everything, array)
        )
        return jax.tree.map(lambda a, b: jnp.where(reached, a, b), new, before)

    return lax.fori_loop(0, size, entering_turn, start)


def rms_gain(value, gain):
    return value * lax.rsqrt(jnp.mean(value * value, axis=-1, keepdims=True) + EPS) * gain


def product(first_op, second_op):
    return jnp.dot(first_op, second_op, preferred_element_type=jnp.float32)


def product_tn(first_op, second_op):
    return lax.dot_general(
        first_op, second_op, (((0,), (0,)), ((), ())), preferred_element_type=jnp.float32
    )


def product_nt(first_op, second_op):
    return lax.dot_general(
        first_op, second_op, (((1,), (1,)), ((), ())), preferred_element_type=jnp.float32
    )


def exact_gelu(value):
    return jax.nn.gelu(value, approximate=False)


def chain_step(earlier, later):
    return (earlier[0] * later[0], later[0] * earlier[1] + later[1])


def pack_terms(term_list, dim_list, part_count):
    flat_list = [
        jnp.moveaxis(term, axis_pos, 0).reshape(part_count, -1)
        for term, axis_pos in zip(term_list, dim_list)
    ]
    joined = jnp.concatenate(flat_list, axis=1)
    width_all = joined.shape[1]
    padded_width = -(-width_all // 1024) * 1024
    joined = jnp.pad(joined, ((0, 0), (0, padded_width - width_all)))
    return joined.reshape(part_count * padded_width // 128, 128)


def unpack_terms(piece, term_list, dim_list, part_count):
    flat_piece = piece.reshape(-1)
    results = []
    offset = 0
    for term, axis_pos in zip(term_list, dim_list):
        moved_shape = jnp.moveaxis(term, axis_pos, 0).shape
        piece_shape = (moved_shape[0] // part_count,) + tuple(moved_shape[1:])
        piece_count = math.prod(piece_shape)
        block = flat_piece[offset : offset + piece_count].reshape(piece_shape)
        results.append(jnp.moveaxis(block, 0, axis_pos))
        offset = offset + piece_count
    return results


def state_scan(steps_dt, values, b_rows, c_rows, keep_mask, decay_rates):
    length = steps_dt.shape[0]
    block_len = math.gcd(32, length)

    def advance(cur_state, step_item):
        dt_now, value_now, b_now, c_now, keep_now = step_item
        cur_state = (
            jnp.exp(dt_now[None, :] * decay_rates) * keep_now * cur_state
            + b_now[:, None] * (dt_now * value_now)[None, :]
        )
        return (cur_state, jnp.sum(cur_state * c_now[:, None], axis=0))

    def block_run(cur_state, step_items):
        return lax.scan(advance, cur_state, step_items, unroll=True)

    step_items = (
        steps_dt.reshape(-1, block_len, steps_dt.shape[1]),
        values.reshape(-1, block_len, values.shape[1]),
        b_rows.reshape(-1, block_len, b_rows.shape[1]),
        c_rows.reshape(-1, block_len, c_rows.shape[1]),
        keep_mask.reshape(-1, block_len),
    )
    start_state = jnp.zeros((b_rows.shape[1], steps_dt.shape[1]), jnp.float32)
    final_state, outputs = lax.scan(jax.checkpoint(block_run), start_state, step_items)
    return (outputs.reshape(length, -1), final_state)


def conv_core(extended, conv_taps, conv_bias, same_mask):
    length = same_mask.shape[0]
    conv_sum = conv_bias
    for offset in range(conv_taps.shape[1]):
        conv_sum = (
            conv_sum
            + conv_taps[:, offset]
            * extended[offset : offset + length]
            * same_mask[:, offset][:, None]
        )
    return jax.nn.silu(conv_sum)


def gate_core(logits, onehot):
    return jnp.sum(jax.nn.softmax(logits, axis=-1) * onehot, axis=-1, keepdims=True)


def gate_mix(scanned, carried, values, z_vals, skip_gain):
    return (scanned + carried + skip_gain * values) * jax.nn.silu(z_vals)


def expert_work(slots, grad_slots, up_mat, down_mat):
    hidden = jnp.einsum("ecd,edf->ecf", slots, up_mat, preferred_element_type=jnp.float32)
    activated, gelu_pull = jax.vjp(exact_gelu, hidden)
    activated_b = activated.astype(jnp.bfloat16)
    out_part = jnp.einsum("ecf,efd->ecd", activated_b, down_mat, preferred_element_type=jnp.float32)
    grad_act = jnp.einsum("ecd,efd->ecf", grad_slots, down_mat, preferred_element_type=jnp.float32)
    grad_hidden = gelu_pull(grad_act)[0].astype(jnp.bfloat16)
    grad_down = jnp.einsum(
        "ecf,ecd->efd", activated_b, grad_slots, preferred_element_type=jnp.float32
    )
    grad_up = jnp.einsum("ecd,ecf->edf", slots, grad_hidden, preferred_element_type=jnp.float32)
    grad_disp = jnp.einsum("ecf,edf->ecd", grad_hidden, up_mat, preferred_element_type=jnp.float32)
    return (out_part, grad_disp, grad_up, grad_down)


def shards(
    tokens,
    segment_ids,
    routes,
    cotangent,
    small_params,
    w_in,
    conv_w,
    conv_b,
    w_x,
    w_dt,
    dt_bias,
    a_log,
    d_skip,
    w_out,
    w_up,
    w_down,
):
    mixer_parts = (small_params, w_in, conv_w, conv_b, w_x, w_dt, dt_bias, a_log, d_skip, w_out)
    gathered = (
        lax.all_gather(mixer_parts[0], ("dp", "seq"), axis=0, tiled=True),
        lax.all_gather(mixer_parts[1], ("dp", "seq"), axis=0, tiled=True),
        lax.all_gather(mixer_parts[2], ("dp", "seq"), axis=0, tiled=True),
        lax.all_gather(mixer_parts[3], ("dp", "seq"), axis=0, tiled=True),
        lax.all_gather(mixer_parts[4], ("dp", "seq"), axis=0, tiled=True),
        lax.all_gather(mixer_parts[5], ("dp", "seq"), axis=0, tiled=True),
        lax.all_gather(mixer_parts[6], ("dp", "seq"), axis=0, tiled=True),
        lax.all_gather(mixer_parts[7], ("dp", "seq"), axis=0, tiled=True),
        lax.all_gather(mixer_parts[8], ("dp", "seq"), axis=0, tiled=True),
        lax.all_gather(mixer_parts[9], ("dp", "seq"), axis=0, tiled=True),
    )
    (
        flat_small,
        full_in,
        full_conv,
        full_bias,
        full_x,
        full_dt,
        full_dtb,
        full_alog,
        full_skip,
        full_out,
    ) = gathered
    model_width = tokens.shape[2]
    tok_rows = tokens.shape[1]
    expert_count = w_up.shape[0]
    inner_width = full_in.shape[0] // 2
    rank_width = full_dt.shape[1]
    state_width = full_alog.shape[1]
    tap_count = full_conv.shape[1]
    capacity = tok_rows // 2
    tokens_f = tokens[0].astype(jnp.float32)
    seg_plus = segment_ids[0] + 1
    route_ids = routes[0, :, 0]
    gain_one = flat_small[:model_width].astype(jnp.float32)
    gain_two = flat_small[model_width : 2 * model_width].astype(jnp.float32)
    router_mat = flat_small[2 * model_width :].reshape(model_width, expert_count)
    normed, norm_pull = jax.vjp(rms_gain, tokens_f, gain_one)
    normed_b = normed.astype(jnp.bfloat16)
    mixed_in = product_nt(normed_b, full_in)
    conv_in = mixed_in[:, :inner_width].astype(jnp.bfloat16)
    z_vals = mixed_in[:, inner_width:]
    rim_x, rim_ids = from_behind(
        (
            conv_in[tok_rows - tap_count + 1 :],
            seg_plus[tok_rows - tap_count + 1 :].astype(jnp.bfloat16),
        ),
        "seq",
        1,
    )
    labels = seg_plus.astype(jnp.float32)
    all_labels = jnp.concatenate([rim_ids.astype(jnp.float32), labels])
    same_mask = jnp.stack(
        [all_labels[offset : offset + tok_rows] == labels for offset in range(tap_count)], axis=1
    ).astype(jnp.float32)
    keep_mask = (all_labels[tap_count - 2 : tap_count - 2 + tok_rows] == labels).astype(jnp.float32)
    keep_prefix = jnp.cumprod(keep_mask)
    extended = jnp.concatenate([rim_x, conv_in]).astype(jnp.float32)

    def conv_local(ext_vals, conv_taps, conv_bias):
        return conv_core(ext_vals, conv_taps, conv_bias, same_mask)

    values, conv_pull = jax.vjp(
        conv_local, extended, full_conv.astype(jnp.float32), full_bias.astype(jnp.float32)
    )
    values_b = values.astype(jnp.bfloat16)
    projected = product(values_b, full_x)
    low_rank = projected[:, :rank_width].astype(jnp.bfloat16)
    b_rows = projected[:, rank_width : rank_width + state_width]
    c_rows = projected[:, rank_width + state_width :]
    pre_dt = product_nt(low_rank, full_dt)
    bias_dt = full_dtb.astype(jnp.float32)
    steps_dt = jax.nn.softplus(pre_dt + bias_dt)
    log_rates = full_alog.astype(jnp.float32)
    skip_gain = full_skip.astype(jnp.float32)

    def scan_local(dt_arg, value_arg, b_arg, c_arg, rate_arg):
        return state_scan(dt_arg, value_arg, b_arg, c_arg, keep_mask, -jnp.exp(rate_arg.T))

    def carried_term(dt_arg, c_arg, rate_arg, start_arg):
        rates_now = -jnp.exp(rate_arg.T)
        running = jnp.cumsum(dt_arg, axis=0)
        total = jnp.zeros_like(dt_arg)
        for index in range(rates_now.shape[0]):
            total = (
                total
                + c_arg[:, index : index + 1]
                * jnp.exp(running * rates_now[index][None, :])
                * start_arg[index][None, :]
            )
        return total * keep_prefix[:, None]

    def last_carried(dt_arg, rate_arg, start_arg):
        rates_now = -jnp.exp(rate_arg.T)
        return jnp.exp(rates_now * jnp.sum(dt_arg, axis=0)[None, :]) * keep_prefix[-1] * start_arg

    scan_out, scan_pull = jax.vjp(scan_local, steps_dt, values, b_rows, c_rows, log_rates)
    scanned_local, own_state = scan_out
    decay_rates = -jnp.exp(log_rates.T)
    carry_all = jnp.exp(decay_rates * jnp.sum(steps_dt, axis=0)[None, :]) * keep_prefix[-1]
    empty_state = jnp.zeros((state_width, inner_width), jnp.float32)
    _, start_state = prefix(
        (carry_all, own_state), "seq", chain_step, (jnp.ones_like(carry_all), empty_state)
    )
    carried, carried_pull = jax.vjp(carried_term, steps_dt, c_rows, log_rates, start_state)
    gated, mix_pull = jax.vjp(gate_mix, scanned_local, carried, values, z_vals, skip_gain)
    gated_b = gated.astype(jnp.bfloat16)
    mixer_out = product(gated_b, full_out)
    first_sum = tokens_f + mixer_out
    normed_two, norm_two_pull = jax.vjp(rms_gain, first_sum, gain_two)
    normed_two_b = normed_two.astype(jnp.bfloat16)
    logits = product(normed_two_b, router_mat)
    onehot_int = (route_ids[:, None] == jnp.arange(expert_count)[None, :]).astype(jnp.int32)
    onehot = onehot_int.astype(jnp.float32)

    def gate_local(logit_arg):
        return gate_core(logit_arg, onehot)

    gate_prob, gate_pull = jax.vjp(gate_local, logits)
    slot_pos = jnp.sum((jnp.cumsum(onehot_int, axis=0) - onehot_int) * onehot_int, axis=1)
    slot_index = route_ids * capacity + slot_pos
    dispatched = (
        jnp.zeros((expert_count * capacity, model_width), jnp.bfloat16)
        .at[slot_index]
        .set(normed_two_b)
        .reshape(expert_count, capacity, model_width)
    )
    grad_out = cotangent[0].astype(jnp.float32)
    grad_expert = (gate_prob * grad_out).astype(jnp.bfloat16)
    grad_slots = (
        jnp.zeros((expert_count * capacity, model_width), jnp.bfloat16)
        .at[slot_index]
        .set(grad_expert)
        .reshape(expert_count, capacity, model_width)
    )
    full_up, full_down = (
        lax.all_gather(w_up, ("dp", "seq"), axis=2, tiled=True),
        lax.all_gather(w_down, ("dp", "seq"), axis=1, tiled=True),
    )
    expert_sum, grad_disp_slots, grad_up, grad_down = expert_work(
        dispatched, grad_slots, full_up, full_down
    )
    group_count = lax.axis_size(("dp", "seq"))
    expert_packed = pack_terms((grad_up, grad_down), (2, 1), group_count)
    expert_piece = lax.psum_scatter(expert_packed, ("dp", "seq"), scatter_dimension=0, tiled=True)
    expert_sums = unpack_terms(expert_piece, (grad_up, grad_down), (2, 1), group_count)
    expert_out = expert_sum.reshape(-1, model_width)[slot_index]
    grad_disp = grad_disp_slots.reshape(-1, model_width)[slot_index]
    result = first_sum + gate_prob * expert_out
    back_mixer = (
        lax.all_gather(mixer_parts[0], ("dp", "seq"), axis=0, tiled=True),
        lax.all_gather(mixer_parts[1], ("dp", "seq"), axis=0, tiled=True),
        lax.all_gather(mixer_parts[2], ("dp", "seq"), axis=0, tiled=True),
        lax.all_gather(mixer_parts[3], ("dp", "seq"), axis=0, tiled=True),
        lax.all_gather(mixer_parts[4], ("dp", "seq"), axis=0, tiled=True),
        lax.all_gather(mixer_parts[5], ("dp", "seq"), axis=0, tiled=True),
        lax.all_gather(mixer_parts[6], ("dp", "seq"), axis=0, tiled=True),
        lax.all_gather(mixer_parts[7], ("dp", "seq"), axis=0, tiled=True),
        lax.all_gather(mixer_parts[8], ("dp", "seq"), axis=0, tiled=True),
        lax.all_gather(mixer_parts[9], ("dp", "seq"), axis=0, tiled=True),
    )
    back_flat = back_mixer[0]
    back_in = back_mixer[1]
    back_x = back_mixer[4]
    back_dt = back_mixer[5]
    back_out = back_mixer[9]
    back_router = back_flat[2 * model_width :].reshape(model_width, expert_count)
    grad_gate = jnp.sum(grad_out * expert_out, axis=1, keepdims=True)
    grad_logits = gate_pull(grad_gate)[0].astype(jnp.bfloat16)
    grad_normed_two = grad_disp + product_nt(grad_logits, back_router)
    grad_router = product_tn(normed_two_b, grad_logits)
    grad_first_norm, grad_gain_two = norm_two_pull(grad_normed_two)
    grad_first = grad_out + grad_first_norm
    grad_mixer = grad_first.astype(jnp.bfloat16)
    grad_w_out = product_tn(gated_b, grad_mixer)
    grad_gated = product_nt(grad_mixer, back_out)
    grad_scanned, grad_carried, grad_values_mix, grad_z, grad_skip = mix_pull(grad_gated)
    grad_dt_one, grad_c_one, grad_rates_one, grad_start = carried_pull(grad_carried)
    _, grad_next = entering(
        (carry_all, grad_start), "seq", chain_step, (jnp.ones_like(carry_all), empty_state)
    )
    _, last_pull = jax.vjp(last_carried, steps_dt, log_rates, start_state)
    grad_dt_two, grad_rates_two, _ = last_pull(grad_next)
    grad_dt_scan, grad_values_scan, grad_b, grad_c_scan, grad_rates_scan = scan_pull(
        (grad_scanned, grad_next)
    )
    grad_steps = grad_dt_one + grad_dt_two + grad_dt_scan
    grad_c = grad_c_one + grad_c_scan
    grad_log_rates = grad_rates_one + grad_rates_two + grad_rates_scan
    grad_pre_full = grad_steps * jax.nn.sigmoid(pre_dt + bias_dt)
    grad_bias_dt = jnp.sum(grad_pre_full, axis=0)
    grad_pre = grad_pre_full.astype(jnp.bfloat16)
    grad_w_dt = product_tn(grad_pre, low_rank)
    grad_rank = product(grad_pre, back_dt)
    grad_proj = jnp.concatenate([grad_rank, grad_b, grad_c], axis=1).astype(jnp.bfloat16)
    grad_w_x = product_tn(values_b, grad_proj)
    grad_values = grad_values_mix + grad_values_scan + product_nt(grad_proj, back_x)
    grad_ext, grad_conv, grad_conv_bias = conv_pull(grad_values)
    rim_back = from_behind(grad_ext[: tap_count - 1], "seq", -1)
    grad_conv_in = grad_ext[tap_count - 1 :] + jnp.concatenate(
        [jnp.zeros((tok_rows - tap_count + 1, inner_width), jnp.float32), rim_back]
    )
    grad_mixed = jnp.concatenate([grad_conv_in, grad_z], axis=1).astype(jnp.bfloat16)
    grad_w_in = product_tn(grad_mixed, normed_b)
    grad_normed = product(grad_mixed, back_in)
    grad_tokens_norm, grad_gain_one = norm_pull(grad_normed)
    grad_tokens = grad_first + grad_tokens_norm
    grad_small = jnp.concatenate([grad_gain_one, grad_gain_two, grad_router.reshape(-1)])
    mixer_terms = (
        grad_small,
        grad_w_in,
        grad_conv,
        grad_conv_bias,
        grad_w_x,
        grad_w_dt,
        grad_bias_dt,
        grad_log_rates,
        grad_skip,
        grad_w_out,
    )
    mixer_dims = (0, 0, 0, 0, 0, 0, 0, 0, 0, 0)
    device_count = lax.axis_size(("dp", "seq"))
    mixer_packed = pack_terms(mixer_terms, mixer_dims, device_count)
    mixer_piece = lax.psum_scatter(mixer_packed, ("dp", "seq"), scatter_dimension=0, tiled=True)
    mixer_sums = unpack_terms(mixer_piece, mixer_terms, mixer_dims, device_count)
    return (
        result.astype(jnp.bfloat16)[None],
        grad_tokens.astype(jnp.bfloat16)[None],
        mixer_sums[0],
        mixer_sums[1],
        mixer_sums[2],
        mixer_sums[3],
        mixer_sums[4],
        mixer_sums[5],
        mixer_sums[6],
        mixer_sums[7],
        mixer_sums[8],
        mixer_sums[9],
        expert_sums[0],
        expert_sums[1],
    )


def solution(mesh):
    return jax.shard_map(
        shards,
        mesh=mesh,
        in_specs=(
            P("dp", "seq", None),
            P("dp", "seq"),
            P("dp", "seq", None),
            P("dp", "seq", None),
            P(("dp", "seq")),
            P(("dp", "seq"), None),
            P(("dp", "seq"), None),
            P(("dp", "seq")),
            P(("dp", "seq"), None),
            P(("dp", "seq"), None),
            P(("dp", "seq")),
            P(("dp", "seq"), None),
            P(("dp", "seq")),
            P(("dp", "seq"), None),
            P(None, None, ("dp", "seq")),
            P(None, ("dp", "seq"), None),
        ),
        out_specs=(
            P("dp", "seq", None),
            P("dp", "seq", None),
            P(("dp", "seq")),
            P(("dp", "seq"), None),
            P(("dp", "seq"), None),
            P(("dp", "seq")),
            P(("dp", "seq"), None),
            P(("dp", "seq"), None),
            P(("dp", "seq")),
            P(("dp", "seq"), None),
            P(("dp", "seq")),
            P(("dp", "seq"), None),
            P(None, None, ("dp", "seq")),
            P(None, ("dp", "seq"), None),
        ),
        check_vma=False,
    )
```

profile of v0, /device:TPU:9, one launch (start us, length us, event | category | flops | bytes accessed | tf_op | source)
XLA Modules:
  0.0 4364.9 jit_solution(14078896960394665266)
XLA Ops:
  18.2 40.7 all-reduce.62
  60.1 61.0 %all-gather.3 = bf16[32,72,4]{1,2,0:T(4,128)(2,1)S(1)} all-gather(bf16[1,72,4]{1,2,0:T(4,128)(2,1)S(1)} %bitcast.1373), channel_id=1, replica_groups=mesh['dp'=8,'seq'=4] {'dp','seq'}, dimensions={0}, use_global_device_ids=true | all-gather | bytes 19008 | tf_op jit(solution)/shard_map/all_gather | solution.py:203
  121.3 67.4 %all-gather.4 = bf16[32,72,16]{1,2,0:T(8,128)(2,1)S(1)} all-gather(bf16[1,72,16]{1,2,0:T(8,128)(2,1)S(1)} %bitcast.1367), channel_id=1, replica_groups=mesh['dp'=8,'seq'=4] {'dp','seq'}, dimensions={0}, use_global_device_ids=true | all-gather | bytes 76032 | tf_op jit(solution)/shard_map/all_gather | solution.py:208
  192.0 80.4 %all_gather.66 = bf16[2304,72]{1,0:T(8,128)(2,1)} all-gather(bf16[72,72]{1,0:T(8,128)(2,1)S(1)} %copy-done.127), channel_id=1, replica_groups=mesh['dp'=8,'seq'=4] {'dp','seq'}, dimensions={0}, use_global_device_ids=true | all-gather | bytes 342144 | tf_op jit(solution)/shard_map/all_gather | solution.py:206
  273.1 86.4 %all_gather.65 = bf16[2304,104]{1,0:T(8,128)(2,1)} all-gather(bf16[72,104]{1,0:T(8,128)(2,1)S(1)} %copy-done.128), channel_id=1, replica_groups=mesh['dp'=8,'seq'=4] {'dp','seq'}, dimensions={0}, use_global_device_ids=true | all-gather | bytes 494208 | tf_op jit(solution)/shard_map/all_gather | solution.py:205
  394.7 543.2 %while.70 = (s32[]{:T(128)}, f32[16,2304]{1,0:T(8,128)S(1)}, f32[8,32,2304]{2,1,0:T(8,128)}, f32[8,16,2304]{2,1,0:T(8,128)}, f32[8,32,2304]{2,1,0:T(8,128)}, /*i...) while((s32[]{:T(128)}, f32[16,2304]{1,0:T(8,128)S(1)}, ...), condition=%wide.region_34.35_spmd.clone, body=%wide.region_1.34_spmd.clone.sunk | while | flops 11317282 | bytes 11811733 | solution.py:141
  1154.5 22.7 fusion.181
  1186.3 1344.6 %while.73 = (s32[]{:T(128)}, f32[16,2304]{1,0:T(8,128)}, f32[16,2304]{1,0:T(8,128)S(1)}, f32[8,32,2304]{2,1,0:T(8,128)}, f32[8,32,2304]{2,1,0:T(8,128)}, /*index...) while((s32[]{:T(128)}, f32[16,2304]{1,0:T(8,128)}, ...), condition=%wide.region_201.202_spmd.clone, body=%wide.region_72.201_spmd.clone.sunk | while | flops 50097156 | bytes 35862116 | solution.py:141
  1305.8 22.8 select_add_fusion.2
  1473.8 22.8 select_add_fusion.2
  1641.8 22.8 select_add_fusion.2
  1701.9 22.2 multiply_reduce_fusion.288
  1809.8 22.8 select_add_fusion.2
  1869.9 22.2 multiply_reduce_fusion.288
  1977.8 22.8 select_add_fusion.2
  2145.8 22.8 select_add_fusion.2
  2313.8 22.8 select_add_fusion.2
  2481.8 22.8 select_add_fusion.2
  2624.2 63.9 %copy.145 = f32[3072,4,1152]{2,1,0:T(4,128)} copy(f32[3072,4,1152]{0,2,1:T(8,128)} %convolution_bitcast_fusion.1) | data formatting | bytes 113246208 | tf_op jit(solution)/shard_map/transpose | solution.py:94
  2688.1 73.8 %reshape.2411 = f32[32,442368]{1,0:T(8,128)} reshape(f32[3072,4,1152]{2,1,0:T(4,128)} %copy.145) | data formatting | bytes 113246208 | tf_op jit(solution)/shard_map/reshape | solution.py:94
  2761.9 62.3 %copy.147 = f32[3072,4,1152]{2,1,0:T(4,128)} copy(f32[3072,4,1152]{2,0,1:T(8,128)} %convolution_bitcast_fusion) | data formatting | bytes 113246208 | tf_op jit(solution)/shard_map/transpose | solution.py:94
  2824.2 74.3 %reshape.2412 = f32[32,442368]{1,0:T(8,128)} reshape(f32[3072,4,1152]{2,1,0:T(4,128)} %copy.147) | data formatting | bytes 113246208 | tf_op jit(solution)/shard_map/reshape | solution.py:94
  2918.1 22.3 reshape.2379
  2942.0 59.4 %dynamic-update-slice.5 = f32[32,263376]{1,0:T(8,128)} dynamic-update-slice(f32[32,263376]{1,0:T(8,128)} %dynamic-update-slice.4, f32[32,165888]{1,0:T(8,128)} %reshape.2379, s32[]{} %constant.600, s32[]{} %constant.601) | dynamic-update-slice | bytes 42467332
  3017.2 31.1 dynamic-update-slice.13
  3048.3 22.7 pad.229
  3071.1 31.7 reshape.2404
  3102.8 82.9 %pad_maximum_fusion = f32[32,884736]{1,0:T(8,128)} fusion(f32[32,442368]{1,0:T(8,128)} %reshape.2412, f32[32,442368]{1,0:T(8,128)} %reshape.2411), kind=kLoop, calls=%fused_computation.826 | loop fusion | flops 28311552 | bytes 226492416 | tf_op jit(solution)/shard_map/concatenate | solution.py:97
  3185.8 174.8 %reshape.2413 = f32[221184,128]{1,0:T(8,128)} reshape(f32[32,884736]{1,0:T(8,128)} %pad_maximum_fusion) | data formatting | bytes 226492416 | tf_op jit(solution)/shard_map/reshape | solution.py:101
  3363.6 72.2 %reduce-scatter.3.cloned.1.call-done = f32[2064,128]{1,0:T(8,128)} async-done(((f32[66048,128]{1,0:T(8,128)}), f32[2064,128]{1,0:T(8,128)}) %reduce-scatter.3.cloned.1.call-update) | async-done | bytes 1056784 | tf_op jit(solution)/shard_map/reduce_scatter | solution.py:424
  3445.9 55.1 %slice.2882 = f32[66048,4]{1,0:T(8,128)} reshape(f32[2064,128]{1,0:T(8,128)S(1)} %copy-done.44) | data formatting | bytes 2113536 | tf_op jit(solution)/shard_map/slice | solution.py:112
  3503.0 846.0 %reduce-scatter.5.cloned.1.call-done = f32[6912,128]{1,0:T(8,128)} async-done(((f32[221184,128]{1,0:T(8,128)}), f32[6912,128]{1,0:T(8,128)}) %reduce-scatter.5.cloned.1.call-update) | async-done | bytes 3538960 | tf_op jit(solution)/shard_map/reduce_scatter | solution.py:345
  (2105 shorter events, 2092.0 us)
Async XLA Ops:
  7.2 183.2 %copy-start.120 = (s32[1,256,1]{1,2,0:T(1,128)S(1)}, s32[1,256,1]{1,2,0:T(1,128)}, u32[]{:S(2)}) copy-start(s32[1,256,1]{1,2,0:T(1,128)} %param.26) | copy-start | bytes 3076
  7.2 114.0 %copy-start.213 = (bf16[72,16]{0,1:T(8,128)(2,1)S(1)}, bf16[72,16]{0,1:T(8,128)(2,1)}, u32[]{:S(2)}) copy-start(bf16[72,16]{0,1:T(8,128)(2,1)} %param.35) | copy-start | bytes 6916
  7.3 184.5 %copy-start.22 = (bf16[1,256,1152]{2,1,0:T(8,128)(2,1)S(1)}, bf16[1,256,1152]{2,1,0:T(8,128)(2,1)}, u32[]{:S(2)}) copy-start(bf16[1,256,1152]{2,1,0:T(8,128)(2,1)} %param.24) | copy-start | bytes 1769476
  7.3 353.8 %all-gather.10.cloned.1.call-start = ((), (), s32[]{:S(2)}) async-start(), calls=%async_computation.2 | async-start | bytes 10948608 | tf_op jit(solution)/shard_map/all_gather | solution.py:202
  8.0 982.5 %all-gather.12.cloned.1.call-start = ((), (), s32[]{:S(2)}) async-start(), calls=%async_computation.3 | async-start | bytes 5474304 | tf_op jit(solution)/shard_map/all_gather | solution.py:210
  8.8 183.3 %copy-start.127 = (bf16[72,72]{1,0:T(8,128)(2,1)S(1)}, bf16[72,72]{1,0:T(8,128)(2,1)}, u32[]{:S(2)}) copy-start(bf16[72,72]{1,0:T(8,128)(2,1)} %param.33) | copy-start | bytes 31108
  8.8 990.1 %all-gather.14.cloned.1.call-start = ((), (), s32[]{:S(2)}) async-start(), calls=%async_computation.4 | async-start | bytes 29196288 | tf_op jit(solution)/shard_map/all_gather | solution.py:337
  9.5 263.0 %copy-start.184 = (s32[1,256]{1,0:T(1,128)S(1)}, s32[1,256]{1,0:T(1,128)}, u32[]{:S(2)}) copy-start(s32[1,256]{1,0:T(1,128)} %param.25) | copy-start | bytes 3076
  9.5 263.6 %copy-start.128 = (bf16[72,104]{1,0:T(8,128)(2,1)S(1)}, bf16[72,104]{1,0:T(8,128)(2,1)}, u32[]{:S(2)}) copy-start(bf16[72,104]{1,0:T(8,128)(2,1)} %param.32) | copy-start | bytes 44932
  9.5 1022.6 %all-gather.16.cloned.1.call-start = ((), (), s32[]{:S(2)}) async-start(), calls=%async_computation.5 | async-start | bytes 29196288 | tf_op jit(solution)/shard_map/all_gather | solution.py:338
  10.1 3425.7 %reduce-scatter.3.cloned.1.call-start = ((), (), s32[]{:S(2)}) async-start(), calls=%async_computation.6 | async-start | bytes 34873344 | tf_op jit(solution)/shard_map/reduce_scatter | solution.py:424
  10.9 348.6 %collective-permute-start.1 = (bf16[3]{0:T(256)(128)(2,1)S(1)}, bf16[3]{0:T(256)(128)(2,1)S(1)}, u32[]{:S(2)}, u32[]{:S(2)}) collective-permute-start(bf16[3]{0:T(256)(128)(2,1)S(1)} %fusion.240), channel_id=1, source_target_pairs={{0,1},{1,2},{2,3},{4,5},{5,6},{6,7},{8,9},{9,10},{10,11},{12,13},{... | collective-permute-start | bytes 26 | tf_op jit(solution)/shard_map/ppermute | solution.py:14
  189.0 202.7 %copy-start.54 = (f32[2304,16]{0,1:T(8,128)}, f32[2304,16]{0,1:T(8,128)S(1)}, u32[]{:S(2)}) copy-start(f32[2304,16]{0,1:T(8,128)S(1)} %reshape.2471) | copy-start | bytes 442372
  190.4 169.9 %copy-start.214 = (s32[256,1]{0,1:T(1,128)}, s32[256,1]{0,1:T(1,128)S(1)}, u32[]{:S(2)}) copy-start(s32[256,1]{0,1:T(1,128)S(1)} %compare_select_fusion.2) | copy-start | bytes 3076
  191.8 189.8 %copy-start.86 = (f32[2304]{0:T(1024)}, f32[2304]{0:T(1024)S(1)}, u32[]{:S(2)}) copy-start(f32[2304]{0:T(1024)S(1)} %get-tuple-element.1360) | copy-start | bytes 27652
  191.8 189.8 %copy-start.88 = (f32[2304]{0:T(1024)}, f32[2304]{0:T(1024)S(1)}, u32[]{:S(2)}) copy-start(f32[2304]{0:T(1024)S(1)} %get-tuple-element.1361) | copy-start | bytes 27652
  191.8 189.8 %copy-start.90 = (f32[2304]{0:T(1024)}, f32[2304]{0:T(1024)S(1)}, u32[]{:S(2)}) copy-start(f32[2304]{0:T(1024)S(1)} %get-tuple-element.1362) | copy-start | bytes 27652
  191.8 189.8 %copy-start.92 = (f32[2304]{0:T(1024)}, f32[2304]{0:T(1024)S(1)}, u32[]{:S(2)}) copy-start(f32[2304]{0:T(1024)S(1)} %get-tuple-element.1363) | copy-start | bytes 27652
  192.0 167.4 %copy-start.182 = (f32[256]{0:T(256)}, f32[256]{0:T(256)S(1)}, u32[]{:S(2)}) copy-start(f32[256]{0:T(256)S(1)} %fusion.199) | copy-start | bytes 3076
  272.5 101.0 %copy-start.129 = (f32[256]{0:T(256)}, f32[256]{0:T(256)S(1)}, u32[]{:S(2)}) copy-start(f32[256]{0:T(256)S(1)} %fusion.238) | copy-start | bytes 3076
  273.1 100.4 %copy-start.69 = (f32[1152]{0:T(1024)}, f32[1152]{0:T(1024)S(1)}, u32[]{:S(2)}) copy-start(f32[1152]{0:T(1024)S(1)} %get-tuple-element.1805) | copy-start | bytes 13828
  373.5 7.8 collective-permute-start
  1191.5 109.4 %copy-start.4 = (f32[32,2304]{1,0:T(8,128)}, f32[32,2304]{1,0:T(8,128)S(1)}, u32[]{:S(2)}) copy-start(f32[32,2304]{1,0:T(8,128)S(1)} %dynamic-slice_bitcast_fusion.14) | copy-start | bytes 884740 | tf_op jit(solution)/shard_map/transpose(jvp())/while
  1359.5 109.4 %copy-start.4 = (f32[32,2304]{1,0:T(8,128)}, f32[32,2304]{1,0:T(8,128)S(1)}, u32[]{:S(2)}) copy-start(f32[32,2304]{1,0:T(8,128)S(1)} %dynamic-slice_bitcast_fusion.14) | copy-start | bytes 884740 | tf_op jit(solution)/shard_map/transpose(jvp())/while
  1527.5 109.4 %copy-start.4 = (f32[32,2304]{1,0:T(8,128)}, f32[32,2304]{1,0:T(8,128)S(1)}, u32[]{:S(2)}) copy-start(f32[32,2304]{1,0:T(8,128)S(1)} %dynamic-slice_bitcast_fusion.14) | copy-start | bytes 884740 | tf_op jit(solution)/shard_map/transpose(jvp())/while
  1695.5 109.4 %copy-start.4 = (f32[32,2304]{1,0:T(8,128)}, f32[32,2304]{1,0:T(8,128)S(1)}, u32[]{:S(2)}) copy-start(f32[32,2304]{1,0:T(8,128)S(1)} %dynamic-slice_bitcast_fusion.14) | copy-start | bytes 884740 | tf_op jit(solution)/shard_map/transpose(jvp())/while
  1863.5 109.4 %copy-start.4 = (f32[32,2304]{1,0:T(8,128)}, f32[32,2304]{1,0:T(8,128)S(1)}, u32[]{:S(2)}) copy-start(f32[32,2304]{1,0:T(8,128)S(1)} %dynamic-slice_bitcast_fusion.14) | copy-start | bytes 884740 | tf_op jit(solution)/shard_map/transpose(jvp())/while
  2031.5 109.4 %copy-start.4 = (f32[32,2304]{1,0:T(8,128)}, f32[32,2304]{1,0:T(8,128)S(1)}, u32[]{:S(2)}) copy-start(f32[32,2304]{1,0:T(8,128)S(1)} %dynamic-slice_bitcast_fusion.14) | copy-start | bytes 884740 | tf_op jit(solution)/shard_map/transpose(jvp())/while
  2199.5 109.4 %copy-start.4 = (f32[32,2304]{1,0:T(8,128)}, f32[32,2304]{1,0:T(8,128)S(1)}, u32[]{:S(2)}) copy-start(f32[32,2304]{1,0:T(8,128)S(1)} %dynamic-slice_bitcast_fusion.14) | copy-start | bytes 884740 | tf_op jit(solution)/shard_map/transpose(jvp())/while
  2367.5 109.4 %copy-start.4 = (f32[32,2304]{1,0:T(8,128)}, f32[32,2304]{1,0:T(8,128)S(1)}, u32[]{:S(2)}) copy-start(f32[32,2304]{1,0:T(8,128)S(1)} %dynamic-slice_bitcast_fusion.14) | copy-start | bytes 884740 | tf_op jit(solution)/shard_map/transpose(jvp())/while
  2599.7 298.8 %collective-permute-start.2 = (f32[3,2304]{1,0:T(4,128)S(1)}, f32[3,2304]{1,0:T(4,128)S(1)}, u32[]{:S(2)}, u32[]{:S(2)}) collective-permute-start(f32[3,2304]{1,0:T(4,128)S(1)} %pad_add_fusion.1), channel_id=1, source_target_pairs={{1,0},{2,1},{3,2},{5,4},{6,5},{7,6},{9,8},{10,9},{11,10},{13,12},{... | collective-permute-start | bytes 82952 | tf_op jit(solution)/shard_map/ppermute | solution.py:14
  3102.8 1246.2 %reduce-scatter.5.cloned.1.call-start = ((), (), s32[]{:S(2)}) async-start(), calls=%async_computation.7 | async-start | bytes 116785152 | tf_op jit(solution)/shard_map/reduce_scatter | solution.py:345
  (288 other events, 3532.4 us)
Sparse Core Ops, SparseCore 0:
  10.9 89.0 all-gather.9
  102.8 65.4 all-gather.11
  171.3 182.5 all-gather.13
  356.9 169.1 all-gather.15
  3102.9 332.8 reduce-scatter.2
  3442.1 906.8 reduce-scatter.4
where the time goes:
time: 4410 us; the launch traced here: 4360 us
  other arithmetic  1580 us (36%)
  local copies, waits for them, and re-layouts  1270 us (29%)
  waiting for transfers between devices  925 us (21%)
  blocking collectives  370 us (8%)
  matrix products  181 us (4%)
    reduce_scatter x1, waiting for transfers between devices, shards(): lax.psum_scatter(expert_packed, ('dp', 'seq'), scatter_dimension=0, tiled...  846 us
    reduce_sum x128, other arithmetic, advance(): dt_now[None, :] * decay_rates  492 us
    reduce_sum x80, other arithmetic, advance(): return (cur_state, jnp.sum(cur_state * c_now[:, None], axis=0))  441 us
    reshape x2, local copies, waits for them, and re-layouts, pack_terms(): return joined.reshape(part_count * padded_width // 128, 128)  207 us
    reshape x12, local copies, waits for them, and re-layouts, pack_terms(): jnp.moveaxis(term, axis_pos, 0).reshape(part_count, -1)  186 us
    add_any x8, other arithmetic, state_scan(): lax.scan(jax.checkpoint(block_run), start_state, step_items)  183 us
    concatenate x40, local copies, waits for them, and re-layouts, block_run(): return lax.scan(advance, cur_state, step_items, unroll=True)  173 us
    reduce_sum x88, other arithmetic, advance(): b_now[:, None] * (dt_now * value_now)[None, :]  153 us
  transfers between devices with their start and end apart: 9, of which 3 were waited for; matrix products, arithmetic and copies ran while one was open for 29% of the time, Pallas kernels for 0%

commit v1 on v0

v1 whole, which is shorter than its diff:
```python
import functools
import math

import jax
import jax.numpy as jnp
from jax import lax
from jax.experimental import pallas as pl
from jax.experimental.pallas import tpu as pltpu
from jax.sharding import PartitionSpec as P

F32, BF = jnp.float32, jnp.bfloat16
EPS = 1e-05
STEP = 16
VM = 56 * 1024 * 1024
MESH = pl.DeviceIdType.MESH
NT = (((1,), (1,)), ((), ()))
TN = (((0,), (0,)), ((), ()))


def rowb(block, i, n):
    return jnp.broadcast_to(block[i:i+1, :], (n, block.shape[1]))

def state_kernel(n, dte_ref, dtx_ref, rate_ref, b_ref, state_ref, carry_ref):
    rows, wide = dte_ref.shape
    tiles = wide // 128
    rates = [rate_ref[:, j*128:(j+1)*128] for j in range(tiles)]
    def block(k, carry):
        state, total = carry
        at = pl.multiple_of(k * STEP, STEP)
        dte = dte_ref[pl.ds(at, STEP), :]
        dtx = dtx_ref[pl.ds(at, STEP), :]
        state = list(state)
        for i in range(STEP):
            bs = b_ref[pl.ds((at + i) * n, n), :]
            for j in range(tiles):
                c = slice(j*128, (j+1)*128)
                decay = jnp.exp2(rowb(dte[:, c], i, n) * rates[j])
                state[j] = decay * state[j] + bs * rowb(dtx[:, c], i, n)
        return tuple(state), total + dte
    zero = tuple(jnp.zeros((n, 128), F32) for _ in range(tiles))
    state, total = lax.fori_loop(0, rows // STEP, block, (zero, jnp.zeros((STEP, wide), F32)))
    summed = jnp.sum(total, axis=0, keepdims=True)
    for j in range(tiles):
        c = slice(j*128, (j+1)*128)
        state_ref[:, c] = state[j]
        carry_ref[:, c] = jnp.exp2(jnp.broadcast_to(summed[:, c], (n, 128)) * rates[j])

def state_pass(dte, dtx, rates2, b_wide, wide):
    rows, chans = dte.shape
    n = rates2.shape[0]
    return pl.pallas_call(
        functools.partial(state_kernel, n),
        grid=(chans // wide,),
        in_specs=[pl.BlockSpec((rows, wide), lambda g: (0, g)),
                  pl.BlockSpec((rows, wide), lambda g: (0, g)),
                  pl.BlockSpec((n, wide), lambda g: (0, g)),
                  pl.BlockSpec(b_wide.shape, lambda g: (0, 0))],
        out_specs=[pl.BlockSpec((n, wide), lambda g: (0, g))] * 2,
        out_shape=[jax.ShapeDtypeStruct((n, chans), F32)] * 2,
        compiler_params=pltpu.CompilerParams(vmem_limit_bytes=VM),
        cost_estimate=pl.CostEstimate(flops=8*rows*chans*n, bytes_accessed=8*rows*chans, transcendentals=rows*chans*n),
    )(dte, dtx, rates2, b_wide)

def scan_kernel(n, dte_ref, dtx_ref, rate_ref, b_ref, cblk_ref, start_ref, y_ref, check_ref, hs):
    rows, wide = dte_ref.shape
    tiles = wide // 128
    rates = [rate_ref[:, j*128:(j+1)*128] for j in range(tiles)]
    def block(k, state):
        at = pl.multiple_of(k * STEP, STEP)
        dte = dte_ref[pl.ds(at, STEP), :]
        dtx = dtx_ref[pl.ds(at, STEP), :]
        state = list(state)
        kn = pl.multiple_of(k * n, n)
        for j in range(tiles):
            check_ref[pl.ds(kn, n), j*128:(j+1)*128] = state[j]
        for i in range(STEP):
            bs = b_ref[pl.ds((at + i) * n, n), :]
            for j in range(tiles):
                c = slice(j*128, (j+1)*128)
                decay = jnp.exp2(rowb(dte[:, c], i, n) * rates[j])
                state[j] = decay * state[j] + bs * rowb(dtx[:, c], i, n)
                hs[i*n:(i+1)*n, c] = state[j].astype(BF)
        y_ref[pl.ds(at, STEP), :] = jnp.dot(cblk_ref[pl.ds(at, STEP), :], hs[...], preferred_element_type=F32)
        return tuple(state)
    start = tuple(start_ref[:, j*128:(j+1)*128] for j in range(tiles))
    lax.fori_loop(0, rows // STEP, block, start)

def scan_pass(dte, dtx, rates2, b_wide, c_blk, start, wide):
    rows, chans = dte.shape
    n = rates2.shape[0]
    return pl.pallas_call(
        functools.partial(scan_kernel, n),
        grid=(chans // wide,),
        in_specs=[pl.BlockSpec((rows, wide), lambda g: (0, g)),
                  pl.BlockSpec((rows, wide), lambda g: (0, g)),
                  pl.BlockSpec((n, wide), lambda g: (0, g)),
                  pl.BlockSpec(b_wide.shape, lambda g: (0, 0)),
                  pl.BlockSpec(c_blk.shape, lambda g: (0, 0)),
                  pl.BlockSpec((n, wide), lambda g: (0, g))],
        out_specs=[pl.BlockSpec((rows, wide), lambda g: (0, g)),
                   pl.BlockSpec((rows // STEP * n, wide), lambda g: (0, g))],
        out_shape=[jax.ShapeDtypeStruct((rows, chans), F32),
                   jax.ShapeDtypeStruct((rows // STEP * n, chans), F32)],
        scratch_shapes=[pltpu.VMEM((STEP * n, wide), BF)],
        compiler_params=pltpu.CompilerParams(vmem_limit_bytes=VM),
        cost_estimate=pl.CostEstimate(flops=10*rows*chans*n, bytes_accessed=12*rows*chans, transcendentals=rows*chans*n),
    )(dte, dtx, rates2, b_wide, c_blk, start)

def back_state_kernel(n, dte_ref, gs_ref, rate_ref, c_ref, out_ref):
    rows, wide = dte_ref.shape
    tiles = wide // 128
    rates = [rate_ref[:, j*128:(j+1)*128] for j in range(tiles)]
    def block(k, state):
        at = pl.multiple_of(rows - STEP - k * STEP, STEP)
        dte = dte_ref[pl.ds(at, STEP), :]
        gs = gs_ref[pl.ds(at, STEP), :]
        state = list(state)
        for i in reversed(range(STEP)):
            cs = c_ref[pl.ds((at + i) * n, n), :]
            for j in range(tiles):
                c = slice(j*128, (j+1)*128)
                decay = jnp.exp2(rowb(dte[:, c], i, n) * rates[j])
                state[j] = decay * (state[j] + cs * rowb(gs[:, c], i, n))
        return tuple(state)
    zero = tuple(jnp.zeros((n, 128), F32) for _ in range(tiles))
    state = lax.fori_loop(0, rows // STEP, block, zero)
    for j in range(tiles):
        out_ref[:, j*128:(j+1)*128] = state[j]

def back_state_pass(dte, gs, rates2, c_wide, wide):
    rows, chans = dte.shape
    n = rates2.shape[0]
    return pl.pallas_call(
        functools.partial(back_state_kernel, n),
        grid=(chans // wide,),
        in_specs=[pl.BlockSpec((rows, wide), lambda g: (0, g)),
                  pl.BlockSpec((rows, wide), lambda g: (0, g)),
                  pl.BlockSpec((n, wide), lambda g: (0, g)),
                  pl.BlockSpec(c_wide.shape, lambda g: (0, 0))],
        out_specs=pl.BlockSpec((n, wide), lambda g: (0, g)),
        out_shape=jax.ShapeDtypeStruct((n, chans), F32),
        compiler_params=pltpu.CompilerParams(vmem_limit_bytes=VM),
        cost_estimate=pl.CostEstimate(flops=8*rows*chans*n, bytes_accessed=8*rows*chans, transcendentals=rows*chans*n),
    )(dte, gs, rates2, c_wide)

def back_kernel(n, dt_ref, dte_ref, dtx_ref, gs_ref, rate_ref, rawrate_ref, b_ref, c_ref, bblk_ref, oblk_ref, check_ref, next_ref,
                gdtx_ref, gdt_ref, glog_ref, gb_ref, gc_ref, us, decs, hs, ls, ps):
    rows, wide = dte_ref.shape
    tiles = wide // 128
    rates = [rate_ref[:, j*128:(j+1)*128] for j in range(tiles)]
    @pl.when(pl.program_id(0) == 0)
    def _():
        gb_ref[...] = jnp.zeros_like(gb_ref)
        gc_ref[...] = jnp.zeros_like(gc_ref)
    glog_ref[...] = jnp.zeros_like(glog_ref)
    def block(k, later):
        kk = rows // STEP - 1 - k
        at = pl.multiple_of(kk * STEP, STEP)
        kn = pl.multiple_of(kk * n, n)
        dte = dte_ref[pl.ds(at, STEP), :]
        dtx = dtx_ref[pl.ds(at, STEP), :]
        state = [check_ref[pl.ds(kn, n), j*128:(j+1)*128] for j in range(tiles)]
        for i in range(STEP):
            bs = b_ref[pl.ds((at + i) * n, n), :]
            for j in range(tiles):
                c = slice(j*128, (j+1)*128)
                decay = jnp.exp2(rowb(dte[:, c], i, n) * rates[j])
                kept = decay * state[j]
                state[j] = kept + bs * rowb(dtx[:, c], i, n)
                decs[i*n:(i+1)*n, c] = decay
                us[i*n:(i+1)*n, c] = kept
                hs[i*n:(i+1)*n, c] = state[j].astype(BF)
        later = list(later)
        dt = dt_ref[pl.ds(at, STEP), :]
        gs = gs_ref[pl.ds(at, STEP), :]
        logs = [glog_ref[:, j*128:(j+1)*128] for j in range(tiles)]
        for i in reversed(range(STEP)):
            cs = c_ref[pl.ds((at + i) * n, n), :]
            for j in range(tiles):
                c = slice(j*128, (j+1)*128)
                adj = later[j] + cs * rowb(gs[:, c], i, n)
                part = adj * us[i*n:(i+1)*n, c] * rawrate_ref[:, c]
                later[j] = adj * decs[i*n:(i+1)*n, c]
                logs[j] = logs[j] + part * rowb(dt[:, c], i, n)
                ls[i*n:(i+1)*n, c] = adj.astype(BF)
                ps[i*n:(i+1)*n, c] = part.astype(BF)
        for j in range(tiles):
            glog_ref[:, j*128:(j+1)*128] = logs[j]
        gdtx_ref[pl.ds(at, STEP), :] = jnp.dot(bblk_ref[pl.ds(at, STEP), :], ls[...], preferred_element_type=F32)
        gdt_ref[pl.ds(at, STEP), :] = jnp.dot(oblk_ref[...], ps[...], preferred_element_type=F32)
        nt = (((1,), (1,)), ((), ()))
        gb_ref[pl.ds(at, STEP), :] += lax.dot_general(dtx.astype(BF), ls[...], nt, preferred_element_type=F32)
        gc_ref[pl.ds(at, STEP), :] += lax.dot_general(gs.astype(BF), hs[...], nt, preferred_element_type=F32)
        return tuple(later)
    start = tuple(next_ref[:, j*128:(j+1)*128] for j in range(tiles))
    lax.fori_loop(0, rows // STEP, block, start)

def back_pass(dt, dte, dtx, gs, rates2, rates, b_wide, c_wide, b_blk, o_blk, check, nxt, wide):
    rows, chans = dte.shape
    n = rates2.shape[0]
    col = lambda r: pl.BlockSpec((r, wide), lambda g: (0, g))
    whole = lambda a: pl.BlockSpec(a.shape, lambda g: (0, 0))
    return pl.pallas_call(
        functools.partial(back_kernel, n),
        grid=(chans // wide,),
        in_specs=[col(rows)] * 4 + [col(n)] * 2 + [whole(b_wide), whole(c_wide), whole(b_blk), whole(o_blk), col(rows // STEP * n), col(n)],
        out_specs=[col(rows), col(rows), col(n), pl.BlockSpec((rows, STEP * n), lambda g: (0, 0)), pl.BlockSpec((rows, STEP * n), lambda g: (0, 0))],
        out_shape=[jax.ShapeDtypeStruct((rows, chans), F32)] * 2 + [jax.ShapeDtypeStruct((n, chans), F32)] + [jax.ShapeDtypeStruct((rows, STEP * n), F32)] * 2,
        scratch_shapes=[pltpu.VMEM((STEP * n, wide), F32)] * 2 + [pltpu.VMEM((STEP * n, wide), BF)] * 3,
        compiler_params=pltpu.CompilerParams(vmem_limit_bytes=VM),
        cost_estimate=pl.CostEstimate(flops=26*rows*chans*n, bytes_accessed=24*rows*chans, transcendentals=rows*chans*n),
    )(dt, dte, dtx, gs, rates2, rates, b_wide, c_wide, b_blk, o_blk, check, nxt)

def block_diag(vals):
    rows, n = vals.shape
    same = (jnp.arange(rows)[:, None] % STEP) == (jnp.arange(STEP * n)[None, :] // n)
    return jnp.where(same, jnp.tile(vals, (1, STEP)), 0)

def block_undiag(full, n):
    rows = full.shape[0]
    same = (jnp.arange(rows)[:, None] % STEP) == (jnp.arange(STEP * n)[None, :] // n)
    return jnp.sum(jnp.where(same, full, 0).reshape(rows, STEP, n), axis=1)


def expert_kernel(slot_ref, grad_ref, up_ref, down_ref, out_ref, disp_ref, gup_ref, gdown_ref):
    slots, grads, up, down = slot_ref[...], grad_ref[...], up_ref[...], down_ref[...]
    hidden = lax.dot_general(slots, up, NT, preferred_element_type=F32)
    phi = 0.5 * (1.0 + lax.erf(hidden * (1.0 / math.sqrt(2.0))))
    act = (hidden * phi).astype(BF)
    slope = phi + hidden * jnp.exp(hidden * hidden * -0.5) * (1.0 / math.sqrt(2.0 * math.pi))
    gact = lax.dot_general(grads, down, NT, preferred_element_type=F32)
    ghid = (gact * slope).astype(BF)
    @pl.when(pl.program_id(0) == 0)
    def _():
        out_ref[...] = jnp.zeros_like(out_ref)
        disp_ref[...] = jnp.zeros_like(disp_ref)
    out_ref[...] += jnp.dot(act, down, preferred_element_type=F32)
    disp_ref[...] += jnp.dot(ghid, up, preferred_element_type=F32)
    gup_ref[...] = lax.dot_general(ghid, slots, TN, preferred_element_type=F32).astype(gup_ref.dtype)
    gdown_ref[...] = lax.dot_general(act, grads, TN, preferred_element_type=F32).astype(gdown_ref.dtype)

def expert_pass(slots, grads, up, down, block):
    rows, width = slots.shape
    units = up.shape[0]
    whole = pl.BlockSpec((rows, width), lambda g: (0, 0))
    part = pl.BlockSpec((block, width), lambda g: (g, 0))
    return pl.pallas_call(
        expert_kernel,
        grid=(units // block,),
        in_specs=[whole, whole, part, part],
        out_specs=[whole, whole, part, part],
        out_shape=[jax.ShapeDtypeStruct((rows, width), F32)] * 2 + [jax.ShapeDtypeStruct((units, width), BF)] * 2,
        compiler_params=pltpu.CompilerParams(vmem_limit_bytes=VM),
        cost_estimate=pl.CostEstimate(flops=12*rows*units*width, bytes_accessed=8*units*width + 12*rows*width, transcendentals=2*rows*units),
    )(slots, grads, up, down)


def flip(value, bit):
    return value + bit - 2 * bit * (lax.rem(value // bit, 2))


def greet(partners):
    barrier = pltpu.get_barrier_semaphore()
    for partner in partners:
        pl.semaphore_signal(barrier, inc=1, device_id=partner, device_id_type=MESH)
    pl.semaphore_wait(barrier, len(partners))


class ZSwap:
    def __init__(self, pairs, local, send, recv, count):
        self.pairs, self.local, self.send, self.recv, self.count = pairs, local, send, recv, count

    def own(self):
        z = lax.axis_index("seq")
        return [pltpu.make_async_copy(src.at[z], dst.at[z], self.local.at[i]) for i, (src, dst) in enumerate(self.pairs)]

    def out(self):
        dp, z = lax.axis_index("dp"), lax.axis_index("seq")
        made = []
        for j in range(1, self.count):
            peer = lax.rem(z + j, self.count)
            for i, (src, dst) in enumerate(self.pairs):
                made.append(pltpu.make_async_remote_copy(src.at[peer], dst.at[z], self.send.at[i, j - 1], self.recv.at[i, j - 1], device_id=(dp, peer), device_id_type=MESH))
        return made

    def start(self):
        for copy in self.out() + self.own():
            copy.start()

    def wait(self):
        dp, z = lax.axis_index("dp"), lax.axis_index("seq")
        for copy in self.own():
            copy.wait()
        for copy in self.out():
            copy.wait_send()
        for j in range(1, self.count):
            source = lax.rem(z + self.count - j, self.count)
            for i, (src, dst) in enumerate(self.pairs):
                pltpu.make_async_remote_copy(src.at[z], dst.at[source], self.send.at[i, j - 1], self.recv.at[i, j - 1], device_id=(dp, source), device_id_type=MESH).wait_recv()


def gather_kernel(parts, count, in_ref, rest_ref, up_ref, down_ref, tok_ref, ids_ref, gin_ref, grest_ref, gup_ref, gdown_ref, rim_ref, rimids_ref,
                  local_sem, send, recv, share_send, share_recv, pair_send, pair_recv, swap_local, swap_send, swap_recv, rim_send, rim_recv):
    dp, z = lax.axis_index("dp"), lax.axis_index("seq")
    chip, core = dp // 2, lax.rem(dp, 2)
    srcs, dsts = (in_ref, rest_ref), (gin_ref, grest_ref)
    sibling = (flip(dp, 1), z)
    peers = [lax.rem(z + j, count) for j in range(1, count)]
    greet([sibling, (flip(dp, 4), z), (flip(dp, 2), z)] + [(dp, peer) for peer in peers])

    tail = pl.ds(tok_ref.shape[0] - rim_ref.shape[0], rim_ref.shape[0])
    rims = [pltpu.make_async_remote_copy(src, dst, rim_send.at[i], rim_recv.at[i], device_id=(dp, lax.rem(z + 1, count)), device_id_type=MESH)
            for i, (src, dst) in enumerate(((tok_ref.at[tail], rim_ref), (ids_ref, rimids_ref)))]
    for copy in rims:
        copy.start()
    mine = []
    for i, (src, dst) in enumerate(zip(srcs, dsts)):
        local = pltpu.make_async_copy(src, dst.at[chip, core, z], local_sem.at[i])
        pair = pltpu.make_async_remote_copy(src, dst.at[chip, core, z], pair_send.at[i], pair_recv.at[i], device_id=sibling, device_id_type=MESH)
        local.start()
        pair.start()
        mine += [local, pair]
    for copy in mine:
        copy.wait()
    swap = ZSwap(((up_ref, gup_ref), (down_ref, gdown_ref)), swap_local, swap_send, swap_recv, count)

    def role(which, first_bit, second_bit):
        chunks = parts[which]
        first, second = (flip(dp, first_bit), z), (flip(dp, second_bit), z)
        first_chip, second_chip = flip(chip, first_bit // 2), flip(chip, second_bit // 2)
        both_chip = flip(first_chip, second_bit // 2)

        def copies(at_chip, at_z, slot, to, send_s, recv_s):
            made = []
            for i, (ref, lo, size) in enumerate(chunks):
                view = dsts[ref].at[at_chip, :, at_z, pl.ds(lo, size)]
                made.append(pltpu.make_async_remote_copy(view, view, send_s.at[slot, i], recv_s.at[slot, i], device_id=to, device_id_type=MESH))
            return made

        def start(made):
            for copy in made:
                copy.start()

        def wait_recv(made):
            for copy in made:
                copy.wait_recv()

        def along_first(k):
            return copies(chip, k, 4 + k, first, send, recv)

        def along_second(k, far):
            return copies(first_chip if far else chip, k, 8 + 4 * far + k, second, send, recv)

        def came_first(k):
            return copies(first_chip, k, 4 + k, first, send, recv)

        def came_second(k, far):
            return copies(both_chip if far else second_chip, k, 8 + 4 * far + k, second, send, recv)

        def share(at_chip, k, offset):
            return copies(at_chip, k, 4 * offset + k, sibling, share_send, share_recv)

        def spread(k):
            start(along_second(k, 0))
            start(along_first(k))

        def rest(k):
            wait_recv(came_first(k))
            start(along_second(k, 1))
            start(share(first_chip, k, 1))

        @pl.when(z > 0)
        def _():
            start(copies(chip, z, z, (dp, z - 1), send, recv))

        @pl.when(z < count - 1)
        def _():
            start(copies(chip, z, z + count * 5, (dp, z + 1), send, recv))

        def below(hop, work):
            pl.when(z - hop >= 0)(lambda: work(z - hop))

        def above(hop, work):
            pl.when(z + hop <= count - 1)(lambda: work(z + hop))

        def from_below(k):
            wait_recv(copies(chip, k, k + count * 5, (dp, z), send, recv))

            @pl.when(z < count - 1)
            def _():
                start(copies(chip, k, k + count * 5, (dp, z + 1), send, recv))

            spread(k)
            start(share(chip, k, 0))

        def from_above(k):
            wait_recv(copies(chip, k, k, (dp, z), send, recv))

            @pl.when(z > 0)
            def _():
                start(copies(chip, k, k, (dp, z - 1), send, recv))

            spread(k)
            start(share(chip, k, 0))

        spread(z)
        for hop in range(1, count):
            below(hop, from_below)
            above(hop, from_above)
            if hop == 1:
                rest(z)
            else:
                below(hop - 1, rest)
                above(hop - 1, rest)
        swap.start()
        below(count - 1, rest)
        above(count - 1, rest)

        def finish(k, _):
            for far in (0, 1):
                wait_recv(came_second(k, far))
                start(share(both_chip if far else second_chip, k, 2 + far))
            return 0

        lax.fori_loop(0, count, finish, 0)

        def drain(k, _):
            for copy in along_first(k) + along_second(k, 0) + along_second(k, 1):
                copy.wait_send()
            for offset, at_chip in enumerate((chip, first_chip, second_chip, both_chip)):
                if offset:
                    for copy in share(at_chip, k, offset):
                        copy.wait_send()
                else:
                    @pl.when(k != z)
                    def _():
                        for copy in share(at_chip, k, offset):
                            copy.wait_send()

            @pl.when((k <= z) & (z < count - 1))
            def _():
                for copy in copies(chip, k, k + count * 5, (dp, z), send, recv):
                    copy.wait_send()

            @pl.when((k >= z) & (z > 0))
            def _():
                for copy in copies(chip, k, k, (dp, z), send, recv):
                    copy.wait_send()
            return 0

        lax.fori_loop(0, count, drain, 0)

        other = parts[1 - which]

        def shared(k, _):
            for offset, at_chip in enumerate((chip, second_chip, first_chip, both_chip)):
                def wait():
                    for i, (ref, lo, size) in enumerate(other):
                        view = dsts[ref].at[at_chip, :, k, pl.ds(lo, size)]
                        pltpu.make_async_remote_copy(view, view, share_send.at[4 * offset + k, i], share_recv.at[4 * offset + k, i], device_id=sibling, device_id_type=MESH).wait_recv()
                if offset:
                    wait()
                else:
                    pl.when(k != z)(wait)
            return 0

        lax.fori_loop(0, count, shared, 0)

    pl.when(core == 0)(lambda: role(0, 4, 2))
    pl.when(core == 1)(lambda: role(1, 2, 4))
    swap.wait()
    for copy in rims:
        copy.wait()


def gather_all(w_in, rest, up, down, tok, ids, cut, count):
    parts = (((0, 0, cut),), ((0, cut, w_in.shape[0] - cut), (1, 0, rest.shape[0])))
    shape = lambda a: jax.ShapeDtypeStruct((4, 2, count) + a.shape, a.dtype)
    sems = lambda *s: pltpu.SemaphoreType.DMA(s)
    return pl.pallas_call(
        functools.partial(gather_kernel, parts, count),
        in_specs=[pl.BlockSpec(memory_space=pl.ANY)] * 6,
        out_specs=[pl.BlockSpec(memory_space=pl.ANY)] * 6,
        out_shape=[shape(w_in), shape(rest), jax.ShapeDtypeStruct(up.shape, up.dtype), jax.ShapeDtypeStruct(down.shape, down.dtype),
                   jax.ShapeDtypeStruct((16, tok.shape[1]), tok.dtype), jax.ShapeDtypeStruct(ids.shape, ids.dtype)],
        scratch_shapes=[sems(2), sems(24, 2), sems(24, 2), sems(16, 2), sems(16, 2), sems(2), sems(2), sems(2), sems(2, count - 1), sems(2, count - 1), sems(2), sems(2)],
        compiler_params=pltpu.CompilerParams(collective_id=1, has_side_effects=True),
        cost_estimate=pl.CostEstimate(flops=0, bytes_accessed=200_000_000, transcendentals=0),
        name="gather_all",
    )(w_in, rest, up, down, tok, ids)


def scatter_kernel(parts, count, in_ref, rest_ref, up_ref, down_ref, oin_ref, orest_ref, oup_ref, odown_ref, mine_a, mine_b, sib_a, sib_b, far_a, far_b, near_a, near_b, zgot_a, zgot_b, final_a, final_b,
                   load_sem, sib_send, sib_recv, two_send, two_recv, one_send, one_recv, z_send, z_recv, end_send, end_recv, end_local,
                   swap_local, swap_send, swap_recv):
    dp, z = lax.axis_index("dp"), lax.axis_index("seq")
    chip, core = dp // 2, lax.rem(dp, 2)
    srcs, outs = (in_ref, rest_ref), (oin_ref, orest_ref)
    mine, sib, far_got, near_got, z_got, final = (mine_a, mine_b), (sib_a, sib_b), (far_a, far_b), (near_a, near_b), (zgot_a, zgot_b), (final_a, final_b)
    sibling = (flip(dp, 1), z)
    peers = [(dp, lax.rem(z + j, count)) for j in range(1, count)]
    greet([sibling, (flip(dp, 4), z), (flip(dp, 2), z)] + peers)

    swap = ZSwap(((up_ref, oup_ref), (down_ref, odown_ref)), swap_local, swap_send, swap_recv, count)

    def role(which, first_bit, second_bit):
        chunks, other = parts[which], parts[1 - which]
        first, second = (flip(dp, first_bit), z), (flip(dp, second_bit), z)
        first_chip, second_chip = flip(chip, first_bit // 2), flip(chip, second_bit // 2)
        both_chip = flip(first_chip, second_bit // 2)
        steps = [lax.rem(z + 1 + j, count) for j in range(count)]

        def loads(col, k):
            slot = col * count + k
            return [pltpu.make_async_copy(srcs[ref].at[col, :, k, pl.ds(lo, size)], mine[ref].at[slot, :, pl.ds(0, size)], load_sem.at[slot, ref])
                    for ref, lo, size in chunks]

        def sibling_copies(col, k, pieces):
            slot = col * count + k
            return [pltpu.make_async_remote_copy(srcs[ref].at[col, :, k, pl.ds(lo, size)], sib[ref].at[slot, :, pl.ds(0, size)],
                                                 sib_send.at[slot, ref], sib_recv.at[slot, ref], device_id=sibling, device_id_type=MESH)
                    for ref, lo, size in pieces]

        def send(col, k, dst, slot, send_s, recv_s, to):
            return [pltpu.make_async_remote_copy(mine[ref].at[col * count + k, :, pl.ds(0, size)], dst[ref].at[slot, :, pl.ds(0, size)],
                                                 send_s.at[slot, ref], recv_s.at[slot, ref], device_id=to, device_id_type=MESH)
                    for ref, lo, size in chunks]

        def start(copies):
            for copy in copies:
                copy.start()

        def wait_recv(copies):
            for copy in copies:
                copy.wait_recv()

        def wait_send(copies):
            for copy in copies:
                copy.wait_send()

        def add(col, k, terms, last=False):
            slot = col * count + k
            for copy in loads(col, k):
                copy.wait()
            wait_recv(sibling_copies(col, k, chunks))
            for ref, lo, size in chunks:
                def rows(r, _):
                    at = pl.ds(pl.multiple_of(r * 16, 16), 16)
                    for c in range(2):
                        total = mine[ref][slot, c, at, :].astype(F32) + sib[ref][slot, c, at, :].astype(F32)
                        for buf, place in terms:
                            total = total + buf[ref][place, c, at, :].astype(F32)
                        if last:
                            final[ref][c, at, :] = total
                        else:
                            mine[ref][slot, c, at, :] = total.astype(BF)
                    return 0

                lax.fori_loop(0, size // 16, rows, 0)

        for k in steps:
            for col, sib_col in ((both_chip, both_chip), (second_chip, first_chip), (first_chip, second_chip), (chip, chip)):
                start(sibling_copies(sib_col, k, other) + loads(col, k))

        swap.start()

        def stage_one(k):
            for far, col in ((1, both_chip), (0, second_chip)):
                add(col, k, ())
                start(send(col, k, far_got, far * count + k, two_send, two_recv, second))

        def stage_two(k):
            wait_recv(send(first_chip, k, far_got, count + k, two_send, two_recv, second))
            add(first_chip, k, ((far_got, count + k),))
            start(send(first_chip, k, near_got, k, one_send, one_recv, first))

        def stage_three(j, k):
            wait_recv(send(chip, k, far_got, k, two_send, two_recv, second))
            wait_recv(send(chip, k, near_got, k, one_send, one_recv, first))
            if j < count - 1:
                add(chip, k, ((far_got, k), (near_got, k)))
                start(send(chip, k, z_got, j, z_send, z_recv, (dp, k)))

        for j in range(count + 2):
            if j < count:
                stage_one(steps[j])
            if 1 <= j <= count:
                stage_two(steps[j - 1])
            if j >= 2:
                stage_three(j - 2, steps[j - 2])

        for j in range(count - 1):
            wait_recv(send(chip, z, z_got, j, z_send, z_recv, (dp, z)))
        add(chip, z, ((far_got, z), (near_got, z)) + tuple((z_got, j) for j in range(count - 1)), last=True)
        locals_, remotes = [], []
        for ref, lo, size in chunks:
            locals_.append(pltpu.make_async_copy(final[ref].at[which, pl.ds(0, size)], outs[ref].at[pl.ds(lo, size)], end_local.at[ref]))
            remotes.append(pltpu.make_async_remote_copy(final[ref].at[1 - which, pl.ds(0, size)], outs[ref].at[pl.ds(lo, size)],
                                                        end_send.at[which, ref], end_recv.at[which, ref], device_id=sibling, device_id_type=MESH))
        start(locals_ + remotes)
        for copy in locals_:
            copy.wait()
        wait_send(remotes)
        for ref, lo, size in other:
            pltpu.make_async_remote_copy(final[ref].at[which, pl.ds(0, size)], outs[ref].at[pl.ds(lo, size)],
                                         end_send.at[1 - which, ref], end_recv.at[1 - which, ref], device_id=sibling, device_id_type=MESH).wait_recv()
        for j, k in enumerate(steps):
            for col in (chip, first_chip, second_chip, both_chip):
                wait_send(sibling_copies(col, k, other))
            wait_send(send(both_chip, k, far_got, count + k, two_send, two_recv, second))
            wait_send(send(second_chip, k, far_got, k, two_send, two_recv, second))
            wait_send(send(first_chip, k, near_got, k, one_send, one_recv, first))
            if j < count - 1:
                wait_send(send(chip, k, z_got, j, z_send, z_recv, (dp, k)))

    pl.when(core == 0)(lambda: role(0, 4, 2))
    pl.when(core == 1)(lambda: role(1, 2, 4))
    swap.wait()


def scatter_all(g_in, g_rest, up, down, cut, collective_id):
    count = g_in.shape[2]
    rows_in, rows_rest = g_in.shape[3], g_rest.shape[3]
    parts = (((0, 0, cut),), ((0, cut, rows_in - cut), (1, 0, rows_rest)))
    sems = lambda *s: pltpu.SemaphoreType.DMA(s)
    places = 4 * count

    def bufs(k, kind=BF):
        lead = (k, 2) if k else (2,)
        return [pltpu.VMEM(lead + (max(cut, rows_in - cut), g_in.shape[4]), kind), pltpu.VMEM(lead + (rows_rest, g_rest.shape[4]), kind)]

    return pl.pallas_call(
        functools.partial(scatter_kernel, parts, count),
        in_specs=[pl.BlockSpec(memory_space=pl.ANY)] * 4,
        out_specs=[pl.BlockSpec(memory_space=pl.ANY)] * 4,
        out_shape=[jax.ShapeDtypeStruct(g_in.shape[3:], F32), jax.ShapeDtypeStruct(g_rest.shape[3:], F32), jax.ShapeDtypeStruct(up.shape, up.dtype), jax.ShapeDtypeStruct(down.shape, down.dtype)],
        scratch_shapes=bufs(places) + bufs(places) + bufs(2 * count) + bufs(count) + bufs(count - 1) + bufs(0, F32)
        + [sems(places, 2), sems(places, 2), sems(places, 2), sems(2 * count, 2), sems(2 * count, 2), sems(count, 2), sems(count, 2),
           sems(count - 1, 2), sems(count - 1, 2), sems(2, 2), sems(2, 2), sems(2), sems(2), sems(2, count - 1), sems(2, count - 1)],
        compiler_params=pltpu.CompilerParams(collective_id=collective_id, has_side_effects=True, vmem_limit_bytes=VM),
        cost_estimate=pl.CostEstimate(flops=0, bytes_accessed=200_000_000, transcendentals=0),
        name="scatter_all",
    )(g_in, g_rest, up, down)


def unpack_kernel(own, width_b, pack_ref, low_ref, high_ref, small_ref, tall):
    blocks = pack_ref.shape[0]
    for b in range(blocks):
        block = pack_ref[b].astype(F32)
        tall[b * own : (b + 1) * own, :] = block[:own]
        small_ref[b : b + 1, :] = block[own : own + 1]
    for j in range(tall.shape[0] // 128):
        turned = tall[j * 128 : (j + 1) * 128, :].T
        low_ref[:, j * 128 : (j + 1) * 128] = turned[:width_b].astype(BF)
        high_ref[:, j * 128 : (j + 1) * 128] = turned[width_b:]


def unpack(pack, own, width_b):
    blocks, _, cols = pack.shape
    chans = blocks * own
    if own % 8:
        turned = pack[:, :own].reshape(chans, cols).T
        return turned[:width_b], turned[width_b:].astype(F32), pack[:, own].astype(F32)
    return pl.pallas_call(
        functools.partial(unpack_kernel, own, width_b),
        out_shape=[jax.ShapeDtypeStruct((width_b, chans), BF), jax.ShapeDtypeStruct((cols - width_b, chans), F32), jax.ShapeDtypeStruct((blocks, cols), F32)],
        scratch_shapes=[pltpu.VMEM((chans, cols), F32)],
        compiler_params=pltpu.CompilerParams(vmem_limit_bytes=VM),
        name="unpack_small",
    )(pack)


def pack_kernel(own, x_ref, dt_ref, log_ref, misc_ref, small_ref, out_ref, wide, tall):
    at = 0
    for ref in (x_ref, dt_ref, log_ref, misc_ref):
        wide[at : at + ref.shape[0], :] = ref[...]
        at += ref.shape[0]
    wide[at:, :] = jnp.zeros((wide.shape[0] - at, wide.shape[1]), F32)
    for j in range(tall.shape[0] // 128):
        tall[j * 128 : (j + 1) * 128, :] = wide[:, j * 128 : (j + 1) * 128].T
    cols = wide.shape[0]
    first = lax.broadcasted_iota(jnp.int32, (8, cols), 0) == 0
    for b in range(out_ref.shape[0]):
        tail = jnp.where(first, jnp.broadcast_to(small_ref[b : b + 1, :], (8, cols)), 0.0)
        out_ref[b] = jnp.concatenate([tall[b * own : (b + 1) * own, :], tail], axis=0).astype(BF)


def pack_grads(x_t, dt_t, log_t, misc, small, own):
    blocks, cols = small.shape
    chans = x_t.shape[1]
    rows = own + -own % 16
    if own % 8:
        turned = jnp.concatenate([x_t, dt_t, log_t, misc]).T.reshape(blocks, own, -1)
        turned = jnp.pad(turned, ((0, 0), (0, 0), (0, cols - turned.shape[2])))
        return jnp.concatenate([turned, small[:, None], jnp.zeros((blocks, rows - own - 1, cols), F32)], axis=1).astype(BF)
    return pl.pallas_call(
        functools.partial(pack_kernel, own),
        out_shape=jax.ShapeDtypeStruct((blocks, rows, cols), BF),
        scratch_shapes=[pltpu.VMEM((cols, chans), F32), pltpu.VMEM((chans, cols), F32)],
        compiler_params=pltpu.CompilerParams(vmem_limit_bytes=VM),
        name="pack_small",
    )(x_t, dt_t, log_t, misc, small)


def finish_kernel(own, cuts, pack_ref, up_ref, down_ref, up_out, down_out, row_out, *col_outs):
    piece, width = up_ref.shape[1:]
    filler = -piece % 128

    down_out[0] = down_ref[0].astype(F32)
    tall = up_ref[0].astype(F32)
    if filler:
        tall = jnp.concatenate([tall, jnp.zeros((filler, width), F32)], axis=0)
    for j in range(width // 128):
        up_out[0, j * 128 : (j + 1) * 128, :] = tall[:, j * 128 : (j + 1) * 128].T[:, :piece]

    @pl.when(pl.program_id(0) == 0)
    def _():
        row_out[...] = pack_ref[own : own + 1, :]
        for (lo, size), out in zip(cuts, col_outs):
            out[...] = pack_ref[0:own, lo : lo + size]


def finish(pack, up, down, own, cuts):
    experts, piece, width = up.shape
    if own % 8:
        return [jnp.swapaxes(up.astype(F32), 1, 2), down.astype(F32), pack[own : own + 1]] + [pack[:own, lo : lo + size] for lo, size in cuts]
    whole = lambda shape: pl.BlockSpec(shape, lambda e: (0,) * len(shape))
    part = lambda shape: pl.BlockSpec((1,) + shape[1:], lambda e: (e, 0, 0))
    shapes = [(experts, width, piece), (experts, piece, width), (1, pack.shape[1])] + [(own, size) for _, size in cuts]
    return pl.pallas_call(
        functools.partial(finish_kernel, own, cuts),
        grid=(experts,),
        in_specs=[whole(pack.shape), part(up.shape), part(down.shape)],
        out_specs=[part(shapes[0]), part(shapes[1])] + [whole(s) for s in shapes[2:]],
        out_shape=[jax.ShapeDtypeStruct(s, F32) for s in shapes],
        compiler_params=pltpu.CompilerParams(vmem_limit_bytes=VM),
        name="finish",
    )(pack, up, down)


def chain_kernel(step, pieces, carry_ref, own_ref, out_ref, inbox, outbox, send, recv):
    dp, z = lax.axis_index("dp"), lax.axis_index("seq")
    last = lax.axis_size("seq") - 1
    has_before = z > 0 if step > 0 else z < last
    has_after = z < last if step > 0 else z > 0
    barrier = pltpu.get_barrier_semaphore()

    def neighbours(act):
        pl.when(has_before)(lambda: act(z - step))
        pl.when(has_after)(lambda: act(z + step))

    neighbours(lambda peer: pl.semaphore_signal(barrier, inc=1, device_id=(dp, peer), device_id_type=MESH))
    count = last + 1
    pl.semaphore_wait(barrier, (z + last) // count + (2 * last - z) // count)
    wide = own_ref.shape[1] // pieces

    def copy(g):
        return pltpu.make_async_remote_copy(outbox.at[g], inbox.at[g], send.at[g], recv.at[g], device_id=(dp, z + step), device_id_type=MESH)

    def back(g):
        return pltpu.make_async_remote_copy(outbox.at[g], inbox.at[g], send.at[g], recv.at[g], device_id=(dp, z - step), device_id_type=MESH)

    for g in range(pieces):
        c = slice(g * wide, (g + 1) * wide)

        @pl.when(has_before)
        def _():
            back(g).wait_recv()
            out_ref[:, c] = inbox[g].astype(F32)

        @pl.when(jnp.logical_not(has_before))
        def _():
            out_ref[:, c] = jnp.zeros((out_ref.shape[0], wide), F32)

        @pl.when(has_after)
        def _():
            outbox[g] = (carry_ref[:, c] * out_ref[:, c] + own_ref[:, c]).astype(BF)
            copy(g).start()

    @pl.when(has_after)
    def _():
        for g in range(pieces):
            copy(g).wait_send()


def chain(carry, own, step, collective_id):
    pieces = 3
    n, chans = own.shape
    return pl.pallas_call(
        functools.partial(chain_kernel, step, pieces),
        in_specs=[pl.BlockSpec(memory_space=pltpu.VMEM)] * 2,
        out_specs=pl.BlockSpec(memory_space=pltpu.VMEM),
        out_shape=jax.ShapeDtypeStruct((n, chans), F32),
        scratch_shapes=[pltpu.VMEM((pieces, n, chans // pieces), BF)] * 2 + [pltpu.SemaphoreType.DMA((pieces,))] * 2,
        compiler_params=pltpu.CompilerParams(collective_id=collective_id, has_side_effects=True),
        name="chain",
    )(carry, own)


def dot(a, b):
    return jnp.dot(a, b, preferred_element_type=F32)


def dot_nt(a, b):
    return lax.dot_general(a, b, NT, preferred_element_type=F32)


def dot_tn(a, b):
    return lax.dot_general(a, b, TN, preferred_element_type=F32)


def shift(value, axis, steps):
    count = lax.axis_size(axis)
    first, last = (max(0, -steps), min(count, count - steps))
    return lax.ppermute(value, axis, [(source, source + steps) for source in range(first, last)])


def rms_scale(value):
    return lax.rsqrt(jnp.mean(value * value, axis=-1, keepdims=True) + EPS)


def rms_back(value, gain, grad):
    scale = rms_scale(value)
    scaled = grad * gain
    grad_gain = jnp.sum(grad * (value * scale), axis=0)
    return scale * scaled - value * (scale * scale * scale) * jnp.mean(value * scaled, axis=-1, keepdims=True), grad_gain


def swap(value):
    return lax.all_to_all(value, "seq", 0, 0)


def shards(tokens, segment_ids, routes, cotangent, small_params, w_in, conv_w, conv_b, w_x, w_dt, dt_bias, a_log, d_skip, w_out, w_up, w_down):
    both = ("dp", "seq")
    devices = lax.axis_size(both)
    width = tokens.shape[2]
    rows = tokens.shape[1]
    experts = w_up.shape[0]
    chans = w_in.shape[0] * devices // 2
    own = w_out.shape[0]
    rank = w_dt.shape[1]
    n = a_log.shape[1]
    taps = conv_w.shape[1]
    slots = rows // 2
    halo = 16
    wide = 768

    tok_b = tokens[0]
    seg_plus = segment_ids[0] + 1

    columns = (w_x, w_dt, a_log, conv_w, conv_b[:, None], dt_bias[:, None], d_skip[:, None])
    packed = jnp.concatenate(columns, axis=1)
    share = small_params.shape[0]
    packed = jnp.pad(packed, ((0, -own % 16), (0, 256 - packed.shape[1])))
    packed = packed + jnp.pad(small_params[None], ((own, -own % 16 - 1), (0, 256 - share)))
    direct = lax.axis_size("dp") == 8 and lax.axis_size("seq") == 4
    up_t = jnp.swapaxes(w_up, 1, 2)
    full_out = lax.all_gather(w_out, both, axis=0, tiled=True)
    if direct:
        last_ids = jnp.broadcast_to(seg_plus[rows - halo :, None], (halo, 128))
        all_in, all_pack, part_up, part_down, rim_tok, rim_ids = gather_all(w_in, packed, up_t, w_down, tok_b, last_ids, 80, 4)
        rim_ids = jnp.where(lax.axis_index("seq") > 0, rim_ids[:, 0], 0)
    else:
        all_in, all_pack = lax.all_gather(w_in, both), lax.all_gather(packed, both)
        part_up, part_down = swap(up_t), swap(w_down)
        rim_tok = shift(tok_b[rows - halo :], "seq", 1)
        rim_ids = shift(seg_plus[rows - halo :], "seq", 1)
    full_in = all_in.reshape(2 * chans, width)
    low_t, high_t, small = unpack(all_pack.reshape(devices, -1, 256), own, rank + w_x.shape[1])
    full_up = lax.all_gather(part_up, "dp", axis=0).reshape(-1, width)
    full_down = lax.all_gather(part_down, "dp", axis=0).reshape(-1, width)
    xcols = w_x.shape[1]
    full_x_t, full_dt_t = low_t[:xcols], low_t[xcols:]
    alog_t, conv_f, bias_row, dtb_row, skip = high_t[:n], high_t[n : n + taps], high_t[n + taps : n + taps + 1], high_t[n + taps + 1 : n + taps + 2], high_t[n + taps + 2 : n + taps + 3]
    flat_small = small[:, :share].reshape(-1)
    gain_one = flat_small[:width]
    gain_two = flat_small[width : 2 * width]
    router = flat_small[2 * width :].reshape(width, experts).astype(BF)
    route_ids = routes[0]
    onehot = (route_ids == jnp.arange(experts)[None, :]).astype(BF)
    before = (jnp.arange(rows)[:, None] > jnp.arange(rows)[None, :]).astype(BF)
    place = jnp.sum(dot(before, onehot) * onehot.astype(F32), axis=1).astype(jnp.int32)
    slot_of = route_ids[:, 0] * slots + place
    gather_mat = (slot_of[:, None] == jnp.arange(experts * slots)[None, :]).astype(BF)
    grad_out_b = cotangent[0]
    grad_out = grad_out_b.astype(F32)
    go_local, full_in = lax.optimization_barrier((dot_tn(gather_mat, grad_out_b).astype(BF), full_in))
    go_slots = swap(go_local.reshape(experts, slots, width)).reshape(-1, width)

    tok_ext = jnp.concatenate([rim_tok, tok_b]).astype(F32)
    tok_f = tok_b.astype(F32)
    ids_ext = jnp.concatenate([rim_ids, seg_plus])
    same = jnp.stack([ids_ext[halo - taps + 1 + k : halo - taps + 1 + k + rows] == seg_plus for k in range(taps)], axis=1).astype(F32)
    keep = same[:, taps - 2 : taps - 1]
    normed_ext = (tok_ext * rms_scale(tok_ext) * gain_one).astype(BF)
    normed = normed_ext[halo:]
    conv_in = dot_nt(normed_ext, full_in[:chans]).astype(BF).astype(F32)
    z = dot_nt(normed, full_in[chans:])
    conv_sum = bias_row
    for k in range(taps):
        lo = halo - taps + 1 + k
        conv_sum = conv_sum + conv_f[k : k + 1] * conv_in[lo : lo + rows] * same[:, k : k + 1]
    values = conv_sum * jax.nn.sigmoid(conv_sum)
    values_b = values.astype(BF)
    projected = dot_nt(values_b, full_x_t)
    low_rank = projected[:, :rank].astype(BF)
    b_rows = projected[:, rank : rank + n]
    c_rows = projected[:, rank + n :]
    pre_dt = dot(low_rank, full_dt_t) + dtb_row
    dt = jax.nn.softplus(pre_dt)
    dt_keep = jnp.where(keep > 0, dt, 1e30)
    dtx, go_slots = lax.optimization_barrier((dt * values, go_slots))
    rates = -jnp.exp(alog_t)
    rates2 = rates * math.log2(math.e)
    b_wide = jnp.broadcast_to(b_rows[:, :, None], (rows, n, 128)).reshape(rows * n, 128)
    c_wide = jnp.broadcast_to(c_rows[:, :, None], (rows, n, 128)).reshape(rows * n, 128)
    own_state, carry = state_pass(dt_keep, dtx, rates2, b_wide, wide)
    start = chain(carry, own_state, 1, 3)
    scanned, checks = scan_pass(dt_keep, dtx, rates2, b_wide, block_diag(c_rows).astype(BF), start, wide)
    sig_z = jax.nn.sigmoid(z)
    gated = ((scanned + skip * values) * (z * sig_z)).astype(BF)
    first_sum = tok_f + dot(gated, full_out)
    normed_two = (first_sum * rms_scale(first_sum) * gain_two).astype(BF)

    n2_slots = swap(dot_tn(gather_mat, normed_two).astype(BF).reshape(experts, slots, width)).reshape(-1, width)
    probs = jax.nn.softmax(dot(n2_slots, router), axis=-1)
    mine = (jnp.arange(experts) == lax.axis_index("seq")).astype(F32)[None]
    gate = jnp.sum(probs * mine, axis=1, keepdims=True)
    ge_slots = (gate * go_slots.astype(F32)).astype(BF)
    expert_out, grad_disp, grad_up, grad_down = expert_pass(n2_slots, ge_slots, full_up, full_down, 768)
    grad_gate = jnp.sum(go_slots.astype(F32) * expert_out, axis=1, keepdims=True)
    grad_logits = (grad_gate * gate * (mine - probs)).astype(BF)
    grad_router = dot_tn(n2_slots, grad_logits)
    grad_n2_slots = (grad_disp + dot_nt(grad_logits, router)).astype(BF)
    grad_n2 = dot(gather_mat, swap(grad_n2_slots.reshape(experts, slots, width)).reshape(-1, width))
    mixed_slots = swap((gate * expert_out).astype(BF).reshape(experts, slots, width)).reshape(-1, width)
    mixed_out = (first_sum + dot(gather_mat, mixed_slots)).astype(BF)
    part_gup = lax.psum_scatter(grad_up, "dp", scatter_dimension=0, tiled=True).reshape(experts, -1, width)
    part_gdown = lax.psum_scatter(grad_down, "dp", scatter_dimension=0, tiled=True).reshape(experts, -1, width)

    grad_norm_two, grad_gain_two = rms_back(first_sum, gain_two, grad_n2)
    grad_first = grad_out + grad_norm_two
    grad_mixer = grad_first.astype(BF)
    grad_w_out = dot_tn(gated, grad_mixer)
    grad_gated = dot_nt(grad_mixer, full_out)
    silu_z = z * sig_z
    grad_scanned = grad_gated * silu_z
    grad_z = grad_gated * (scanned + skip * values) * (sig_z * (1.0 + z * (1.0 - sig_z)))
    grad_z_b = grad_z.astype(BF)
    grad_skip = jnp.sum(grad_scanned * values, axis=0)
    grad_start = back_state_pass(dt_keep, grad_scanned, rates2, c_wide, wide)
    nxt = chain(carry, grad_start, -1, 4)
    ones_blk = block_diag(jnp.ones((STEP, n), F32)).astype(BF)
    g_dtx, g_dt, g_log, gb_full, gc_full = back_pass(
        dt, dt_keep, dtx, grad_scanned, rates2, rates, b_wide, c_wide, block_diag(b_rows).astype(BF), ones_blk, checks, nxt, wide
    )
    grad_dt = g_dt + g_dtx * values
    grad_pre_f = grad_dt * jax.nn.sigmoid(pre_dt)
    grad_dtb = jnp.sum(grad_pre_f, axis=0)
    grad_pre = grad_pre_f.astype(BF)
    grad_dt_t = dot_tn(low_rank, grad_pre)
    grad_proj = jnp.concatenate([dot_nt(grad_pre, full_dt_t), block_undiag(gb_full, n), block_undiag(gc_full, n)], axis=1).astype(BF)
    grad_x_t = dot_tn(grad_proj, values_b)
    grad_values = grad_scanned * skip + g_dtx * dt + dot(grad_proj, full_x_t)
    sig_c = jax.nn.sigmoid(conv_sum)
    grad_conv_sum = grad_values * (sig_c * (1.0 + conv_sum * (1.0 - sig_c)))
    grad_bias = jnp.sum(grad_conv_sum, axis=0)
    grad_taps = []
    grad_ext = None
    for k in range(taps):
        lo = halo - taps + 1 + k
        masked = grad_conv_sum * same[:, k : k + 1]
        grad_taps.append(jnp.sum(masked * conv_in[lo : lo + rows], axis=0))
        term = jnp.pad(masked * conv_f[k : k + 1], ((lo, halo - lo), (0, 0)))
        grad_ext = term if grad_ext is None else grad_ext + term
    rim_back = shift(grad_ext[halo - 8 : halo], "seq", -1)
    grad_conv_in = (grad_ext[halo:] + jnp.pad(rim_back, ((rows - 8, 0), (0, 0)))).astype(BF)
    grad_w_in = dot_tn(jnp.concatenate([grad_conv_in, grad_z_b], axis=1), normed).astype(BF)
    grad_normed = dot(grad_conv_in, full_in[:chans]) + dot(grad_z_b, full_in[chans:])
    grad_norm_one, grad_gain_one = rms_back(tok_f, gain_one, grad_normed)
    tokens_grad = (grad_first + grad_norm_one).astype(BF)

    grad_small = jnp.concatenate([grad_gain_one, grad_gain_two, grad_router.reshape(-1)])
    misc = jnp.stack(grad_taps + [grad_bias, grad_dtb, grad_skip, jnp.zeros_like(grad_bias)])
    grad_packed = pack_grads(grad_x_t, grad_dt_t, g_log, misc, jnp.pad(grad_small.reshape(devices, -1), ((0, 0), (0, 256 - share))), own)
    if direct:
        sum_in, sum_pack, sum_up, sum_down = scatter_all(
            grad_w_in.reshape(4, 2, 4, 2 * own, width), grad_packed.reshape((4, 2, 4) + grad_packed.shape[1:]), part_gup, part_gdown, 80, 2
        )
    else:
        sum_in = lax.psum_scatter(grad_w_in, both, scatter_dimension=0, tiled=True).astype(F32)
        sum_pack = lax.psum_scatter(grad_packed, both, scatter_dimension=0, tiled=True)[0].astype(F32)
        sum_up, sum_down = swap(part_gup), swap(part_gdown)
    grad_w_out = lax.optimization_barrier((grad_w_out.astype(BF), part_gup, part_gdown))[0]
    sum_out = lax.psum_scatter(grad_w_out, both, scatter_dimension=0, tiled=True).astype(F32)
    cuts, at = [], 0
    for column in columns:
        cuts.append((at, column.shape[1]))
        at += column.shape[1]
    up_out, down_out, s_row, s_x, s_dt, s_log, s_conv, s_bias, s_dtb, s_skip = finish(sum_pack, sum_up, sum_down, own, tuple(cuts))
    return (
        mixed_out[None],
        tokens_grad[None],
        s_row[0, :share],
        sum_in,
        s_conv,
        s_bias[:, 0],
        s_x,
        s_dt,
        s_dtb[:, 0],
        s_log,
        s_skip[:, 0],
        sum_out,
        up_out,
        down_out,
    )


def solution(mesh):
    split = ("dp", "seq")
    token, row, mat, vec = P("dp", "seq", None), P("dp", "seq"), P(split, None), P(split)
    return jax.shard_map(
        shards,
        mesh=mesh,
        in_specs=(token, row, token, token, vec, mat, mat, vec, mat, mat, vec, mat, vec, mat, P(None, None, split), P(None, split, None)),
        out_specs=(token, token, vec, mat, mat, vec, mat, mat, vec, mat, vec, mat, P(None, None, split), P(None, split, None)),
        check_vma=False,
    )
```

time: 4410 us -> 594 us (0.13)
  other arithmetic: 1580 us -> 32.2 us
  local copies, waits for them, and re-layouts: 1270 us -> 35.8 us
  waiting for transfers between devices: 925 us -> 43.6 us
  blocking collectives: 370 us -> 0 us
  Pallas kernels: 0 us -> 346 us
  matrix products: 181 us -> 79.7 us
    reduce_sum x307 -> x8, other arithmetic: 1120 us -> 10.8 us  [the longest x1 4.51 us: shards(): grad_dtb = jnp.sum(grad_pre_f, axis=0)]
    reduce_scatter x2, waiting for transfers between devices: 918 us -> 3.68 us  [the longest x1 3.68 us: shards(): lax.psum_scatter(grad_down, 'dp', scatter_dimension=0, tiled=True)]
    reshape x56 -> x2, local copies, waits for them, and re-layouts: 400 us -> 0.96 us  [the longest x1 0.86 us: shards(): flat_small = small[:, :share].reshape(-1)]
    pallas_call x0 -> x12, Pallas kernels: none -> 346 us  [the longest x1 104 us: gather_all(): pl.pallas_call(functools.partial(gather_kernel, parts, count), in_specs=[...]
    all_gather x7 -> x0, blocking collectives: 329 us -> none  [the longest x1 86.4 us: shards(): lax.all_gather(mixer_parts[4], ('dp', 'seq'), axis=0, tiled=True)]
    add_any x58 -> x0, other arithmetic: 227 us -> none  [the longest x8 183 us: state_scan(): lax.scan(jax.checkpoint(block_run), start_state, step_items)]
    concatenate x41 -> x1, local copies, waits for them, and re-layouts: 204 us -> 0.86 us  [shards(): packed = jnp.concatenate(columns, axis=1)]
    broadcast_in_dim x260 -> x9, local copies, waits for them, and re-layouts: 149 us -> 7.74 us  [the longest x2 2.06 us: shards(): jnp.broadcast_to(b_rows[:, :, None], (rows, n, 128)).reshape(rows * n, 128)]
  transfers between devices with their start and end apart: 9 -> 11, of which waited for: 3 -> 3; matrix products, arithmetic and copies ran while one was open for 29% -> 23% of each run, Pallas kernels for 0% -> 54%
where the time goes in v1:
time: 594 us; the launch traced here: 583 us
  Pallas kernels  346 us (58%)
  matrix products  79.7 us (13%)
  waiting for transfers between devices  43.6 us (7%)
  local copies, waits for them, and re-layouts  35.8 us (6%)
  other arithmetic  32.2 us (5%)
  starting transfers between devices  30.5 us (5%)
  between operations  15.8 us (3%)
    pallas_call x1, Pallas kernels, gather_all(): pl.pallas_call(functools.partial(gather_kernel, parts, count), in_specs=[...  104 us
    pallas_call x1, Pallas kernels, scatter_all(): pl.pallas_call(functools.partial(scatter_kernel, parts, count), in_specs=...  99 us
    pallas_call x1, Pallas kernels, back_pass(): pl.pallas_call(functools.partial(back_kernel, n), grid=(chans // wide,),...  47.6 us
    all_to_all x4, waiting for transfers between devices, swap(): return lax.all_to_all(value, 'seq', 0, 0)  38 us
    dot_general x9, matrix products, dot(): return jnp.dot(a, b, preferred_element_type=F32)  36.8 us
    pallas_call x1, Pallas kernels, expert_pass(): pl.pallas_call(expert_kernel, grid=(units // block,), in_specs=[whole, wh...  30.3 us
    all_to_all x4, starting transfers between devices, swap(): return lax.all_to_all(value, 'seq', 0, 0)  27.7 us
    dot_general x6, matrix products, dot_nt(): return lax.dot_general(a, b, NT, preferred_element_type=F32)  23.3 us
  transfers between devices with their start and end apart: 11, of which 3 were waited for; matrix products, arithmetic and copies ran while one was open for 23% of the time, Pallas kernels for 54%

profile of v1, /device:TPU:9, one launch (start us, length us, event | category | flops | bytes accessed | tf_op | source)
XLA Modules:
  0.0 583.2 jit_solution(16250541734972213355)
XLA Ops:
  15.4 104.1 %gather_all.1 = (bf16[4,2,4,144,1152]{4,3,2,1,0:T(8,128)(2,1)}, bf16[4,2,4,80,256]{4,3,2,1,0:T(8,128)(2,1)}, bf16[4,96,1152]{2,1,0:T(8,128)(2,1)}, bf16[4,96,115...) custom-call(bf16[144,1152]{1,0:T(8,128)(2,1)} %in_ref.1, bf16[80,256]{1,0:T(8,128)(2,1)} %pad_add_fusion.2.rest_ref, ...), custom_call_target="tpu_custom_call" | custom-call | bytes 200000000 | tf_op jit(solution)/shard_map/gather_all/pallas_call | solution.py:480
  122.2 5.5 all-to-all-start
  127.8 2.9 unpack_small.1
  134.7 4.6 fusion.12
  144.2 8.0 %compare_select_fusion = (f32[256,2304]{1,0:T(8,128)}, f32[256,2304]{1,0:T(8,128)}, f32[256,2304]{1,0:T(8,128)}, f32[256,2304]{1,0:T(8,128)}) fusion(pred[256]{0:T(512)(128)(4,1)S(1)} %compare_reduce_fusion, f32[256,2304]{1,0:T(8,128)} %copy-done.14, f32[2304]{0:T(1024)} %get-tuple-element.148, bf16[176,2304]{1,0:T(8,128)(2,1)} %get-tuple-element.62, ...), kind=kOutput, calls=%fused_computation.2 | convolution fusion | flops 92602368 | bytes 12177664 | tf_op jit(solution)/shard_map/dot_general | solution.py:801
  155.8 9.7 %shard_map.263 = (f32[16,2304]{1,0:T(8,128)}, f32[16,2304]{1,0:T(8,128)}) custom-call(f32[256,2304]{1,0:T(8,128)} %get-tuple-element.166.dte_ref, f32[256,2304]{1,0:T(8,128)} %get-tuple-element.64.dtx_ref, f32[16,2304]{1,0:T(8,128)} %get-tuple-element.171.rate_ref, f32[4096,128]{1,0:T(8,128)} %broadcast_in_dim.111.b_ref), custom_call_target="tpu_custom_call" | custom-call | flops 75497472 | bytes 4718592 | tf_op jit(solution)/shard_map/pallas_call | solution.py:51
  165.5 6.7 %chain.2.start_ref = f32[16,2304]{1,0:T(8,128)} custom-call(f32[16,2304]{1,0:T(8,128)} %get-tuple-element.65.carry_ref, f32[16,2304]{1,0:T(8,128)} %get-tuple-element.66.own_ref), custom_call_target="tpu_custom_call" | custom-call | tf_op jit(solution)/shard_map/chain/pallas_call | solution.py:789
  172.2 20.0 %shard_map.264 = (f32[256,2304]{1,0:T(8,128)}, f32[256,2304]{1,0:T(8,128)}) custom-call(f32[256,2304]{1,0:T(8,128)} %get-tuple-element.166.dte_ref, f32[256,2304]{1,0:T(8,128)} %get-tuple-element.64.dtx_ref, f32[16,2304]{1,0:T(8,128)} %get-tuple-element.171.rate_ref, f32[4096,128]{1,0:T(8,128)} %broadcast_in_dim.111.b_ref, ...), custom_call_target="tpu_custom_call" | custom-call | flops 94371840 | bytes 7077888 | tf_op jit(solution)/shard_map/pallas_call | solution.py:91
  192.3 7.0 %multiply_convert_fusion.2 = (bf16[256,2304]{1,0:T(8,128)(2,1)}, f32[256,2304]{1,0:T(8,128)}) fusion(f32[256,2304]{1,0:T(8,128)} %get-tuple-element.67, f32[2304]{0:T(1024)S(1)} %get-tuple-element.147, f32[256,2304]{1,0:T(8,128)S(1)} %copy-done.15, bf16[4608,1152]{1,0:T(8,128)(2,1)} %bitcast.100, bf16[272,1152]{1,0:T(8,128)(2,1)S(1)} %copy-done.21), kind=kOutput, calls=%fused_computation.43 | convolution fusion | flops 1366032384 | bytes 14168064 | tf_op jit(solution)/shard_map/dot_general | solution.py:805
  199.3 5.5 multiply_reduce_fusion.7
  207.5 5.8 all-to-all-start.1
  215.5 20.7 %all-to-all-done.1 = bf16[4,128,1152]{2,1,0:T(8,128)(2,1)} async-done(((bf16[4,128,1152]{2,1,0:T(8,128)(2,1)}), bf16[4,128,1152]{2,1,0:T(8,128)(2,1)}, u32[]{:S(2)}, u32[]{:S(2)}) %all-to-all-start.1) | async-done | bytes 1179680 | tf_op jit(solution)/shard_map/all_to_all | solution.py:830
  242.3 30.3 %shard_map.265 = (f32[512,1152]{1,0:T(8,128)}, f32[512,1152]{1,0:T(8,128)}, bf16[3072,1152]{1,0:T(8,128)(2,1)}, bf16[3072,1152]{1,0:T(8,128)(2,1)}) custom-call(bf16[512,1152]{1,0:T(8,128)(2,1)} %bitcast.19.slot_ref, bf16[512,1152]{1,0:T(8,128)(2,1)} %fusion.21.grad_ref, bf16[3072,1152]{1,0:T(8,128)(2,1)} %bitcast.105, bf16[3072,1152]{1,0:T(8,128)(2,1)} %bitcast.106), custom_call_target="tpu_custom_call" | custom-call | flops 21743271936 | bytes 35389440 | tf_op jit(solution)/shard_map/pallas_call | solution.py:247
  273.3 3.5 fusion.22
  278.5 7.2 %all-to-all-start.3 = ((bf16[4,128,1152]{2,1,0:T(8,128)(2,1)}), bf16[4,128,1152]{2,1,0:T(8,128)(2,1)}, u32[]{:S(2)}, u32[]{:S(2)}) async-start(bf16[4,128,1152]{2,1,0:T(8,128)(2,1)} %bitcast.68), calls=%async_computation.3 | async-start | bytes 2359296 | tf_op jit(solution)/shard_map/all_to_all | solution.py:830
  286.9 2.8 fusion.80
  291.2 17.3 %all-to-all-done.3 = bf16[4,128,1152]{2,1,0:T(8,128)(2,1)} async-done(((bf16[4,128,1152]{2,1,0:T(8,128)(2,1)}), bf16[4,128,1152]{2,1,0:T(8,128)(2,1)}, u32[]{:S(2)}, u32[]{:S(2)}) %all-to-all-start.3) | async-done | bytes 1179680 | tf_op jit(solution)/shard_map/all_to_all | solution.py:830
  308.6 9.1 %all-to-all-start.2 = ((bf16[4,128,1152]{2,1,0:T(8,128)(2,1)}), bf16[4,128,1152]{2,1,0:T(8,128)(2,1)}, u32[]{:S(2)}, u32[]{:S(2)}) async-start(bf16[4,128,1152]{2,1,0:T(8,128)(2,1)} %bitcast.70), calls=%async_computation.2 | async-start | bytes 2359296 | tf_op jit(solution)/shard_map/all_to_all | solution.py:830
  322.5 7.8 %multiply_reduce_fusion = (f32[2304]{0:T(1024)S(1)}, f32[256,2304]{1,0:T(8,128)}, bf16[256,2304]{1,0:T(8,128)(2,1)}) fusion(f32[256,2304]{1,0:T(8,128)S(1)} %copy-done.16, f32[256,2304]{1,0:T(8,128)} %get-tuple-element.193, f32[256,2304]{1,0:T(8,128)S(1)} %copy-done.80, f32[2304]{0:T(1024)S(1)} %copy-done.61, ...), kind=kOutput, calls=%fused_computation.35 | convolution fusion | flops 1371043584 | bytes 17123328 | tf_op jit(solution)/shard_map/dot_general | solution.py:805
  332.3 9.5 %shard_map.266.own_ref = f32[16,2304]{1,0:T(8,128)} custom-call(f32[256,2304]{1,0:T(8,128)} %get-tuple-element.166.dte_ref, f32[256,2304]{1,0:T(8,128)} %get-tuple-element.155.gs_ref, f32[16,2304]{1,0:T(8,128)} %get-tuple-element.171.rate_ref, f32[4096,128]{1,0:T(8,128)} %broadcast_in_dim.115.c_ref), custom_call_target="tpu_custom_call" | custom-call | flops 75497472 | bytes 4718592 | tf_op jit(solution)/shard_map/pallas_call | solution.py:133
  341.8 8.3 %chain.3.next_ref = f32[16,2304]{1,0:T(8,128)} custom-call(f32[16,2304]{1,0:T(8,128)} %get-tuple-element.65.carry_ref, f32[16,2304]{1,0:T(8,128)} %shard_map.266.own_ref), custom_call_target="tpu_custom_call" | custom-call | tf_op jit(solution)/shard_map/chain/pallas_call | solution.py:789
  350.1 47.6 %shard_map.267 = (f32[256,2304]{1,0:T(8,128)}, f32[256,2304]{1,0:T(8,128)}, f32[16,2304]{1,0:T(8,128)}, f32[256,256]{1,0:T(8,128)}, f32[256,256]{1,0:T(8,128)}) custom-call(f32[256,2304]{1,0:T(8,128)} %get-tuple-element.165.dt_ref, f32[256,2304]{1,0:T(8,128)} %get-tuple-element.166.dte_ref, f32[256,2304]{1,0:T(8,128)} %get-tuple-element.64.dtx_ref, ...), custom_call_target="tpu_custom_call" | custom-call | flops 245366784 | bytes 14155776 | tf_op jit(solution)/shard_map/pallas_call | solution.py:203
  397.8 4.5 fusion.85
  404.9 4.2 convolution_convert_fusion.1
  409.0 3.7 reduce-scatter.8.cloned.1.call-done
  419.4 8.1 %multiply_reduce_fusion.1 = (f32[2304]{0:T(1024)S(1)}, f32[2304]{0:T(1024)S(1)}, f32[2304]{0:T(1024)S(1)}, f32[2304]{0:T(1024)S(1)}, f32[2304]{0:T(1024)S(1)}, /...) fusion(f32[272,2304]{1,0:T(8,128)S(1)} %fusion.12, ...), kind=kOutput, calls=%fused_computation.36 | convolution fusion | flops 143475456 | bytes 28940288 | tf_op jit(solution)/shard_map/dot_general | solution.py:801
  446.5 5.4 fusion.39
  452.7 2.9 pack_small.1
  457.2 6.2 %convolution_convert_fusion = bf16[4608,1152]{1,0:T(8,128)(2,1)} fusion(bf16[256,2304]{1,0:T(8,128)(2,1)S(1)} %copy-done.78, bf16[256,2304]{1,0:T(8,128)(2,1)S(1)} %fusion.23, bf16[272,1152]{1,0:T(8,128)(2,1)S(1)} %copy-done.22), kind=kOutput, calls=%fused_computation | convolution fusion | flops 2727936000 | bytes 13565952 | tf_op jit(solution)/shard_map/dot_general | solution.py:809
  463.4 99.0 %scatter_all.1 = (f32[144,1152]{1,0:T(8,128)}, f32[80,256]{1,0:T(8,128)}, bf16[4,96,1152]{2,1,0:T(8,128)(2,1)}, bf16[4,96,1152]{2,1,0:T(8,128)(2,1)}) custom-call(bf16[4,2,4,144,1152]{4,3,2,1,0:T(8,128)(2,1)} %bitcast.66, bf16[4,2,4,80,256]{4,3,2,1,0:T(8,128)(2,1)} %bitcast.67, bf16[4,96,1152]{2,1,0:T(8,128)(2,1)} %bitcast.75, bf16[4,96,1152]{2,1,0:T(8,128)(2,1)} %bitcast.76), custom_call_target="tpu_custom_call" | custom-call | bytes 200000000 | tf_op jit(solution)/shard_map/scatter_all/pallas_call | solution.py:632
  562.4 4.7 finish.1
  567.2 3.0 copy.69
  (289 shorter events, 81.8 us)
Async XLA Ops:
  7.2 192.1 %all-gather.6.cloned.1.call-start = ((), (), s32[]{:S(2)}) async-start(), calls=%async_computation.7 | async-start | bytes 5474304 | tf_op jit(solution)/shard_map/all_gather | solution.py:858
  7.9 234.4 %all-gather.8.cloned.1.call-start = ((), (), s32[]{:S(2)}) async-start(), calls=%async_computation.10 | async-start | bytes 7962624 | tf_op jit(solution)/shard_map/all_gather | solution.py:870
  12.5 107.8 %copy-start.76 = (s32[1,256,1]{1,2,0:T(1,128)S(1)}, s32[1,256,1]{1,2,0:T(1,128)}, u32[]{:S(2)}) copy-start(s32[1,256,1]{1,2,0:T(1,128)} %param.18) | copy-start | bytes 3076
  13.4 107.2 %copy-start.12 = (bf16[1,256,1152]{2,1,0:T(8,128)(2,1)S(1)}, bf16[1,256,1152]{2,1,0:T(8,128)(2,1)}, u32[]{:S(2)}) copy-start(bf16[1,256,1152]{2,1,0:T(8,128)(2,1)} %param.19) | copy-start | bytes 1769476
  119.5 122.8 %all-gather.10.cloned.1.call-start = ((), (), s32[]{:S(2)}) async-start(), calls=%async_computation.11 | async-start | bytes 7962624 | tf_op jit(solution)/shard_map/all_gather | solution.py:871
  120.5 84.9 %copy-start.52 = (s32[256]{0:T(256)}, s32[256]{0:T(256)S(1)}, u32[]{:S(2)}) copy-start(s32[256]{0:T(256)S(1)} %convert_add_fusion) | copy-start | bytes 3076
  120.5 11.4 %copy-start.3 = (bf16[1,256,1152]{2,1,0:T(8,128)(2,1)S(1)}, bf16[1,256,1152]{2,1,0:T(8,128)(2,1)}, u32[]{:S(2)}) copy-start(bf16[1,256,1152]{2,1,0:T(8,128)(2,1)} %param.16) | copy-start | bytes 1769476
  122.2 31.6 %all-to-all-start = ((bf16[4,128,1152]{2,1,0:T(8,128)(2,1)}), bf16[4,128,1152]{2,1,0:T(8,128)(2,1)}, u32[]{:S(2)}, u32[]{:S(2)}) async-start(bf16[4,128,1152]{2,1,0:T(8,128)(2,1)} %bitcast.15), calls=%async_computation | async-start | bytes 2359296 | tf_op jit(solution)/shard_map/all_to_all | solution.py:830
  134.3 57.9 %copy-start.60 = (f32[2304]{0:T(1024)}, f32[2304]{0:T(1024)S(1)}, u32[]{:S(2)}) copy-start(f32[2304]{0:T(1024)S(1)} %get-tuple-element.147) | copy-start | bytes 27652
  134.5 70.9 %copy-start.26 = (f32[1152]{0:T(1024)}, f32[1152]{0:T(1024)S(1)}, u32[]{:S(2)}) copy-start(f32[1152]{0:T(1024)S(1)} %get-tuple-element.174) | copy-start | bytes 13828
  172.2 20.1 %copy-start.15 = (f32[256,2304]{1,0:T(8,128)S(1)}, f32[256,2304]{1,0:T(8,128)}, u32[]{:S(2)}) copy-start(f32[256,2304]{1,0:T(8,128)} %copy-done.14) | copy-start | bytes 7077892
  172.2 20.1 %copy-start.21 = (bf16[272,1152]{1,0:T(8,128)(2,1)S(1)}, bf16[272,1152]{1,0:T(8,128)(2,1)}, u32[]{:S(2)}) copy-start(bf16[272,1152]{1,0:T(8,128)(2,1)} %copy-done.20) | copy-start | bytes 1880068
  207.5 28.6 %all-to-all-start.1 = ((bf16[4,128,1152]{2,1,0:T(8,128)(2,1)}), bf16[4,128,1152]{2,1,0:T(8,128)(2,1)}, u32[]{:S(2)}, u32[]{:S(2)}) async-start(bf16[4,128,1152]{2,1,0:T(8,128)(2,1)} %bitcast.69), calls=%async_computation.1 | async-start | bytes 2359296 | tf_op jit(solution)/shard_map/all_to_all | solution.py:830
  213.3 195.7 %reduce-scatter.6.cloned.1.call-start = ((), (), s32[]{:S(2)}) async-start(), calls=%async_computation.8 | async-start | bytes 7962624 | tf_op jit(solution)/shard_map/reduce_scatter | solution.py:938
  272.7 140.1 %reduce-scatter.8.cloned.1.call-start = ((), (), s32[]{:S(2)}) async-start(), calls=%async_computation.9 | async-start | bytes 7962624 | tf_op jit(solution)/shard_map/reduce_scatter | solution.py:939
  278.5 30.1 %all-to-all-start.3 = ((bf16[4,128,1152]{2,1,0:T(8,128)(2,1)}), bf16[4,128,1152]{2,1,0:T(8,128)(2,1)}, u32[]{:S(2)}, u32[]{:S(2)}) async-start(bf16[4,128,1152]{2,1,0:T(8,128)(2,1)} %bitcast.68), calls=%async_computation.3 | async-start | bytes 2359296 | tf_op jit(solution)/shard_map/all_to_all | solution.py:830
  286.9 30.9 %copy-start.27 = (f32[1152]{0:T(1024)S(1)}, f32[1152]{0:T(1024)}, u32[]{:S(2)}) copy-start(f32[1152]{0:T(1024)} %copy-done.26) | copy-start | bytes 13828
  286.9 30.9 %copy-start.53 = (s32[256]{0:T(256)S(1)}, s32[256]{0:T(256)}, u32[]{:S(2)}) copy-start(s32[256]{0:T(256)} %copy-done.52) | copy-start | bytes 3076
  286.9 30.9 %copy-start.59 = (f32[256]{0:T(256)S(1)}, f32[256]{0:T(256)}, u32[]{:S(2)}) copy-start(f32[256]{0:T(256)} %copy-done.58) | copy-start | bytes 3076
  308.6 132.5 %all-to-all-start.2 = ((bf16[4,128,1152]{2,1,0:T(8,128)(2,1)}), bf16[4,128,1152]{2,1,0:T(8,128)(2,1)}, u32[]{:S(2)}, u32[]{:S(2)}) async-start(bf16[4,128,1152]{2,1,0:T(8,128)(2,1)} %bitcast.70), calls=%async_computation.2 | async-start | bytes 2359296 | tf_op jit(solution)/shard_map/all_to_all | solution.py:830
  317.7 255.7 %reduce-scatter.10.cloned.1.call-start = ((), (), s32[]{:S(2)}) async-start(), calls=%async_computation.12 | async-start | bytes 5474304
  350.0 47.7 %copy-start.10 = (f32[256,2304]{1,0:T(8,128)S(1)}, f32[256,2304]{1,0:T(8,128)}, u32[]{:S(2)}) copy-start(f32[256,2304]{1,0:T(8,128)} %get-tuple-element.191) | copy-start | bytes 7077892
  350.1 47.7 %copy-start.29 = (f32[2304]{0:T(1024)S(1)}, f32[2304]{0:T(1024)}, u32[]{:S(2)}) copy-start(f32[2304]{0:T(1024)} %copy-done.28) | copy-start | bytes 27652
  350.1 47.7 %copy-start.31 = (f32[2304]{0:T(1024)S(1)}, f32[2304]{0:T(1024)}, u32[]{:S(2)}) copy-start(f32[2304]{0:T(1024)} %copy-done.30) | copy-start | bytes 27652
  350.1 47.7 %copy-start.33 = (f32[2304]{0:T(1024)S(1)}, f32[2304]{0:T(1024)}, u32[]{:S(2)}) copy-start(f32[2304]{0:T(1024)} %copy-done.32) | copy-start | bytes 27652
  350.1 47.7 %copy-start.35 = (f32[2304]{0:T(1024)S(1)}, f32[2304]{0:T(1024)}, u32[]{:S(2)}) copy-start(f32[2304]{0:T(1024)} %copy-done.34) | copy-start | bytes 27652
  350.1 47.7 %copy-start.37 = (f32[2304]{0:T(1024)S(1)}, f32[2304]{0:T(1024)}, u32[]{:S(2)}) copy-start(f32[2304]{0:T(1024)} %copy-done.36) | copy-start | bytes 27652
  350.1 47.7 %copy-start.63 = (f32[256,1]{0,1:T(1,128)S(1)}, f32[256,1]{0,1:T(1,128)}, u32[]{:S(2)}) copy-start(f32[256,1]{0,1:T(1,128)} %copy-done.62) | copy-start | bytes 3076
  350.1 47.7 %copy-start.65 = (f32[256,1]{0,1:T(1,128)S(1)}, f32[256,1]{0,1:T(1,128)}, u32[]{:S(2)}) copy-start(f32[256,1]{0,1:T(1,128)} %copy-done.64) | copy-start | bytes 3076
  350.1 47.7 %copy-start.67 = (f32[256,1]{0,1:T(1,128)S(1)}, f32[256,1]{0,1:T(1,128)}, u32[]{:S(2)}) copy-start(f32[256,1]{0,1:T(1,128)} %copy-done.66) | copy-start | bytes 3076
  350.1 47.7 %copy-start.69 = (f32[256,1]{0,1:T(1,128)S(1)}, f32[256,1]{0,1:T(1,128)}, u32[]{:S(2)}) copy-start(f32[256,1]{0,1:T(1,128)} %copy-done.68) | copy-start | bytes 3076
  427.6 17.0 %collective-permute-start = (f32[8,2304]{1,0:T(8,128)S(1)}, f32[8,2304]{1,0:T(8,128)S(1)}, u32[]{:S(2)}, u32[]{:S(2)}) collective-permute-start(f32[8,2304]{1,0:T(8,128)S(1)} %pad_add_fusion.1), channel_id=1, source_target_pairs={{1,0},{2,1},{3,2},{5,4},{6,5},{7,6},{9,8},{10,9},{11,10},{13,12},{... | collective-permute-start | bytes 221192 | tf_op jit(solution)/shard_map/ppermute | solution.py:815
  (63 other events, 269.2 us)
Sparse Core Ops, SparseCore 0:
  10.9 84.7 all-gather.5
  119.7 51.8 all-gather.7
  173.5 48.8 all-gather.9
  272.8 70.4 reduce-scatter.5
  347.1 65.5 reduce-scatter.7
  418.3 138.9 reduce-scatter.9

commit v2 on v1

--- a/solution.py
+++ b/solution.py
@@ -222,39 +222,6 @@
     return jnp.sum(jnp.where(same, full, 0).reshape(rows, STEP, n), axis=1)
 
 
-def expert_kernel(slot_ref, grad_ref, up_ref, down_ref, out_ref, disp_ref, gup_ref, gdown_ref):
-    slots, grads, up, down = slot_ref[...], grad_ref[...], up_ref[...], down_ref[...]
-    hidden = lax.dot_general(slots, up, NT, preferred_element_type=F32)
-    phi = 0.5 * (1.0 + lax.erf(hidden * (1.0 / math.sqrt(2.0))))
-    act = (hidden * phi).astype(BF)
-    slope = phi + hidden * jnp.exp(hidden * hidden * -0.5) * (1.0 / math.sqrt(2.0 * math.pi))
-    gact = lax.dot_general(grads, down, NT, preferred_element_type=F32)
-    ghid = (gact * slope).astype(BF)
-    @pl.when(pl.program_id(0) == 0)
-    def _():
-        out_ref[...] = jnp.zeros_like(out_ref)
-        disp_ref[...] = jnp.zeros_like(disp_ref)
-    out_ref[...] += jnp.dot(act, down, preferred_element_type=F32)
-    disp_ref[...] += jnp.dot(ghid, up, preferred_element_type=F32)
-    gup_ref[...] = lax.dot_general(ghid, slots, TN, preferred_element_type=F32).astype(gup_ref.dtype)
-    gdown_ref[...] = lax.dot_general(act, grads, TN, preferred_element_type=F32).astype(gdown_ref.dtype)
-
-def expert_pass(slots, grads, up, down, block):
-    rows, width = slots.shape
-    units = up.shape[0]
-    whole = pl.BlockSpec((rows, width), lambda g: (0, 0))
-    part = pl.BlockSpec((block, width), lambda g: (g, 0))
-    return pl.pallas_call(
-        expert_kernel,
-        grid=(units // block,),
-        in_specs=[whole, whole, part, part],
-        out_specs=[whole, whole, part, part],
-        out_shape=[jax.ShapeDtypeStruct((rows, width), F32)] * 2 + [jax.ShapeDtypeStruct((units, width), BF)] * 2,
-        compiler_params=pltpu.CompilerParams(vmem_limit_bytes=VM),
-        cost_estimate=pl.CostEstimate(flops=12*rows*units*width, bytes_accessed=8*units*width + 12*rows*width, transcendentals=2*rows*units),
-    )(slots, grads, up, down)
-
-
 def flip(value, bit):
     return value + bit - 2 * bit * (lax.rem(value // bit, 2))
 
@@ -299,7 +266,7 @@
                 pltpu.make_async_remote_copy(src.at[z], dst.at[source], self.send.at[i, j - 1], self.recv.at[i, j - 1], device_id=(dp, source), device_id_type=MESH).wait_recv()
 
 
-def gather_kernel(parts, count, in_ref, rest_ref, up_ref, down_ref, tok_ref, ids_ref, gin_ref, grest_ref, gup_ref, gdown_ref, rim_ref, rimids_ref,
+def gather_kernel(parts, count, in_ref, rest_ref, up_ref, tok_ref, ids_ref, gin_ref, grest_ref, gup_ref, rim_ref, rimids_ref,
                   local_sem, send, recv, share_send, share_recv, pair_send, pair_recv, swap_local, swap_send, swap_recv, rim_send, rim_recv):
     dp, z = lax.axis_index("dp"), lax.axis_index("seq")
     chip, core = dp // 2, lax.rem(dp, 2)
@@ -322,19 +289,19 @@
         mine += [local, pair]
     for copy in mine:
         copy.wait()
-    swap = ZSwap(((up_ref, gup_ref), (down_ref, gdown_ref)), swap_local, swap_send, swap_recv, count)
+    swap = ZSwap(((up_ref, gup_ref),), swap_local, swap_send, swap_recv, count)
 
     def role(which, first_bit, second_bit):
-        chunks = parts[which]
+        subs = parts[which]
         first, second = (flip(dp, first_bit), z), (flip(dp, second_bit), z)
         first_chip, second_chip = flip(chip, first_bit // 2), flip(chip, second_bit // 2)
         both_chip = flip(first_chip, second_bit // 2)
 
-        def copies(at_chip, at_z, slot, to, send_s, recv_s):
+        def copies(sub, at_chip, at_z, slot, to, send_s, recv_s):
             made = []
-            for i, (ref, lo, size) in enumerate(chunks):
+            for i, (ref, lo, size) in enumerate(subs[sub]):
                 view = dsts[ref].at[at_chip, :, at_z, pl.ds(lo, size)]
-                made.append(pltpu.make_async_remote_copy(view, view, send_s.at[slot, i], recv_s.at[slot, i], device_id=to, device_id_type=MESH))
+                made.append(pltpu.make_async_remote_copy(view, view, send_s.at[sub, slot, i], recv_s.at[sub, slot, i], device_id=to, device_id_type=MESH))
             return made
 
         def start(made):
@@ -345,37 +312,38 @@
             for copy in made:
                 copy.wait_recv()
 
-        def along_first(k):
-            return copies(chip, k, 4 + k, first, send, recv)
-
-        def along_second(k, far):
-            return copies(first_chip if far else chip, k, 8 + 4 * far + k, second, send, recv)
-
-        def came_first(k):
-            return copies(first_chip, k, 4 + k, first, send, recv)
-
-        def came_second(k, far):
-            return copies(both_chip if far else second_chip, k, 8 + 4 * far + k, second, send, recv)
-
-        def share(at_chip, k, offset):
-            return copies(at_chip, k, 4 * offset + k, sibling, share_send, share_recv)
-
-        def spread(k):
-            start(along_second(k, 0))
-            start(along_first(k))
+        def along_first(sub, k):
+            return copies(sub, chip, k, 4 + k, first, send, recv)
+
+        def along_second(sub, k, far):
+            return copies(sub, first_chip if far else chip, k, 8 + 4 * far + k, second, send, recv)
+
+        def came_first(sub, k):
+            return copies(sub, first_chip, k, 4 + k, first, send, recv)
+
+        def came_second(sub, k, far):
+            return copies(sub, both_chip if far else second_chip, k, 8 + 4 * far + k, second, send, recv)
+
+        def share(sub, at_chip, k, offset):
+            return copies(sub, at_chip, k, 4 * offset + k, sibling, share_send, share_recv)
+
+        def up(sub, k):
+            return copies(sub, chip, k, k + count * 5, (dp, z + 1), send, recv)
+
+        def down(sub, k):
+            return copies(sub, chip, k, k, (dp, z - 1), send, recv)
+
+        both = range(len(subs))
+
+        def spread(sub, k):
+            start(along_first(sub, k))
+            start(along_second(sub, k, 0))
 
         def rest(k):
-            wait_recv(came_first(k))
-            start(along_second(k, 1))
-            start(share(first_chip, k, 1))
-
-        @pl.when(z > 0)
-        def _():
-            start(copies(chip, z, z, (dp, z - 1), send, recv))
-
-        @pl.when(z < count - 1)
-        def _():
-            start(copies(chip, z, z + count * 5, (dp, z + 1), send, recv))
+            for sub in both:
+                wait_recv(came_first(sub, k))
+                start(along_second(sub, k, 1))
+                start(share(sub, first_chip, k, 1))
 
         def below(hop, work):
             pl.when(z - hop >= 0)(lambda: work(z - hop))
@@ -384,80 +352,68 @@
             pl.when(z + hop <= count - 1)(lambda: work(z + hop))
 
         def from_below(k):
-            wait_recv(copies(chip, k, k + count * 5, (dp, z), send, recv))
-
-            @pl.when(z < count - 1)
-            def _():
-                start(copies(chip, k, k + count * 5, (dp, z + 1), send, recv))
-
-            spread(k)
-            start(share(chip, k, 0))
+            for sub in both:
+                wait_recv(up(sub, k))
+                pl.when(z < count - 1)(lambda: start(up(sub, k)))
+                spread(sub, k)
+                start(share(sub, chip, k, 0))
 
         def from_above(k):
-            wait_recv(copies(chip, k, k, (dp, z), send, recv))
-
-            @pl.when(z > 0)
-            def _():
-                start(copies(chip, k, k, (dp, z - 1), send, recv))
-
-            spread(k)
-            start(share(chip, k, 0))
-
-        spread(z)
+            for sub in both:
+                wait_recv(down(sub, k))
+                pl.when(z > 0)(lambda: start(down(sub, k)))
+                spread(sub, k)
+                start(share(sub, chip, k, 0))
+
+        for sub in both:
+            pl.when(z > 0)(lambda: start(down(sub, z)))
+            pl.when(z < count - 1)(lambda: start(up(sub, z)))
+            spread(sub, z)
         for hop in range(1, count):
             below(hop, from_below)
             above(hop, from_above)
+            if hop == count - 2:
+                swap.start()
             if hop == 1:
                 rest(z)
             else:
                 below(hop - 1, rest)
                 above(hop - 1, rest)
-        swap.start()
         below(count - 1, rest)
         above(count - 1, rest)
 
         def finish(k, _):
             for far in (0, 1):
-                wait_recv(came_second(k, far))
-                start(share(both_chip if far else second_chip, k, 2 + far))
+                for sub in both:
+                    wait_recv(came_second(sub, k, far))
+                    start(share(sub, both_chip if far else second_chip, k, 2 + far))
             return 0
 
         lax.fori_loop(0, count, finish, 0)
 
         def drain(k, _):
-            for copy in along_first(k) + along_second(k, 0) + along_second(k, 1):
-                copy.wait_send()
-            for offset, at_chip in enumerate((chip, first_chip, second_chip, both_chip)):
-                if offset:
-                    for copy in share(at_chip, k, offset):
-                        copy.wait_send()
-                else:
-                    @pl.when(k != z)
-                    def _():
-                        for copy in share(at_chip, k, offset):
-                            copy.wait_send()
-
-            @pl.when((k <= z) & (z < count - 1))
-            def _():
-                for copy in copies(chip, k, k + count * 5, (dp, z), send, recv):
+            def wait_send(made):
+                for copy in made:
                     copy.wait_send()
 
-            @pl.when((k >= z) & (z > 0))
-            def _():
-                for copy in copies(chip, k, k, (dp, z), send, recv):
-                    copy.wait_send()
+            for sub in both:
+                wait_send(along_first(sub, k) + along_second(sub, k, 0) + along_second(sub, k, 1))
+                for offset, at_chip in ((1, first_chip), (2, second_chip), (3, both_chip)):
+                    wait_send(share(sub, at_chip, k, offset))
+                pl.when(k != z)(lambda: wait_send(share(sub, chip, k, 0)))
+                pl.when((k <= z) & (z < count - 1))(lambda: wait_send(up(sub, k)))
+                pl.when((k >= z) & (z > 0))(lambda: wait_send(down(sub, k)))
             return 0
 
         lax.fori_loop(0, count, drain, 0)
-
-        other = parts[1 - which]
 
         def shared(k, _):
             for offset, at_chip in enumerate((chip, second_chip, first_chip, both_chip)):
                 def wait():
-                    for i, (ref, lo, size) in enumerate(other):
-                        view = dsts[ref].at[at_chip, :, k, pl.ds(lo, size)]
-                        pltpu.make_async_remote_copy(view, view, share_send.at[4 * offset + k, i], share_recv.at[4 * offset + k, i], device_id=sibling, device_id_type=MESH).wait_recv()
+                    for sub, chunks in enumerate(parts[1 - which]):
+                        for i, (ref, lo, size) in enumerate(chunks):
+                            view = dsts[ref].at[at_chip, :, k, pl.ds(lo, size)]
+                            pltpu.make_async_remote_copy(view, view, share_send.at[sub, 4 * offset + k, i], share_recv.at[sub, 4 * offset + k, i], device_id=sibling, device_id_type=MESH).wait_recv()
                 if offset:
                     wait()
                 else:
@@ -473,24 +429,24 @@
         copy.wait()
 
 
-def gather_all(w_in, rest, up, down, tok, ids, cut, count):
-    parts = (((0, 0, cut),), ((0, cut, w_in.shape[0] - cut), (1, 0, rest.shape[0])))
+def gather_all(w_in, rest, up, tok, ids, cut, count):
+    parts = ((((0, 0, 48),), ((0, 48, cut - 48),)), (((0, cut, 48),), ((0, cut + 48, w_in.shape[0] - cut - 48), (1, 0, rest.shape[0]))))
     shape = lambda a: jax.ShapeDtypeStruct((4, 2, count) + a.shape, a.dtype)
     sems = lambda *s: pltpu.SemaphoreType.DMA(s)
     return pl.pallas_call(
         functools.partial(gather_kernel, parts, count),
-        in_specs=[pl.BlockSpec(memory_space=pl.ANY)] * 6,
-        out_specs=[pl.BlockSpec(memory_space=pl.ANY)] * 6,
-        out_shape=[shape(w_in), shape(rest), jax.ShapeDtypeStruct(up.shape, up.dtype), jax.ShapeDtypeStruct(down.shape, down.dtype),
+        in_specs=[pl.BlockSpec(memory_space=pl.ANY)] * 5,
+        out_specs=[pl.BlockSpec(memory_space=pl.ANY)] * 5,
+        out_shape=[shape(w_in), shape(rest), jax.ShapeDtypeStruct(up.shape, up.dtype),
                    jax.ShapeDtypeStruct((16, tok.shape[1]), tok.dtype), jax.ShapeDtypeStruct(ids.shape, ids.dtype)],
-        scratch_shapes=[sems(2), sems(24, 2), sems(24, 2), sems(16, 2), sems(16, 2), sems(2), sems(2), sems(2), sems(2, count - 1), sems(2, count - 1), sems(2), sems(2)],
+        scratch_shapes=[sems(2), sems(2, 24, 2), sems(2, 24, 2), sems(2, 16, 2), sems(2, 16, 2), sems(2), sems(2), sems(1), sems(1, count - 1), sems(1, count - 1), sems(2), sems(2)],
         compiler_params=pltpu.CompilerParams(collective_id=1, has_side_effects=True),
         cost_estimate=pl.CostEstimate(flops=0, bytes_accessed=200_000_000, transcendentals=0),
         name="gather_all",
-    )(w_in, rest, up, down, tok, ids)
-
-
-def scatter_kernel(parts, count, in_ref, rest_ref, up_ref, down_ref, oin_ref, orest_ref, oup_ref, odown_ref, mine_a, mine_b, sib_a, sib_b, far_a, far_b, near_a, near_b, zgot_a, zgot_b, final_a, final_b,
+    )(w_in, rest, up, tok, ids)
+
+
+def scatter_kernel(parts, count, in_ref, rest_ref, proj_ref, oin_ref, orest_ref, oproj_ref, mine_a, mine_b, sib_a, sib_b, far_a, far_b, near_a, near_b, zgot_a, zgot_b, final_a, final_b,
                    load_sem, sib_send, sib_recv, two_send, two_recv, one_send, one_recv, z_send, z_recv, end_send, end_recv, end_local,
                    swap_local, swap_send, swap_recv):
     dp, z = lax.axis_index("dp"), lax.axis_index("seq")
@@ -501,7 +457,7 @@
     peers = [(dp, lax.rem(z + j, count)) for j in range(1, count)]
     greet([sibling, (flip(dp, 4), z), (flip(dp, 2), z)] + peers)
 
-    swap = ZSwap(((up_ref, oup_ref), (down_ref, odown_ref)), swap_local, swap_send, swap_recv, count)
+    swap = ZSwap(((proj_ref, oproj_ref),), swap_local, swap_send, swap_recv, count)
 
     def role(which, first_bit, second_bit):
         chunks, other = parts[which], parts[1 - which]
@@ -618,7 +574,7 @@
     swap.wait()
 
 
-def scatter_all(g_in, g_rest, up, down, cut, collective_id):
+def scatter_all(g_in, g_rest, proj, cut, collective_id):
     count = g_in.shape[2]
     rows_in, rows_rest = g_in.shape[3], g_rest.shape[3]
     parts = (((0, 0, cut),), ((0, cut, rows_in - cut), (1, 0, rows_rest)))
@@ -631,16 +587,16 @@
 
     return pl.pallas_call(
         functools.partial(scatter_kernel, parts, count),
-        in_specs=[pl.BlockSpec(memory_space=pl.ANY)] * 4,
-        out_specs=[pl.BlockSpec(memory_space=pl.ANY)] * 4,
-        out_shape=[jax.ShapeDtypeStruct(g_in.shape[3:], F32), jax.ShapeDtypeStruct(g_rest.shape[3:], F32), jax.ShapeDtypeStruct(up.shape, up.dtype), jax.ShapeDtypeStruct(down.shape, down.dtype)],
+        in_specs=[pl.BlockSpec(memory_space=pl.ANY)] * 3,
+        out_specs=[pl.BlockSpec(memory_space=pl.ANY)] * 3,
+        out_shape=[jax.ShapeDtypeStruct(g_in.shape[3:], F32), jax.ShapeDtypeStruct(g_rest.shape[3:], F32), jax.ShapeDtypeStruct(proj.shape, proj.dtype)],
         scratch_shapes=bufs(places) + bufs(places) + bufs(2 * count) + bufs(count) + bufs(count - 1) + bufs(0, F32)
         + [sems(places, 2), sems(places, 2), sems(places, 2), sems(2 * count, 2), sems(2 * count, 2), sems(count, 2), sems(count, 2),
-           sems(count - 1, 2), sems(count - 1, 2), sems(2, 2), sems(2, 2), sems(2), sems(2), sems(2, count - 1), sems(2, count - 1)],
+           sems(count - 1, 2), sems(count - 1, 2), sems(2, 2), sems(2, 2), sems(2), sems(1), sems(1, count - 1), sems(1, count - 1)],
         compiler_params=pltpu.CompilerParams(collective_id=collective_id, has_side_effects=True, vmem_limit_bytes=VM),
         cost_estimate=pl.CostEstimate(flops=0, bytes_accessed=200_000_000, transcendentals=0),
         name="scatter_all",
-    )(g_in, g_rest, up, down)
+    )(g_in, g_rest, proj)
 
 
 def unpack_kernel(own, width_b, pack_ref, low_ref, high_ref, small_ref, tall):
@@ -702,12 +658,12 @@
     )(x_t, dt_t, log_t, misc, small)
 
 
-def finish_kernel(own, cuts, pack_ref, up_ref, down_ref, up_out, down_out, row_out, *col_outs):
-    piece, width = up_ref.shape[1:]
+def finish_kernel(own, cuts, pack_ref, exp_ref, proj_ref, up_out, down_out, row_out, proj_out, *col_outs):
+    piece, width = exp_ref.shape[2:]
     filler = -piece % 128
 
-    down_out[0] = down_ref[0].astype(F32)
-    tall = up_ref[0].astype(F32)
+    down_out[0] = exp_ref[0, 1].astype(F32)
+    tall = exp_ref[0, 0].astype(F32)
     if filler:
         tall = jnp.concatenate([tall, jnp.zeros((filler, width), F32)], axis=0)
     for j in range(width // 128):
@@ -716,26 +672,27 @@
     @pl.when(pl.program_id(0) == 0)
     def _():
         row_out[...] = pack_ref[own : own + 1, :]
+        proj_out[...] = sum(proj_ref[k].astype(F32) for k in range(proj_ref.shape[0]))[:own]
         for (lo, size), out in zip(cuts, col_outs):
             out[...] = pack_ref[0:own, lo : lo + size]
 
 
-def finish(pack, up, down, own, cuts):
-    experts, piece, width = up.shape
+def finish(pack, both, proj, own, cuts):
+    experts, _, piece, width = both.shape
     if own % 8:
-        return [jnp.swapaxes(up.astype(F32), 1, 2), down.astype(F32), pack[own : own + 1]] + [pack[:own, lo : lo + size] for lo, size in cuts]
+        return [jnp.swapaxes(both[:, 0].astype(F32), 1, 2), both[:, 1].astype(F32), pack[own : own + 1], jnp.sum(proj[:, :own].astype(F32), axis=0)] + [pack[:own, lo : lo + size] for lo, size in cuts]
     whole = lambda shape: pl.BlockSpec(shape, lambda e: (0,) * len(shape))
     part = lambda shape: pl.BlockSpec((1,) + shape[1:], lambda e: (e, 0, 0))
-    shapes = [(experts, width, piece), (experts, piece, width), (1, pack.shape[1])] + [(own, size) for _, size in cuts]
+    shapes = [(experts, width, piece), (experts, piece, width), (1, pack.shape[1]), (own, width)] + [(own, size) for _, size in cuts]
     return pl.pallas_call(
         functools.partial(finish_kernel, own, cuts),
         grid=(experts,),
-        in_specs=[whole(pack.shape), part(up.shape), part(down.shape)],
+        in_specs=[whole(pack.shape), pl.BlockSpec((1,) + both.shape[1:], lambda e: (e, 0, 0, 0)), whole(proj.shape)],
         out_specs=[part(shapes[0]), part(shapes[1])] + [whole(s) for s in shapes[2:]],
         out_shape=[jax.ShapeDtypeStruct(s, F32) for s in shapes],
         compiler_params=pltpu.CompilerParams(vmem_limit_bytes=VM),
         name="finish",
-    )(pack, up, down)
+    )(pack, both, proj)
 
 
 def chain_kernel(step, pieces, carry_ref, own_ref, out_ref, inbox, outbox, send, recv):
@@ -795,6 +752,148 @@
         compiler_params=pltpu.CompilerParams(collective_id=collective_id, has_side_effects=True),
         name="chain",
     )(carry, own)
+
+
+def experts_kernel(block, piece, pick_ref, n2_ref, go_ref, router_ref, up_hbm, down_hbm, back_ref, late_ref, mixed_ref, grouter_ref, gexp_hbm,
+                   up, down, gup, gdown, outbox, inbox, ret, total, disp, load_sem, store_sem, own_sem, out_send, out_recv, back_own, back_send, back_recv):
+    dp, z = lax.axis_index("dp"), lax.axis_index("seq")
+    count = lax.axis_size("seq")
+    peers = [lax.rem(z + j, count) for j in range(1, count)]
+    blocks = up.shape[0] // block
+    rows, width = total.shape
+    each = rows // count
+
+    def loads(b):
+        at = pl.ds(pl.multiple_of(b * block, block), block)
+        return [pltpu.make_async_copy(up_hbm.at[at], up.at[at], load_sem.at[b, 0]), pltpu.make_async_copy(down_hbm.at[at], down.at[at], load_sem.at[b, 1])]
+
+    def stores(b):
+        made = []
+        for i in range(block // piece):
+            at = pl.ds(pl.multiple_of(b * block + i * piece, 16), piece)
+            to = b * (block // piece) + i
+            made.append(pltpu.make_async_copy(gup.at[at], gexp_hbm.at[to, 0], store_sem.at[to, 0]))
+            made.append(pltpu.make_async_copy(gdown.at[at], gexp_hbm.at[to, 1], store_sem.at[to, 1]))
+        return made
+
+    def send(half, j):
+        return pltpu.make_async_remote_copy(outbox.at[half, peers[j]], inbox.at[half, z], out_send.at[half, j], out_recv.at[half, j], device_id=(dp, peers[j]), device_id_type=MESH)
+
+    def came(half, j):
+        return pltpu.make_async_remote_copy(outbox.at[half, z], inbox.at[half, lax.rem(z + count - 1 - j, count)], out_send.at[half, j], out_recv.at[half, j], device_id=(dp, z), device_id_type=MESH)
+
+    def kept(half):
+        return pltpu.make_async_copy(outbox.at[half, z], inbox.at[half, z], own_sem.at[half])
+
+    def give(half, j):
+        return pltpu.make_async_remote_copy(ret.at[half, peers[j]], back_ref.at[z], back_send.at[half, j], back_recv.at[half, j], device_id=(dp, peers[j]), device_id_type=MESH)
+
+    def got(half, j):
+        return pltpu.make_async_remote_copy(ret.at[half, z], back_ref.at[lax.rem(z + count - 1 - j, count)], back_send.at[half, j], back_recv.at[half, j], device_id=(dp, z), device_id_type=MESH)
+
+    def give_own(half):
+        return pltpu.make_async_copy(ret.at[half, z], back_ref.at[z], back_own.at[half])
+
+    greet([(dp, peer) for peer in peers])
+    for half in range(2):
+        picked = lax.dot_general(pick_ref[:, half * rows : (half + 1) * rows], n2_ref[...], TN, preferred_element_type=F32)
+        outbox[half] = picked.astype(BF).reshape(count, each, width)
+        for j in range(count - 1):
+            send(half, j).start()
+        kept(half).start()
+    for b in range(blocks):
+        for copy in loads(b):
+            copy.start()
+    lanes = lax.broadcasted_iota(jnp.int32, (rows, router_ref.shape[1]), 1)
+    mine = (lanes == z).astype(F32)
+    for half in range(2):
+        kept(half).wait()
+        for j in range(count - 1):
+            came(half, j).wait_recv()
+        slots = inbox[half].reshape(rows, width)
+        go = go_ref[:, half * each : (half + 1) * each, :].reshape(rows, width).astype(F32)
+        logits = jnp.where(lanes < count, jnp.dot(slots, router_ref[...], preferred_element_type=F32), -1e30)
+        powers = jnp.exp(logits - jnp.max(logits, axis=1, keepdims=True))
+        probs = jnp.where(lanes < count, powers / jnp.sum(powers, axis=1, keepdims=True), 0.0)
+        gate = jnp.sum(probs * mine, axis=1, keepdims=True)
+        grads = (gate * go).astype(BF)
+        total[...] = jnp.zeros_like(total)
+        disp[...] = jnp.zeros_like(disp)
+
+        def units(b, _):
+            at = pl.ds(pl.multiple_of(b * block, block), block)
+            if half == 0:
+                for copy in loads(b):
+                    copy.wait()
+            hidden = lax.dot_general(slots, up[at, :], NT, preferred_element_type=F32)
+            phi = 0.5 * (1.0 + lax.erf(hidden * (1.0 / math.sqrt(2.0))))
+            act = (hidden * phi).astype(BF)
+            slope = phi + hidden * jnp.exp(hidden * hidden * -0.5) * (1.0 / math.sqrt(2.0 * math.pi))
+            ghid = (lax.dot_general(grads, down[at, :], NT, preferred_element_type=F32) * slope).astype(BF)
+            total[...] += jnp.dot(act, down[at, :], preferred_element_type=F32)
+            disp[...] += jnp.dot(ghid, up[at, :], preferred_element_type=F32)
+            new_up = lax.dot_general(ghid, slots, TN, preferred_element_type=F32)
+            new_down = lax.dot_general(act, grads, TN, preferred_element_type=F32)
+            if half == 0:
+                gup[at, :] = new_up.astype(BF)
+                gdown[at, :] = new_down.astype(BF)
+            else:
+                gup[at, :] = (gup[at, :].astype(F32) + new_up).astype(BF)
+                gdown[at, :] = (gdown[at, :].astype(F32) + new_down).astype(BF)
+                for copy in stores(b):
+                    copy.start()
+            return 0
+
+        lax.fori_loop(0, blocks, units, 0)
+        expert_out = total[...]
+        mixed_ref[:, half * each : (half + 1) * each, :] = (gate * expert_out).astype(BF).reshape(count, each, width)
+        grad_gate = jnp.sum(go * expert_out, axis=1, keepdims=True)
+        grad_logits = (grad_gate * gate * (mine - probs)).astype(BF)
+        grad_n2 = disp[...] + lax.dot_general(grad_logits, router_ref[...], NT, preferred_element_type=F32)
+        if half == 0:
+            ret[half] = grad_n2.astype(BF).reshape(count, each, width)
+            for j in range(count - 1):
+                give(half, j).start()
+            give_own(half).start()
+        else:
+            late_ref[...] = grad_n2.astype(BF).reshape(count, each, width)
+        grouter = lax.dot_general(slots, grad_logits, TN, preferred_element_type=F32)
+        if half == 0:
+            grouter_ref[...] = grouter
+        else:
+            grouter_ref[...] += grouter
+    for b in range(blocks):
+        for copy in stores(b):
+            copy.wait()
+    give_own(0).wait()
+    for j in range(count - 1):
+        send(0, j).wait_send()
+        send(1, j).wait_send()
+        give(0, j).wait_send()
+        got(0, j).wait_recv()
+
+
+def experts_pass(pick, n2, go, router, up, down, block, piece, collective_id):
+    count, slots, width = go.shape
+    units = up.shape[0]
+    rows = count * slots // 2
+    vmem = pl.BlockSpec(memory_space=pltpu.VMEM)
+    hbm = pl.BlockSpec(memory_space=pl.ANY)
+    sems = lambda *s: pltpu.SemaphoreType.DMA(s)
+    blocks = units // block
+    return pl.pallas_call(
+        functools.partial(experts_kernel, block, piece),
+        in_specs=[vmem] * 4 + [hbm] * 2,
+        out_specs=[hbm, vmem, vmem, vmem, hbm],
+        out_shape=[jax.ShapeDtypeStruct((count, slots // 2, width), BF)] * 2 + [jax.ShapeDtypeStruct((count, slots, width), BF), jax.ShapeDtypeStruct(router.shape, F32),
+                   jax.ShapeDtypeStruct((units // piece, 2, piece, width), BF)],
+        scratch_shapes=[pltpu.VMEM(up.shape, BF)] * 4
+        + [pltpu.VMEM((2, count, slots // 2, width), BF)] * 2 + [pltpu.VMEM((1, count, slots // 2, width), BF)] + [pltpu.VMEM((rows, width), F32)] * 2
+        + [sems(blocks, 2), sems(units // piece, 2), sems(2), sems(2, count - 1), sems(2, count - 1), sems(1), sems(1, count - 1), sems(1, count - 1)],
+        compiler_params=pltpu.CompilerParams(collective_id=collective_id, has_side_effects=True, vmem_limit_bytes=VM),
+        cost_estimate=pl.CostEstimate(flops=24 * rows * units * width, bytes_accessed=100_000_000, transcendentals=4 * rows * units),
+        name="experts",
+    )(pick, n2, go, router, up, down)
 
 
 def dot(a, b):
@@ -858,17 +957,19 @@
     full_out = lax.all_gather(w_out, both, axis=0, tiled=True)
     if direct:
         last_ids = jnp.broadcast_to(seg_plus[rows - halo :, None], (halo, 128))
-        all_in, all_pack, part_up, part_down, rim_tok, rim_ids = gather_all(w_in, packed, up_t, w_down, tok_b, last_ids, 80, 4)
+        all_in, all_pack, part_up, rim_tok, rim_ids = gather_all(w_in, packed, up_t, tok_b, last_ids, 80, 4)
+        down_late, all_in = lax.optimization_barrier((w_down, all_in))
+        part_down = swap(down_late)
         rim_ids = jnp.where(lax.axis_index("seq") > 0, rim_ids[:, 0], 0)
     else:
         all_in, all_pack = lax.all_gather(w_in, both), lax.all_gather(packed, both)
         part_up, part_down = swap(up_t), swap(w_down)
         rim_tok = shift(tok_b[rows - halo :], "seq", 1)
         rim_ids = shift(seg_plus[rows - halo :], "seq", 1)
-    full_in = all_in.reshape(2 * chans, width)
+    full_in = lax.optimization_barrier(all_in.reshape(2 * chans, width))
     low_t, high_t, small = unpack(all_pack.reshape(devices, -1, 256), own, rank + w_x.shape[1])
+    small, part_up = lax.optimization_barrier((small, part_up))
     full_up = lax.all_gather(part_up, "dp", axis=0).reshape(-1, width)
-    full_down = lax.all_gather(part_down, "dp", axis=0).reshape(-1, width)
     xcols = w_x.shape[1]
     full_x_t, full_dt_t = low_t[:xcols], low_t[xcols:]
     alog_t, conv_f, bias_row, dtb_row, skip = high_t[:n], high_t[n : n + taps], high_t[n + taps : n + taps + 1], high_t[n + taps + 1 : n + taps + 2], high_t[n + taps + 2 : n + taps + 3]
@@ -882,11 +983,11 @@
     place = jnp.sum(dot(before, onehot) * onehot.astype(F32), axis=1).astype(jnp.int32)
     slot_of = route_ids[:, 0] * slots + place
     gather_mat = (slot_of[:, None] == jnp.arange(experts * slots)[None, :]).astype(BF)
+    half = slots // 2
+    pick_of = place // half * (experts * half) + route_ids[:, 0] * half + place % half
+    pick = (pick_of[:, None] == jnp.arange(experts * slots)[None, :]).astype(BF)
     grad_out_b = cotangent[0]
     grad_out = grad_out_b.astype(F32)
-    go_local, full_in = lax.optimization_barrier((dot_tn(gather_mat, grad_out_b).astype(BF), full_in))
-    go_slots = swap(go_local.reshape(experts, slots, width)).reshape(-1, width)
-
     tok_ext = jnp.concatenate([rim_tok, tok_b]).astype(F32)
     tok_f = tok_b.astype(F32)
     ids_ext = jnp.concatenate([rim_ids, seg_plus])
@@ -909,34 +1010,34 @@
     pre_dt = dot(low_rank, full_dt_t) + dtb_row
     dt = jax.nn.softplus(pre_dt)
     dt_keep = jnp.where(keep > 0, dt, 1e30)
-    dtx, go_slots = lax.optimization_barrier((dt * values, go_slots))
+    dtx = dt * values
     rates = -jnp.exp(alog_t)
     rates2 = rates * math.log2(math.e)
     b_wide = jnp.broadcast_to(b_rows[:, :, None], (rows, n, 128)).reshape(rows * n, 128)
     c_wide = jnp.broadcast_to(c_rows[:, :, None], (rows, n, 128)).reshape(rows * n, 128)
     own_state, carry = state_pass(dt_keep, dtx, rates2, b_wide, wide)
+    carry, part_down = lax.optimization_barrier((carry, part_down))
+    full_down = lax.all_gather(part_down, "dp", axis=0).reshape(-1, width)
     start = chain(carry, own_state, 1, 3)
+    go_local, start = lax.optimization_barrier((dot_tn(gather_mat, grad_out_b).astype(BF), start))
+    go_slots = swap(go_local.reshape(experts, slots, width))
     scanned, checks = scan_pass(dt_keep, dtx, rates2, b_wide, block_diag(c_rows).astype(BF), start, wide)
+    scanned, go_slots = lax.optimization_barrier((scanned, go_slots))
     sig_z = jax.nn.sigmoid(z)
     gated = ((scanned + skip * values) * (z * sig_z)).astype(BF)
     first_sum = tok_f + dot(gated, full_out)
     normed_two = (first_sum * rms_scale(first_sum) * gain_two).astype(BF)
 
-    n2_slots = swap(dot_tn(gather_mat, normed_two).astype(BF).reshape(experts, slots, width)).reshape(-1, width)
-    probs = jax.nn.softmax(dot(n2_slots, router), axis=-1)
-    mine = (jnp.arange(experts) == lax.axis_index("seq")).astype(F32)[None]
-    gate = jnp.sum(probs * mine, axis=1, keepdims=True)
-    ge_slots = (gate * go_slots.astype(F32)).astype(BF)
-    expert_out, grad_disp, grad_up, grad_down = expert_pass(n2_slots, ge_slots, full_up, full_down, 768)
-    grad_gate = jnp.sum(go_slots.astype(F32) * expert_out, axis=1, keepdims=True)
-    grad_logits = (grad_gate * gate * (mine - probs)).astype(BF)
-    grad_router = dot_tn(n2_slots, grad_logits)
-    grad_n2_slots = (grad_disp + dot_nt(grad_logits, router)).astype(BF)
-    grad_n2 = dot(gather_mat, swap(grad_n2_slots.reshape(experts, slots, width)).reshape(-1, width))
-    mixed_slots = swap((gate * expert_out).astype(BF).reshape(experts, slots, width)).reshape(-1, width)
-    mixed_out = (first_sum + dot(gather_mat, mixed_slots)).astype(BF)
-    part_gup = lax.psum_scatter(grad_up, "dp", scatter_dimension=0, tiled=True).reshape(experts, -1, width)
-    part_gdown = lax.psum_scatter(grad_down, "dp", scatter_dimension=0, tiled=True).reshape(experts, -1, width)
+    piece = w_up.shape[2]
+    router_wide = jnp.pad(router, ((0, 0), (0, 128 - experts)))
+    back_n2, late_n2, mixed_back, grad_router, grad_exp = experts_pass(pick, normed_two, go_slots, router_wide, full_up, full_down, 768, piece if piece % 16 == 0 else 768, 5)
+    grad_router = grad_router[:, :experts]
+    late_n2 = swap(late_n2)
+    grad_n2 = dot(pick, jnp.concatenate([back_n2.reshape(-1, width), late_n2.reshape(-1, width)]))
+    mixed_slots = swap(mixed_back).reshape(-1, width)
+    if piece % 16:
+        grad_exp = jnp.swapaxes(jnp.swapaxes(grad_exp, 0, 1).reshape(2, -1, piece, width), 0, 1)
+    part_exp = lax.psum_scatter(grad_exp, "dp", scatter_dimension=0, tiled=True)
 
     grad_norm_two, grad_gain_two = rms_back(first_sum, gain_two, grad_n2)
     grad_first = grad_out + grad_norm_two
@@ -954,6 +1055,9 @@
     g_dtx, g_dt, g_log, gb_full, gc_full = back_pass(
         dt, dt_keep, dtx, grad_scanned, rates2, rates, b_wide, c_wide, block_diag(b_rows).astype(BF), ones_blk, checks, nxt, wide
     )
+    g_dtx, mixed_slots, part_exp, grad_w_out = lax.optimization_barrier((g_dtx, mixed_slots, part_exp, grad_w_out.astype(BF)))
+    sum_exp = swap(part_exp)
+    mixed_out = (first_sum + dot(gather_mat, mixed_slots)).astype(BF)
     grad_dt = g_dt + g_dtx * values
     grad_pre_f = grad_dt * jax.nn.sigmoid(pre_dt)
     grad_dtb = jnp.sum(grad_pre_f, axis=0)
@@ -983,21 +1087,22 @@
     grad_small = jnp.concatenate([grad_gain_one, grad_gain_two, grad_router.reshape(-1)])
     misc = jnp.stack(grad_taps + [grad_bias, grad_dtb, grad_skip, jnp.zeros_like(grad_bias)])
     grad_packed = pack_grads(grad_x_t, grad_dt_t, g_log, misc, jnp.pad(grad_small.reshape(devices, -1), ((0, 0), (0, 256 - share))), own)
+    part_out = lax.psum_scatter(grad_w_out, "dp", scatter_dimension=0, tiled=True).reshape(-1, own, width)
+    part_out = jnp.pad(part_out, ((0, 0), (0, -own % 16), (0, 0)))
     if direct:
-        sum_in, sum_pack, sum_up, sum_down = scatter_all(
-            grad_w_in.reshape(4, 2, 4, 2 * own, width), grad_packed.reshape((4, 2, 4) + grad_packed.shape[1:]), part_gup, part_gdown, 80, 2
+        grad_packed, sum_exp = lax.optimization_barrier((grad_packed, sum_exp))
+        sum_in, sum_pack, all_out = scatter_all(
+            grad_w_in.reshape(4, 2, 4, 2 * own, width), grad_packed.reshape((4, 2, 4) + grad_packed.shape[1:]), part_out, 80, 2
         )
     else:
         sum_in = lax.psum_scatter(grad_w_in, both, scatter_dimension=0, tiled=True).astype(F32)
         sum_pack = lax.psum_scatter(grad_packed, both, scatter_dimension=0, tiled=True)[0].astype(F32)
-        sum_up, sum_down = swap(part_gup), swap(part_gdown)
-    grad_w_out = lax.optimization_barrier((grad_w_out.astype(BF), part_gup, part_gdown))[0]
-    sum_out = lax.psum_scatter(grad_w_out, both, scatter_dimension=0, tiled=True).astype(F32)
+        all_out = swap(part_out)
     cuts, at = [], 0
     for column in columns:
         cuts.append((at, column.shape[1]))
         at += column.shape[1]
-    up_out, down_out, s_row, s_x, s_dt, s_log, s_conv, s_bias, s_dtb, s_skip = finish(sum_pack, sum_up, sum_down, own, tuple(cuts))
+    up_out, down_out, s_row, sum_out, s_x, s_dt, s_log, s_conv, s_bias, s_dtb, s_skip = finish(sum_pack, sum_exp, all_out, own, tuple(cuts))
     return (
         mixed_out[None],
         tokens_grad[None],

time: 594 us -> 546 us (0.919)
  Pallas kernels: 346 us -> 323 us
  waiting for transfers between devices: 43.6 us -> 27.3 us
  matrix products: 79.7 us -> 71.4 us
  other arithmetic: 32.2 us -> 25.6 us
  starting transfers between devices: 30.5 us -> 36.9 us
    pallas_call x1, Pallas kernels: 99 us -> 69.3 us  [scatter_all(): pl.pallas_call(functools.partial(scatter_kernel, parts, count), in_specs=...]
    pallas_call x1, Pallas kernels: 30.3 us -> 57.2 us  [experts_pass(): pl.pallas_call(functools.partial(experts_kernel, block, piece), in_specs=...]
    pallas_call x1, Pallas kernels: 104 us -> 84.1 us  [gather_all(): pl.pallas_call(functools.partial(gather_kernel, parts, count), in_specs=[...]
    all_to_all x4 -> x5, waiting for transfers between devices: 38 us -> 25.1 us  [swap(): return lax.all_to_all(value, 'seq', 0, 0)]
    dot_general x9 -> x8, matrix products: 36.8 us -> 32.2 us  [dot(): return jnp.dot(a, b, preferred_element_type=F32)]
    all_to_all x4 -> x5, starting transfers between devices: 27.7 us -> 32.2 us  [swap(): return lax.all_to_all(value, 'seq', 0, 0)]
    dot_general x7 -> x5, matrix products: 19.6 us -> 17.7 us  [dot_tn(): return lax.dot_general(a, b, TN, preferred_element_type=F32)]
    dot_general x6 -> x5, matrix products: 23.3 us -> 21.5 us  [dot_nt(): return lax.dot_general(a, b, NT, preferred_element_type=F32)]
  transfers between devices with their start and end apart: 11 -> 11, of which waited for: 3 -> 3; matrix products, arithmetic and copies ran while one was open for 23% -> 22% of each run, Pallas kernels for 54% -> 36%
where the time goes in v2:
time: 546 us; the launch traced here: 539 us
  Pallas kernels  323 us (59%)
  matrix products  71.4 us (13%)
  local copies, waits for them, and re-layouts  39.3 us (7%)
  starting transfers between devices  36.9 us (7%)
  waiting for transfers between devices  27.3 us (5%)
  other arithmetic  25.6 us (5%)
  between operations  14.9 us (3%)
    pallas_call x1, Pallas kernels, gather_all(): pl.pallas_call(functools.partial(gather_kernel, parts, count), in_specs=[...  84.1 us
    pallas_call x1, Pallas kernels, scatter_all(): pl.pallas_call(functools.partial(scatter_kernel, parts, count), in_specs=...  69.3 us
    pallas_call x1, Pallas kernels, experts_pass(): pl.pallas_call(functools.partial(experts_kernel, block, piece), in_specs=...  57.2 us
    pallas_call x1, Pallas kernels, back_pass(): pl.pallas_call(functools.partial(back_kernel, n), grid=(chans // wide,),...  47.1 us
    all_to_all x5, starting transfers between devices, swap(): return lax.all_to_all(value, 'seq', 0, 0)  32.2 us
    dot_general x8, matrix products, dot(): return jnp.dot(a, b, preferred_element_type=F32)  32.2 us
    all_to_all x5, waiting for transfers between devices, swap(): return lax.all_to_all(value, 'seq', 0, 0)  25.1 us
    dot_general x5, matrix products, dot_nt(): return lax.dot_general(a, b, NT, preferred_element_type=F32)  21.5 us
  transfers between devices with their start and end apart: 11, of which 3 were waited for; matrix products, arithmetic and copies ran while one was open for 22% of the time, Pallas kernels for 36%

profile of v2, /device:TPU:9, one launch (start us, length us, event | category | flops | bytes accessed | tf_op | source)
XLA Modules:
  0.0 538.7 jit_solution(984463209851152977)
XLA Ops:
  15.4 84.1 %gather_all.1 = (bf16[4,2,4,144,1152]{4,3,2,1,0:T(8,128)(2,1)}, bf16[4,2,4,80,256]{4,3,2,1,0:T(8,128)(2,1)}, bf16[4,96,1152]{2,1,0:T(8,128)(2,1)}, bf16[16,1152]{1,0:T(8,128)(2,1)}, s32[16,128]{1,0:T(8,128)}) custom-call(bf16[144,1152]{1,0:T(8,128)(2,1)} %in_ref.1, bf16[80,256]{1,0:T(8,128)(2,1)} %pad_add_fusion.2.rest_ref, bf16[4,96,1152]{2,1,0:T(8,128)(2,1)} %bitcast.65, ...), custom_call_target="tpu_custom_call" | custom-call | bytes 200000000 | tf_op jit(solution)/shard_map/gather_all/pallas_call | solution.py:436
  99.6 2.9 unpack_small.1
  102.5 11.5 %all-to-all-start = ((bf16[4,96,1152]{2,1,0:T(8,128)(2,1)}), bf16[4,96,1152]{2,1,0:T(8,128)(2,1)}, u32[]{:S(2)}, u32[]{:S(2)}) async-start(bf16[4,96,1152]{2,1,0:T(8,128)(2,1)} %param.31), calls=%async_computation | async-start | bytes 1769472 | tf_op jit(solution)/shard_map/all_to_all | solution.py:929
  118.1 4.6 fusion.12
  126.1 7.4 %compare_select_fusion = (f32[256,2304]{1,0:T(8,128)}, f32[256,2304]{1,0:T(8,128)}, f32[256,2304]{1,0:T(8,128)}, f32[256,2304]{1,0:T(8,128)}) fusion(pred[256]{0:T(512)(128)(4,1)S(1)} %compare_reduce_fusion, f32[256,2304]{1,0:T(8,128)} %copy-done.9, f32[2304]{0:T(1024)S(1)} %get-tuple-element.170, bf16[176,2304]{1,0:T(8,128)(2,1)} %get-tuple-element.75, ...), kind=kOutput, calls=%fused_computation.2 | convolution fusion | flops 92602368 | bytes 12177920 | tf_op jit(solution)/shard_map/dot_general | solution.py:900
  137.2 9.7 %shard_map.263 = (f32[16,2304]{1,0:T(8,128)}, f32[16,2304]{1,0:T(8,128)}) custom-call(f32[256,2304]{1,0:T(8,128)} %get-tuple-element.186.dte_ref, f32[256,2304]{1,0:T(8,128)} %get-tuple-element.187.dtx_ref, f32[16,2304]{1,0:T(8,128)} %get-tuple-element.189.rate_ref, f32[4096,128]{1,0:T(8,128)} %broadcast_in_dim.108.b_ref), custom_call_target="tpu_custom_call" | custom-call | flops 75497472 | bytes 4718592 | tf_op jit(solution)/shard_map/pallas_call | solution.py:51
  150.5 6.1 %chain.2.start_ref = f32[16,2304]{1,0:T(8,128)} custom-call(f32[16,2304]{1,0:T(8,128)} %get-tuple-element.78.carry_ref, f32[16,2304]{1,0:T(8,128)} %get-tuple-element.79.own_ref), custom_call_target="tpu_custom_call" | custom-call | tf_op jit(solution)/shard_map/chain/pallas_call | solution.py:746
  156.6 6.7 %all-to-all-start.1 = ((bf16[4,128,1152]{2,1,0:T(8,128)(2,1)}), bf16[4,128,1152]{2,1,0:T(8,128)(2,1)}, u32[]{:S(2)}, u32[]{:S(2)}) async-start(bf16[4,128,1152]{2,1,0:T(8,128)(2,1)} %bitcast.61), calls=%async_computation.1 | async-start | bytes 2359296 | tf_op jit(solution)/shard_map/all_to_all | solution.py:929
  170.6 20.3 %shard_map.264 = (f32[256,2304]{1,0:T(8,128)}, f32[256,2304]{1,0:T(8,128)}) custom-call(f32[256,2304]{1,0:T(8,128)} %get-tuple-element.186.dte_ref, f32[256,2304]{1,0:T(8,128)} %get-tuple-element.187.dtx_ref, f32[16,2304]{1,0:T(8,128)} %get-tuple-element.189.rate_ref, f32[4096,128]{1,0:T(8,128)} %broadcast_in_dim.108.b_ref, ...), custom_call_target="tpu_custom_call" | custom-call | flops 94371840 | bytes 7077888 | tf_op jit(solution)/shard_map/pallas_call | solution.py:91
  190.9 8.0 %multiply_convert_fusion.1 = (bf16[256,2304]{1,0:T(8,128)(2,1)}, f32[256,2304]{1,0:T(8,128)}) fusion(f32[256,2304]{1,0:T(8,128)} %get-tuple-element.83, f32[2304]{0:T(1024)S(1)} %copy-done.36, f32[256,2304]{1,0:T(8,128)} %copy-done.9, bf16[4608,1152]{1,0:T(8,128)(2,1)} %bitcast.91, bf16[272,1152]{1,0:T(8,128)(2,1)} %copy-done.15), kind=kOutput, calls=%fused_computation.35 | convolution fusion | flops 1366032384 | bytes 14164992 | tf_op jit(solution)/shard_map/dot_general | solution.py:904
  198.8 4.8 multiply_reduce_fusion.7
  207.1 57.2 %experts.1 = (bf16[4,64,1152]{2,1,0:T(8,128)(2,1)}, bf16[4,64,1152]{2,1,0:T(8,128)(2,1)}, bf16[4,128,1152]{2,1,0:T(8,128)(2,1)}, f32[1152,128]{1,0:T(8,128)}, bf16[32,2,96,1152]{3,2,1,0:T(8,128)(2,1)}) custom-call(bf16[256,512]{1,0:T(8,128)(2,1)} %fusion.51.pick_ref, bf16[256,1152]{1,0:T(8,128)(2,1)} %multiply_convert_fusion.2.n2_ref, ...), custom_call_target="tpu_custom_call" | custom-call | flops 21743271936 | bytes 100000000 | tf_op jit(solution)/shard_map/experts/pallas_call | solution.py:884
  264.4 4.2 all-to-all-start.2
  271.0 9.6 %all-to-all-done.2 = bf16[4,64,1152]{2,1,0:T(8,128)(2,1)} async-done(((bf16[4,64,1152]{2,1,0:T(8,128)(2,1)}), bf16[4,64,1152]{2,1,0:T(8,128)(2,1)}, u32[]{:S(2)}, u32[]{:S(2)}) %all-to-all-start.2) | async-done | bytes 589856 | tf_op jit(solution)/shard_map/all_to_all | solution.py:929
  280.6 5.5 %all-to-all-start.3 = ((bf16[4,128,1152]{2,1,0:T(8,128)(2,1)}), bf16[4,128,1152]{2,1,0:T(8,128)(2,1)}, u32[]{:S(2)}, u32[]{:S(2)}) async-start(bf16[4,128,1152]{2,1,0:T(8,128)(2,1)} %get-tuple-element.91), calls=%async_computation.3 | async-start | bytes 2359296 | tf_op jit(solution)/shard_map/all_to_all | solution.py:929
  291.1 7.7 %multiply_reduce_fusion = (f32[2304]{0:T(1024)S(1)}, f32[256,2304]{1,0:T(8,128)}, bf16[256,2304]{1,0:T(8,128)(2,1)}) fusion(f32[256,2304]{1,0:T(8,128)S(1)} %copy-done.10, f32[256,2304]{1,0:T(8,128)} %get-tuple-element.213, f32[256,2304]{1,0:T(8,128)S(1)} %copy-done.53, f32[2304]{0:T(1024)S(1)} %copy-done.36, ...), kind=kOutput, calls=%fused_computation.28 | convolution fusion | flops 1371043584 | bytes 17123328 | tf_op jit(solution)/shard_map/dot_general | solution.py:904
  300.8 9.5 %shard_map.265.own_ref = f32[16,2304]{1,0:T(8,128)} custom-call(f32[256,2304]{1,0:T(8,128)} %get-tuple-element.186.dte_ref, f32[256,2304]{1,0:T(8,128)} %get-tuple-element.177.gs_ref, f32[16,2304]{1,0:T(8,128)} %get-tuple-element.189.rate_ref, f32[4096,128]{1,0:T(8,128)} %broadcast_in_dim.111.c_ref), custom_call_target="tpu_custom_call" | custom-call | flops 75497472 | bytes 4718592 | tf_op jit(solution)/shard_map/pallas_call | solution.py:133
  310.3 9.2 %chain.3.next_ref = f32[16,2304]{1,0:T(8,128)} custom-call(f32[16,2304]{1,0:T(8,128)} %get-tuple-element.78.carry_ref, f32[16,2304]{1,0:T(8,128)} %shard_map.265.own_ref), custom_call_target="tpu_custom_call" | custom-call | tf_op jit(solution)/shard_map/chain/pallas_call | solution.py:746
  319.5 47.1 %shard_map.266 = (f32[256,2304]{1,0:T(8,128)}, f32[256,2304]{1,0:T(8,128)}, f32[16,2304]{1,0:T(8,128)}, f32[256,256]{1,0:T(8,128)}, f32[256,256]{1,0:T(8,128)}) custom-call(f32[256,2304]{1,0:T(8,128)} %get-tuple-element.185.dt_ref, f32[256,2304]{1,0:T(8,128)} %get-tuple-element.186.dte_ref, f32[256,2304]{1,0:T(8,128)} %get-tuple-element.187.dtx_ref, ...), custom_call_target="tpu_custom_call" | custom-call | flops 245366784 | bytes 14155776 | tf_op jit(solution)/shard_map/pallas_call | solution.py:203
  372.5 5.8 %convolution_convert_fusion.1 = bf16[2304,1152]{1,0:T(8,128)(2,1)} fusion(bf16[256,2304]{1,0:T(8,128)(2,1)} %get-tuple-element.212, f32[256,1152]{1,0:T(8,128)} %copy-done.4), kind=kOutput, calls=%fused_computation.1 | convolution fusion | flops 1361903616 | bytes 7667712 | tf_op jit(solution)/shard_map/dot_general | solution.py:908
  378.2 5.6 %fusion = f32[256,1152]{1,0:T(8,128)} fusion(bf16[256,2304]{1,0:T(8,128)(2,1)} %get-tuple-element.180, bf16[4608,1152]{1,0:T(8,128)(2,1)} %bitcast.92), kind=kOutput, calls=%fused_computation.3 | convolution fusion | flops 1358954496 | bytes 7667712 | tf_op jit(solution)/shard_map/dot_general | solution.py:900
  384.6 4.9 fusion.79
  390.7 4.5 multiply_reduce_fusion.1
  395.2 4.4 collective-permute-start
  406.1 4.4 all-to-all-start.4
  413.0 4.4 fusion.36
  418.2 2.9 pack_small.1
  423.0 6.2 %convolution_convert_fusion = bf16[4608,1152]{1,0:T(8,128)(2,1)} fusion(bf16[256,2304]{1,0:T(8,128)(2,1)S(1)} %copy-done.50, bf16[256,2304]{1,0:T(8,128)(2,1)S(1)} %copy-done.13, bf16[272,1152]{1,0:T(8,128)(2,1)S(1)} %copy-done.16), kind=kOutput, calls=%fused_computation | convolution fusion | flops 2727936000 | bytes 13565952 | tf_op jit(solution)/shard_map/dot_general | solution.py:908
  429.2 15.5 %all-to-all-done.4.exp_ref = bf16[4,2,96,1152]{3,2,1,0:T(8,128)(2,1)} async-done(((bf16[4,2,96,1152]{3,2,1,0:T(8,128)(2,1)}), bf16[4,2,96,1152]{3,2,1,0:T(8,128)(2,1)}, u32[]{:S(2)}, u32[]{:S(2)}) %all-to-all-start.4) | async-done | bytes 1769504 | tf_op jit(solution)/shard_map/all_to_all | solution.py:929
  446.7 69.3 %scatter_all.1 = (f32[144,1152]{1,0:T(8,128)}, f32[80,256]{1,0:T(8,128)}, bf16[4,80,1152]{2,1,0:T(8,128)(2,1)}) custom-call(bf16[4,2,4,144,1152]{4,3,2,1,0:T(8,128)(2,1)} %bitcast.59, bf16[4,2,4,80,256]{4,3,2,1,0:T(8,128)(2,1)} %bitcast.60, bf16[4,80,1152]{2,1,0:T(8,128)(2,1)} %pad.49.proj_ref), custom_call_target="tpu_custom_call" | custom-call | bytes 200000000 | tf_op jit(solution)/shard_map/scatter_all/pallas_call | solution.py:588
  516.0 5.0 finish.1
  528.2 2.9 copy.67
  (221 shorter events, 72.0 us)
Async XLA Ops:
  7.2 191.7 %all-gather.6.cloned.1.call-start = ((), (), s32[]{:S(2)}) async-start(), calls=%async_computation.7 | async-start | bytes 5474304 | tf_op jit(solution)/shard_map/all_gather | solution.py:957
  7.9 197.7 %all-gather.8.cloned.1.call-start = ((), (), s32[]{:S(2)}) async-start(), calls=%async_computation.10 | async-start | bytes 7962624 | tf_op jit(solution)/shard_map/all_gather | solution.py:972
  99.5 14.7 %copy-start.47 = (s32[16,128]{1,0:T(8,128)S(1)}, s32[16,128]{1,0:T(8,128)}, u32[]{:S(2)}) copy-start(s32[16,128]{1,0:T(8,128)} %get-tuple-element.66) | copy-start | bytes 24580
  99.6 15.2 %copy-start = (bf16[1,256,1152]{2,1,0:T(8,128)(2,1)S(1)}, bf16[1,256,1152]{2,1,0:T(8,128)(2,1)}, u32[]{:S(2)}) copy-start(bf16[1,256,1152]{2,1,0:T(8,128)(2,1)} %param.16) | copy-start | bytes 1769476
  99.6 15.2 %copy-start.17 = (bf16[16,1152]{1,0:T(8,128)(2,1)S(1)}, bf16[16,1152]{1,0:T(8,128)(2,1)}, u32[]{:S(2)}) copy-start(bf16[16,1152]{1,0:T(8,128)(2,1)} %get-tuple-element.69) | copy-start | bytes 110596
  102.5 12.0 %copy-start.35 = (f32[32,256]{1,0:T(8,128)S(1)}, f32[32,256]{1,0:T(8,128)}, u32[]{:S(2)}) copy-start(f32[32,256]{1,0:T(8,128)} %get-tuple-element.72) | copy-start | bytes 98308
  102.5 44.4 %all-to-all-start = ((bf16[4,96,1152]{2,1,0:T(8,128)(2,1)}), bf16[4,96,1152]{2,1,0:T(8,128)(2,1)}, u32[]{:S(2)}, u32[]{:S(2)}) async-start(bf16[4,96,1152]{2,1,0:T(8,128)(2,1)} %param.31), calls=%async_computation | async-start | bytes 1769472 | tf_op jit(solution)/shard_map/all_to_all | solution.py:929
  114.0 93.0 %all-gather.10.cloned.1.call-start = ((), (), s32[]{:S(2)}) async-start(), calls=%async_computation.11 | async-start | bytes 7962624 | tf_op jit(solution)/shard_map/all_gather | solution.py:1020
  117.1 5.6 %copy-start.20 = (f32[2304]{0:T(1024)}, f32[2304]{0:T(1024)S(1)}, u32[]{:S(2)}) copy-start(f32[2304]{0:T(1024)S(1)} %get-tuple-element.171) | copy-start | bytes 27652
  117.1 5.6 %copy-start.22 = (f32[2304]{0:T(1024)}, f32[2304]{0:T(1024)S(1)}, u32[]{:S(2)}) copy-start(f32[2304]{0:T(1024)S(1)} %get-tuple-element.172) | copy-start | bytes 27652
  117.1 5.6 %copy-start.24 = (f32[2304]{0:T(1024)}, f32[2304]{0:T(1024)S(1)}, u32[]{:S(2)}) copy-start(f32[2304]{0:T(1024)S(1)} %get-tuple-element.173) | copy-start | bytes 27652
  117.1 5.6 %copy-start.26 = (f32[2304]{0:T(1024)}, f32[2304]{0:T(1024)S(1)}, u32[]{:S(2)}) copy-start(f32[2304]{0:T(1024)S(1)} %get-tuple-element.174) | copy-start | bytes 27652
  117.1 5.6 %copy-start.28 = (f32[2304]{0:T(1024)}, f32[2304]{0:T(1024)S(1)}, u32[]{:S(2)}) copy-start(f32[2304]{0:T(1024)S(1)} %get-tuple-element.175) | copy-start | bytes 27652
  117.2 5.5 %copy-start.43 = (f32[256,1]{0,1:T(1,128)}, f32[256,1]{0,1:T(1,128)S(1)}, u32[]{:S(2)}) copy-start(f32[256,1]{0,1:T(1,128)S(1)} %get-tuple-element.196) | copy-start | bytes 3076
  117.3 5.5 %copy-start.45 = (f32[256,1]{0,1:T(1,128)}, f32[256,1]{0,1:T(1,128)S(1)}, u32[]{:S(2)}) copy-start(f32[256,1]{0,1:T(1,128)S(1)} %get-tuple-element.197) | copy-start | bytes 3076
  125.9 7.7 %copy-start.30 = (f32[256,104]{0,1:T(8,128)}, f32[256,104]{0,1:T(8,128)S(1)}, u32[]{:S(2)}) copy-start(f32[256,104]{0,1:T(8,128)S(1)} %fusion.49) | copy-start | bytes 319492
  137.2 9.7 %copy-start.49 = (s32[1,256,1]{1,2,0:T(1,128)S(1)}, s32[1,256,1]{1,2,0:T(1,128)}, u32[]{:S(2)}) copy-start(s32[1,256,1]{1,2,0:T(1,128)} %param.18) | copy-start | bytes 3076
  147.7 16.1 %copy-start.37 = (s32[256]{0:T(256)}, s32[256]{0:T(256)S(1)}, u32[]{:S(2)}) copy-start(s32[256]{0:T(256)S(1)} %get-tuple-element.206) | copy-start | bytes 3076
  156.6 34.3 %all-to-all-start.1 = ((bf16[4,128,1152]{2,1,0:T(8,128)(2,1)}), bf16[4,128,1152]{2,1,0:T(8,128)(2,1)}, u32[]{:S(2)}, u32[]{:S(2)}) async-start(bf16[4,128,1152]{2,1,0:T(8,128)(2,1)} %bitcast.61), calls=%async_computation.1 | async-start | bytes 2359296 | tf_op jit(solution)/shard_map/all_to_all | solution.py:929
  163.2 220.6 %reduce-scatter.3.cloned.1.call-start = ((), (), s32[]{:S(2)}) async-start(), calls=%async_computation.8 | async-start | bytes 15925248 | tf_op jit(solution)/shard_map/reduce_scatter | solution.py:1040
  170.6 20.3 %copy-start.36 = (f32[2304]{0:T(1024)S(1)}, f32[2304]{0:T(1024)}, u32[]{:S(2)}) copy-start(f32[2304]{0:T(1024)} %get-tuple-element.169) | copy-start | bytes 27652
  198.8 5.8 %copy-start.34 = (f32[1152]{0:T(1024)S(1)}, f32[1152]{0:T(1024)}, u32[]{:S(2)}) copy-start(f32[1152]{0:T(1024)} %get-tuple-element.192) | copy-start | bytes 13828
  264.3 21.8 %copy-start.48 = (s32[256]{0:T(256)S(1)}, s32[256]{0:T(256)}, u32[]{:S(2)}) copy-start(s32[256]{0:T(256)} %get-tuple-element.205) | copy-start | bytes 3076
  264.4 16.2 %all-to-all-start.2 = ((bf16[4,64,1152]{2,1,0:T(8,128)(2,1)}), bf16[4,64,1152]{2,1,0:T(8,128)(2,1)}, u32[]{:S(2)}, u32[]{:S(2)}) async-start(bf16[4,64,1152]{2,1,0:T(8,128)(2,1)} %get-tuple-element.88), calls=%async_computation.2 | async-start | bytes 1179648 | tf_op jit(solution)/shard_map/all_to_all | solution.py:929
  280.6 103.2 %all-to-all-start.3 = ((bf16[4,128,1152]{2,1,0:T(8,128)(2,1)}), bf16[4,128,1152]{2,1,0:T(8,128)(2,1)}, u32[]{:S(2)}, u32[]{:S(2)}) async-start(bf16[4,128,1152]{2,1,0:T(8,128)(2,1)} %get-tuple-element.91), calls=%async_computation.3 | async-start | bytes 2359296 | tf_op jit(solution)/shard_map/all_to_all | solution.py:929
  286.1 158.6 %reduce-scatter.5.cloned.1.call-start = ((), (), s32[]{:S(2)}) async-start(), calls=%async_computation.9 | async-start | bytes 5971968 | tf_op jit(solution)/shard_map/reduce_scatter | solution.py:1090
  289.1 9.7 %copy-start.4 = (f32[256,1152]{1,0:T(8,128)}, f32[256,1152]{1,0:T(8,128)S(1)}, u32[]{:S(2)}) copy-start(f32[256,1152]{1,0:T(8,128)S(1)} %subtract_add_fusion) | copy-start | bytes 3538948
  384.6 6.1 %copy-start.51 = (f32[256,2304]{1,0:T(8,128)S(1)}, f32[256,2304]{1,0:T(8,128)}, u32[]{:S(2)}) copy-start(f32[256,2304]{1,0:T(8,128)} %get-tuple-element.177.gs_ref) | copy-start | bytes 7077892
  395.2 16.0 %collective-permute-start = (f32[8,2304]{1,0:T(8,128)S(1)}, f32[8,2304]{1,0:T(8,128)S(1)}, u32[]{:S(2)}, u32[]{:S(2)}) collective-permute-start(f32[8,2304]{1,0:T(8,128)S(1)} %pad_add_fusion.1), channel_id=1, source_target_pairs={{1,0},{2,1},{3,2},{5,4},{6,5},{7,6},{9,8},{10,9},{11,10},{13,12},{... | collective-permute-start | bytes 221192 | tf_op jit(solution)/shard_map/ppermute | solution.py:914
  406.1 38.6 %all-to-all-start.4 = ((bf16[4,2,96,1152]{3,2,1,0:T(8,128)(2,1)}), bf16[4,2,96,1152]{3,2,1,0:T(8,128)(2,1)}, u32[]{:S(2)}, u32[]{:S(2)}) async-start(bf16[4,2,96,1152]{3,2,1,0:T(8,128)(2,1)} %reduce-scatter.3.cloned.1.call-done), calls=%async_computation.5 | async-start | bytes 3538944 | tf_op jit(solution)/shard_map/all_to_all | solution.py:929
  411.4 6.0 %copy-start.12 = (bf16[256,2304]{1,0:T(8,128)(2,1)}, bf16[256,2304]{1,0:T(8,128)(2,1)S(1)}, u32[]{:S(2)}) copy-start(bf16[256,2304]{1,0:T(8,128)(2,1)S(1)} %fusion.20) | copy-start | bytes 3538948
  521.1 10.0 %copy-start.14 = (f32[144,1152]{1,0:T(8,128)S(1)}, f32[144,1152]{1,0:T(8,128)}, u32[]{:S(2)}) copy-start(f32[144,1152]{1,0:T(8,128)} %get-tuple-element.239) | copy-start | bytes 1990660
  (33 other events, 82.7 us)
Sparse Core Ops, SparseCore 0:
  10.9 82.7 all-gather.5
  102.6 53.5 all-gather.7
  158.2 48.8 all-gather.9
  264.5 102.8 reduce-scatter.2
  384.0 59.0 reduce-scatter.4

commit v3 on v2

--- a/solution.py
+++ b/solution.py
@@ -45,26 +45,114 @@
         state_ref[:, c] = state[j]
         carry_ref[:, c] = jnp.exp2(jnp.broadcast_to(summed[:, c], (n, 128)) * rates[j])
 
-def state_pass(dte, dtx, rates2, b_wide, wide):
-    rows, chans = dte.shape
-    n = rates2.shape[0]
-    return pl.pallas_call(
-        functools.partial(state_kernel, n),
+def front_kernel(halo, ext_ref, normed_ref, wc_ref, wz_ref, xt_ref, taps_ref, bias_ref, same_ref, conv_ref, sum_ref, values_ref, z_ref, proj_ref):
+    rows, wide = sum_ref.shape
+    taps = taps_ref.shape[0]
+    conv_ref[...] = lax.dot_general(ext_ref[...], wc_ref[...], NT, preferred_element_type=F32).astype(BF).astype(F32)
+    z_ref[...] = lax.dot_general(normed_ref[...], wz_ref[...], NT, preferred_element_type=F32)
+    for j in range(wide // 128):
+        c = slice(j * 128, (j + 1) * 128)
+        total = jnp.broadcast_to(bias_ref[:, c], (rows, 128))
+        for k in range(taps):
+            lo = halo - taps + 1 + k
+            total = total + taps_ref[k : k + 1, c] * conv_ref[lo : lo + rows, c] * same_ref[k]
+        sum_ref[:, c] = total
+        values_ref[:, c] = total * jax.nn.sigmoid(total)
+
+    @pl.when(pl.program_id(0) == 0)
+    def _():
+        proj_ref[...] = jnp.zeros_like(proj_ref)
+
+    proj_ref[...] += lax.dot_general(values_ref[...].astype(BF), xt_ref[...], NT, preferred_element_type=F32)
+
+
+def front(normed_ext, normed, full_in, x_t, conv_taps, bias, same, halo, wide):
+    rows, width = normed.shape
+    chans = full_in.shape[0] // 2
+    taps = conv_taps.shape[0]
+    wide_same = jnp.broadcast_to(same.T[:, :, None], (taps, rows, 128))
+    col = lambda r: pl.BlockSpec((r, wide), lambda g: (0, g))
+    whole = lambda a: pl.BlockSpec(a.shape, lambda g: (0,) * len(a.shape))
+    steps = chans // wide
+    f32 = lambda r: jax.ShapeDtypeStruct((r, chans), F32)
+    return pl.pallas_call(
+        functools.partial(front_kernel, halo),
+        grid=(steps,),
+        in_specs=[whole(normed_ext), whole(normed), pl.BlockSpec((wide, width), lambda g: (g, 0)), pl.BlockSpec((wide, width), lambda g: (g + steps, 0)),
+                  col(128), col(taps), col(1), whole(wide_same)],
+        out_specs=[col(rows + halo), col(rows), col(rows), col(rows), pl.BlockSpec((rows, 128), lambda g: (0, 0))],
+        out_shape=[f32(rows + halo), f32(rows), f32(rows), f32(rows), jax.ShapeDtypeStruct((rows, 128), F32)],
+        compiler_params=pltpu.CompilerParams(vmem_limit_bytes=VM),
+        cost_estimate=pl.CostEstimate(flops=4*rows*chans*width, bytes_accessed=4*chans*width + 16*rows*chans, transcendentals=rows*chans),
+        name="front",
+    )(normed_ext, normed, full_in, full_in, x_t, conv_taps, bias, wide_same)
+
+
+def steps_kernel(n, rank_cols, proj_ref, keep_ref, values_ref, dtt_ref, dtb_ref, alog_ref,
+                 low_ref, bw_ref, cw_ref, bblk_ref, cblk_ref, pre_ref, dt_ref, dte_ref, dtx_ref, rate_ref, rate2_ref, state_ref, carry_ref):
+    rows, wide = pre_ref.shape
+    groups = STEP * n
+
+    @pl.when(pl.program_id(0) == 0)
+    def _():
+        proj = proj_ref[...]
+        lanes = lax.broadcasted_iota(jnp.int32, proj.shape, 1)
+        low_ref[...] = jnp.where(lanes < rank_cols, proj, 0.0).astype(BF)
+        row = lax.broadcasted_iota(jnp.int32, (rows, groups), 0)
+        col = lax.broadcasted_iota(jnp.int32, (rows, groups), 1)
+        own = lax.rem(row, STEP) == col // n
+        to_col = lax.rem(lax.broadcasted_iota(jnp.int32, (128, groups), 1), n)
+        from_col = lax.broadcasted_iota(jnp.int32, (128, groups), 0)
+        for i, (wide_ref, blk_ref) in enumerate(((bw_ref, bblk_ref), (cw_ref, cblk_ref))):
+            pick = (from_col == to_col + rank_cols + i * n).astype(F32)
+            tiled = jnp.where(own, jnp.dot(proj, pick, precision=lax.Precision.HIGHEST, preferred_element_type=F32), 0.0)
+            blk_ref[...] = tiled.astype(BF)
+            ones = jnp.ones((STEP, 128), F32)
+            for k in range(rows // STEP):
+                block = tiled[k * STEP : (k + 1) * STEP, :]
+                wide_ref[k * groups : (k + 1) * groups, :] = lax.dot_general(block, ones, TN, precision=lax.Precision.HIGHEST, preferred_element_type=F32)
+
+    pre = jnp.dot(low_ref[...], dtt_ref[...], preferred_element_type=F32) + dtb_ref[...]
+    dt = jax.nn.softplus(pre)
+    pre_ref[...] = pre
+    dt_ref[...] = dt
+    dtx_ref[...] = dt * values_ref[...]
+    for j in range(wide // 128):
+        c = slice(j * 128, (j + 1) * 128)
+        dte_ref[:, c] = jnp.where(keep_ref[...] > 0, dt[:, c], 1e30)
+    rate = -jnp.exp(alog_ref[...])
+    rate_ref[...] = rate
+    rate2_ref[...] = rate * math.log2(math.e)
+    state_kernel(n, dte_ref, dtx_ref, rate2_ref, bw_ref, state_ref, carry_ref)
+
+
+def steps(proj, keep, values, dt_t, dtb, alog_t, rank_cols, wide):
+    rows, chans = values.shape
+    n = alog_t.shape[0]
+    groups = STEP * n
+    wide_keep = jnp.broadcast_to(keep, (rows, 128))
+    col = lambda r: pl.BlockSpec((r, wide), lambda g: (0, g))
+    fixed = lambda *s: pl.BlockSpec(s, lambda g: (0, 0))
+    f32 = lambda *s: jax.ShapeDtypeStruct(s, F32)
+    bf = lambda *s: jax.ShapeDtypeStruct(s, BF)
+    return pl.pallas_call(
+        functools.partial(steps_kernel, n, rank_cols),
         grid=(chans // wide,),
-        in_specs=[pl.BlockSpec((rows, wide), lambda g: (0, g)),
-                  pl.BlockSpec((rows, wide), lambda g: (0, g)),
-                  pl.BlockSpec((n, wide), lambda g: (0, g)),
-                  pl.BlockSpec(b_wide.shape, lambda g: (0, 0))],
-        out_specs=[pl.BlockSpec((n, wide), lambda g: (0, g))] * 2,
-        out_shape=[jax.ShapeDtypeStruct((n, chans), F32)] * 2,
+        in_specs=[fixed(rows, 128), fixed(rows, 128), col(rows), col(128), col(1), col(n)],
+        out_specs=[fixed(rows, 128), fixed(rows * n, 128), fixed(rows * n, 128), fixed(rows, groups), fixed(rows, groups)] + [col(rows)] * 4 + [col(n)] * 4,
+        out_shape=[bf(rows, 128), f32(rows * n, 128), f32(rows * n, 128), bf(rows, groups), bf(rows, groups)] + [f32(rows, chans)] * 4 + [f32(n, chans)] * 4,
         compiler_params=pltpu.CompilerParams(vmem_limit_bytes=VM),
-        cost_estimate=pl.CostEstimate(flops=8*rows*chans*n, bytes_accessed=8*rows*chans, transcendentals=rows*chans*n),
-    )(dte, dtx, rates2, b_wide)
-
-def scan_kernel(n, dte_ref, dtx_ref, rate_ref, b_ref, cblk_ref, start_ref, y_ref, check_ref, hs):
+        cost_estimate=pl.CostEstimate(flops=10*rows*chans*n, bytes_accessed=24*rows*chans, transcendentals=rows*chans*n),
+        name="steps",
+    )(proj, wide_keep, values, dt_t, dtb, alog_t)
+
+
+def scan_kernel(n, dte_ref, dtx_ref, rate_ref, b_ref, cblk_ref, start_ref, values_ref, z_ref, skip_ref, out_ref, tok_ref, gain_ref,
+                y_ref, check_ref, gated_ref, first_ref, normed_ref, hs):
     rows, wide = dte_ref.shape
     tiles = wide // 128
     rates = [rate_ref[:, j*128:(j+1)*128] for j in range(tiles)]
+
     def block(k, state):
         at = pl.multiple_of(k * STEP, STEP)
         dte = dte_ref[pl.ds(at, STEP), :]
@@ -82,29 +170,44 @@
                 hs[i*n:(i+1)*n, c] = state[j].astype(BF)
         y_ref[pl.ds(at, STEP), :] = jnp.dot(cblk_ref[pl.ds(at, STEP), :], hs[...], preferred_element_type=F32)
         return tuple(state)
+
     start = tuple(start_ref[:, j*128:(j+1)*128] for j in range(tiles))
     lax.fori_loop(0, rows // STEP, block, start)
 
-def scan_pass(dte, dtx, rates2, b_wide, c_blk, start, wide):
+    @pl.when(pl.program_id(0) == 0)
+    def _():
+        first_ref[...] = tok_ref[...].astype(F32)
+
+    z = z_ref[...]
+    gated_ref[...] = ((y_ref[...] + skip_ref[...] * values_ref[...]) * (z * jax.nn.sigmoid(z))).astype(BF)
+    first_ref[...] += jnp.dot(gated_ref[...], out_ref[...], preferred_element_type=F32)
+
+    @pl.when(pl.program_id(0) == pl.num_programs(0) - 1)
+    def _():
+        first = first_ref[...]
+        scale = lax.rsqrt(jnp.mean(first * first, axis=1, keepdims=True) + EPS)
+        normed_ref[...] = (first * scale * gain_ref[...]).astype(BF)
+
+
+def scan_pass(dte, dtx, rates2, b_wide, c_blk, start, values, z, skip, full_out, tok, gain, wide):
     rows, chans = dte.shape
     n = rates2.shape[0]
+    width = tok.shape[1]
+    col = lambda r: pl.BlockSpec((r, wide), lambda g: (0, g))
+    whole = lambda a: pl.BlockSpec(a.shape, lambda g: (0, 0))
     return pl.pallas_call(
         functools.partial(scan_kernel, n),
         grid=(chans // wide,),
-        in_specs=[pl.BlockSpec((rows, wide), lambda g: (0, g)),
-                  pl.BlockSpec((rows, wide), lambda g: (0, g)),
-                  pl.BlockSpec((n, wide), lambda g: (0, g)),
-                  pl.BlockSpec(b_wide.shape, lambda g: (0, 0)),
-                  pl.BlockSpec(c_blk.shape, lambda g: (0, 0)),
-                  pl.BlockSpec((n, wide), lambda g: (0, g))],
-        out_specs=[pl.BlockSpec((rows, wide), lambda g: (0, g)),
-                   pl.BlockSpec((rows // STEP * n, wide), lambda g: (0, g))],
-        out_shape=[jax.ShapeDtypeStruct((rows, chans), F32),
-                   jax.ShapeDtypeStruct((rows // STEP * n, chans), F32)],
+        in_specs=[col(rows), col(rows), col(n), whole(b_wide), whole(c_blk), col(n), col(rows), col(rows), col(1), pl.BlockSpec((wide, width), lambda g: (g, 0)), whole(tok), whole(gain)],
+        out_specs=[col(rows), col(rows // STEP * n), col(rows), whole(tok), whole(tok)],
+        out_shape=[jax.ShapeDtypeStruct((rows, chans), F32), jax.ShapeDtypeStruct((rows // STEP * n, chans), F32), jax.ShapeDtypeStruct((rows, chans), BF),
+                   jax.ShapeDtypeStruct((rows, width), F32), jax.ShapeDtypeStruct((rows, width), BF)],
         scratch_shapes=[pltpu.VMEM((STEP * n, wide), BF)],
         compiler_params=pltpu.CompilerParams(vmem_limit_bytes=VM),
         cost_estimate=pl.CostEstimate(flops=10*rows*chans*n, bytes_accessed=12*rows*chans, transcendentals=rows*chans*n),
-    )(dte, dtx, rates2, b_wide, c_blk, start)
+        name="scan_pass",
+    )(dte, dtx, rates2, b_wide, c_blk, start, values, z, skip, full_out, tok, gain)
+
 
 def back_state_kernel(n, dte_ref, gs_ref, rate_ref, c_ref, out_ref):
     rows, wide = dte_ref.shape
@@ -143,16 +246,21 @@
         cost_estimate=pl.CostEstimate(flops=8*rows*chans*n, bytes_accessed=8*rows*chans, transcendentals=rows*chans*n),
     )(dte, gs, rates2, c_wide)
 
-def back_kernel(n, dt_ref, dte_ref, dtx_ref, gs_ref, rate_ref, rawrate_ref, b_ref, c_ref, bblk_ref, oblk_ref, check_ref, next_ref,
-                gdtx_ref, gdt_ref, glog_ref, gb_ref, gc_ref, us, decs, hs, ls, ps):
+def back_kernel(n, rank_cols, dt_ref, dte_ref, dtx_ref, gs_ref, values_ref, pre_ref, skip_ref, rate_ref, rawrate_ref, b_ref, c_ref, bblk_ref, check_ref, next_ref, low_ref, wdt_ref,
+                gval_ref, glog_ref, gwdt_ref, gdtb_ref, gskip_ref, proj_ref, us, decs, hs, ls, ps, gdtx, gdt, gb, gc, rank):
     rows, wide = dte_ref.shape
     tiles = wide // 128
     rates = [rate_ref[:, j*128:(j+1)*128] for j in range(tiles)]
+
     @pl.when(pl.program_id(0) == 0)
     def _():
-        gb_ref[...] = jnp.zeros_like(gb_ref)
-        gc_ref[...] = jnp.zeros_like(gc_ref)
+        gb[...] = jnp.zeros_like(gb)
+        gc[...] = jnp.zeros_like(gc)
+        rank[...] = jnp.zeros_like(rank)
+
+    ones = (lax.broadcasted_iota(jnp.int32, (STEP, STEP * n), 0) == lax.broadcasted_iota(jnp.int32, (STEP, STEP * n), 1) // n).astype(BF)
     glog_ref[...] = jnp.zeros_like(glog_ref)
+
     def block(k, later):
         kk = rows // STEP - 1 - k
         at = pl.multiple_of(kk * STEP, STEP)
@@ -186,40 +294,111 @@
                 ps[i*n:(i+1)*n, c] = part.astype(BF)
         for j in range(tiles):
             glog_ref[:, j*128:(j+1)*128] = logs[j]
-        gdtx_ref[pl.ds(at, STEP), :] = jnp.dot(bblk_ref[pl.ds(at, STEP), :], ls[...], preferred_element_type=F32)
-        gdt_ref[pl.ds(at, STEP), :] = jnp.dot(oblk_ref[...], ps[...], preferred_element_type=F32)
-        nt = (((1,), (1,)), ((), ()))
-        gb_ref[pl.ds(at, STEP), :] += lax.dot_general(dtx.astype(BF), ls[...], nt, preferred_element_type=F32)
-        gc_ref[pl.ds(at, STEP), :] += lax.dot_general(gs.astype(BF), hs[...], nt, preferred_element_type=F32)
+        gdtx[pl.ds(at, STEP), :] = jnp.dot(bblk_ref[pl.ds(at, STEP), :], ls[...], preferred_element_type=F32)
+        gdt[pl.ds(at, STEP), :] = jnp.dot(ones, ps[...], preferred_element_type=F32)
+        gb[pl.ds(at, STEP), :] += lax.dot_general(dtx.astype(BF), ls[...], NT, preferred_element_type=F32)
+        gc[pl.ds(at, STEP), :] += lax.dot_general(gs.astype(BF), hs[...], NT, preferred_element_type=F32)
         return tuple(later)
+
     start = tuple(next_ref[:, j*128:(j+1)*128] for j in range(tiles))
     lax.fori_loop(0, rows // STEP, block, start)
 
-def back_pass(dt, dte, dtx, gs, rates2, rates, b_wide, c_wide, b_blk, o_blk, check, nxt, wide):
+    values = values_ref[...]
+    grad_pre = (gdt[...] + gdtx[...] * values) * jax.nn.sigmoid(pre_ref[...])
+    gdtb_ref[...] = jnp.sum(grad_pre, axis=0, keepdims=True)
+    grad_pre = grad_pre.astype(BF)
+    gwdt_ref[...] = lax.dot_general(low_ref[...], grad_pre, TN, preferred_element_type=F32)
+    rank[...] += lax.dot_general(grad_pre, wdt_ref[...], NT, preferred_element_type=F32)
+    gs = gs_ref[...]
+    gskip_ref[...] = jnp.sum(gs * values, axis=0, keepdims=True)
+    gval_ref[...] = gs * skip_ref[...] + gdtx[...] * dt_ref[...]
+
+    @pl.when(pl.program_id(0) == pl.num_programs(0) - 1)
+    def _():
+        groups = STEP * n
+        row = lax.broadcasted_iota(jnp.int32, (rows, groups), 0)
+        col = lax.broadcasted_iota(jnp.int32, (rows, groups), 1)
+        own = lax.rem(row, STEP) == col // n
+        from_col = lax.rem(lax.broadcasted_iota(jnp.int32, (groups, rank.shape[1]), 0), n)
+        to_col = lax.broadcasted_iota(jnp.int32, (groups, rank.shape[1]), 1)
+        total = rank[...]
+        for i, acc in enumerate((gb, gc)):
+            place = (to_col == from_col + rank_cols + i * n).astype(BF)
+            total = total + jnp.dot(jnp.where(own, acc[...], 0.0).astype(BF), place, preferred_element_type=F32)
+        proj_ref[...] = total.astype(BF)
+
+
+def back_pass(dt, dte, dtx, gs, values, pre, skip, rates2, rates, b_wide, c_wide, b_blk, check, nxt, low, wdt, rank_cols, wide):
     rows, chans = dte.shape
     n = rates2.shape[0]
     col = lambda r: pl.BlockSpec((r, wide), lambda g: (0, g))
     whole = lambda a: pl.BlockSpec(a.shape, lambda g: (0, 0))
-    return pl.pallas_call(
-        functools.partial(back_kernel, n),
+    sq = lambda kind, w=wide: pltpu.VMEM((STEP * n, w), kind)
+    return pl.pallas_call(
+        functools.partial(back_kernel, n, rank_cols),
         grid=(chans // wide,),
-        in_specs=[col(rows)] * 4 + [col(n)] * 2 + [whole(b_wide), whole(c_wide), whole(b_blk), whole(o_blk), col(rows // STEP * n), col(n)],
-        out_specs=[col(rows), col(rows), col(n), pl.BlockSpec((rows, STEP * n), lambda g: (0, 0)), pl.BlockSpec((rows, STEP * n), lambda g: (0, 0))],
-        out_shape=[jax.ShapeDtypeStruct((rows, chans), F32)] * 2 + [jax.ShapeDtypeStruct((n, chans), F32)] + [jax.ShapeDtypeStruct((rows, STEP * n), F32)] * 2,
-        scratch_shapes=[pltpu.VMEM((STEP * n, wide), F32)] * 2 + [pltpu.VMEM((STEP * n, wide), BF)] * 3,
+        in_specs=[col(rows)] * 6 + [col(1)] + [col(n)] * 2 + [whole(b_wide), whole(c_wide), whole(b_blk), col(rows // STEP * n), col(n), whole(low), col(wdt.shape[0])],
+        out_specs=[col(rows), col(n), col(low.shape[1]), col(1), col(1), pl.BlockSpec((rows, 128), lambda g: (0, 0))],
+        out_shape=[jax.ShapeDtypeStruct((rows, chans), F32), jax.ShapeDtypeStruct((n, chans), F32), jax.ShapeDtypeStruct((low.shape[1], chans), F32),
+                   jax.ShapeDtypeStruct((1, chans), F32), jax.ShapeDtypeStruct((1, chans), F32), jax.ShapeDtypeStruct((rows, 128), BF)],
+        scratch_shapes=[sq(F32), sq(F32), sq(BF), sq(BF), sq(BF), pltpu.VMEM((rows, wide), F32), pltpu.VMEM((rows, wide), F32),
+                        pltpu.VMEM((rows, STEP * n), F32), pltpu.VMEM((rows, STEP * n), F32), pltpu.VMEM((rows, 128), F32)],
         compiler_params=pltpu.CompilerParams(vmem_limit_bytes=VM),
         cost_estimate=pl.CostEstimate(flops=26*rows*chans*n, bytes_accessed=24*rows*chans, transcendentals=rows*chans*n),
-    )(dt, dte, dtx, gs, rates2, rates, b_wide, c_wide, b_blk, o_blk, check, nxt)
-
-def block_diag(vals):
-    rows, n = vals.shape
-    same = (jnp.arange(rows)[:, None] % STEP) == (jnp.arange(STEP * n)[None, :] // n)
-    return jnp.where(same, jnp.tile(vals, (1, STEP)), 0)
-
-def block_undiag(full, n):
-    rows = full.shape[0]
-    same = (jnp.arange(rows)[:, None] % STEP) == (jnp.arange(STEP * n)[None, :] // n)
-    return jnp.sum(jnp.where(same, full, 0).reshape(rows, STEP, n), axis=1)
+        name="back_pass",
+    )(dt, dte, dtx, gs, values, pre, skip, rates2, rates, b_wide, c_wide, b_blk, check, nxt, low, wdt)
+
+
+def conv_back_kernel(halo, gval_ref, proj_ref, xt_ref, values_ref, sum_ref, ext_ref, same_ref, later_ref, taps_ref,
+                     gconv_ref, last_ref, rim_ref, gxt_ref, gtaps_ref, pad):
+    rows, wide = gval_ref.shape
+    taps = taps_ref.shape[0]
+    proj = proj_ref[...]
+    grad_values = gval_ref[...] + jnp.dot(proj, xt_ref[...], preferred_element_type=F32)
+    gxt_ref[...] = lax.dot_general(proj, values_ref[...].astype(BF), TN, preferred_element_type=F32)
+    sums = sum_ref[...]
+    sig = jax.nn.sigmoid(sums)
+    pad[0:rows, :] = grad_values * (sig * (1.0 + sums * (1.0 - sig)))
+    pad[rows:, :] = jnp.zeros((pad.shape[0] - rows, wide), F32)
+    row = lax.broadcasted_iota(jnp.int32, (8, 128), 0)
+    for j in range(wide // 128):
+        c = slice(j * 128, (j + 1) * 128)
+        grads = pad[0:rows, c]
+        sums_of = [jnp.sum(grads * same_ref[k] * ext_ref[halo - taps + 1 + k : halo - taps + 1 + k + rows, c], axis=0, keepdims=True) for k in range(taps)]
+        sums_of.append(jnp.sum(grads, axis=0, keepdims=True))
+        total = jnp.zeros((rows, 128), F32)
+        rim = jnp.zeros((8, 128), F32)
+        for k in range(taps):
+            weight = taps_ref[k : k + 1, c]
+            total = total + pad[taps - 1 - k : taps - 1 - k + rows, c] * later_ref[k] * weight
+            if k < taps - 1:
+                moved = pltpu.roll(grads[0:8] * same_ref[k, 0:8, :], 8 - taps + 1 + k, 0)
+                rim = rim + jnp.where(row >= 8 - taps + 1 + k, moved, 0.0) * weight
+        gconv_ref[:, c] = total.astype(BF)
+        last_ref[:, c] = total[rows - 8 :]
+        rim_ref[:, c] = rim
+        gtaps_ref[:, c] = jnp.concatenate(sums_of + [jnp.zeros((8 - len(sums_of), 128), F32)], axis=0)
+
+
+def conv_back(gval, proj, x_t, values, sums, ext, same, conv_taps, halo, wide):
+    rows, chans = gval.shape
+    taps = conv_taps.shape[0]
+    later = jnp.stack([jnp.pad(same[taps - 1 - k :, k], (0, taps - 1 - k)) for k in range(taps)])
+    cover = lambda a: jnp.broadcast_to(a[:, :, None], (taps, rows, 128))
+    col = lambda r: pl.BlockSpec((r, wide), lambda g: (0, g))
+    mask = pl.BlockSpec((taps, rows, 128), lambda g: (0, 0, 0))
+    f32 = lambda r: jax.ShapeDtypeStruct((r, chans), F32)
+    return pl.pallas_call(
+        functools.partial(conv_back_kernel, halo),
+        grid=(chans // wide,),
+        in_specs=[col(rows), pl.BlockSpec(proj.shape, lambda g: (0, 0)), col(x_t.shape[0]), col(rows), col(rows), col(ext.shape[0]), mask, mask, col(taps)],
+        out_specs=[col(rows), col(8), col(8), col(x_t.shape[0]), col(8)],
+        out_shape=[jax.ShapeDtypeStruct((rows, chans), BF), f32(8), f32(8), f32(x_t.shape[0]), f32(8)],
+        scratch_shapes=[pltpu.VMEM((rows + 8, wide), F32)],
+        compiler_params=pltpu.CompilerParams(vmem_limit_bytes=VM),
+        cost_estimate=pl.CostEstimate(flops=60*rows*chans, bytes_accessed=20*rows*chans, transcendentals=rows*chans),
+        name="conv_back",
+    )(gval, proj, x_t, values, sums, ext, cover(same.T), cover(later), conv_taps)
 
 
 def flip(value, bit):
@@ -599,38 +778,40 @@
     )(g_in, g_rest, proj)
 
 
-def unpack_kernel(own, width_b, pack_ref, low_ref, high_ref, small_ref, tall):
-    blocks = pack_ref.shape[0]
-    for b in range(blocks):
+def unpack_kernel(own, x_cols, dt_cols, pack_ref, xt_ref, dtt_ref, high_ref, small_ref, tall):
+    for b in range(pack_ref.shape[0]):
         block = pack_ref[b].astype(F32)
         tall[b * own : (b + 1) * own, :] = block[:own]
         small_ref[b : b + 1, :] = block[own : own + 1]
     for j in range(tall.shape[0] // 128):
-        turned = tall[j * 128 : (j + 1) * 128, :].T
-        low_ref[:, j * 128 : (j + 1) * 128] = turned[:width_b].astype(BF)
-        high_ref[:, j * 128 : (j + 1) * 128] = turned[width_b:]
-
-
-def unpack(pack, own, width_b):
+        c = slice(j * 128, (j + 1) * 128)
+        turned = tall[c, :].T
+        for ref, lo, size in ((xt_ref, 0, x_cols), (dtt_ref, x_cols, dt_cols)):
+            ref[:, c] = jnp.concatenate([turned[lo : lo + size], jnp.zeros((ref.shape[0] - size, 128), F32)], axis=0).astype(BF)
+        high_ref[:, c] = turned[x_cols + dt_cols :]
+
+
+def unpack(pack, own, x_cols, dt_cols):
     blocks, _, cols = pack.shape
     chans = blocks * own
     if own % 8:
         turned = pack[:, :own].reshape(chans, cols).T
-        return turned[:width_b], turned[width_b:].astype(F32), pack[:, own].astype(F32)
-    return pl.pallas_call(
-        functools.partial(unpack_kernel, own, width_b),
-        out_shape=[jax.ShapeDtypeStruct((width_b, chans), BF), jax.ShapeDtypeStruct((cols - width_b, chans), F32), jax.ShapeDtypeStruct((blocks, cols), F32)],
+        grown = lambda a: jnp.pad(a, ((0, 128 - a.shape[0]), (0, 0)))
+        return grown(turned[:x_cols]), grown(turned[x_cols : x_cols + dt_cols]), turned[x_cols + dt_cols :].astype(F32), pack[:, own].astype(F32)
+    return pl.pallas_call(
+        functools.partial(unpack_kernel, own, x_cols, dt_cols),
+        out_shape=[jax.ShapeDtypeStruct((128, chans), BF)] * 2 + [jax.ShapeDtypeStruct((cols - x_cols - dt_cols, chans), F32), jax.ShapeDtypeStruct((blocks, cols), F32)],
         scratch_shapes=[pltpu.VMEM((chans, cols), F32)],
         compiler_params=pltpu.CompilerParams(vmem_limit_bytes=VM),
         name="unpack_small",
     )(pack)
 
 
-def pack_kernel(own, x_ref, dt_ref, log_ref, misc_ref, small_ref, out_ref, wide, tall):
+def pack_kernel(own, sizes, x_ref, dt_ref, log_ref, taps_ref, dtb_ref, skip_ref, small_ref, out_ref, wide, tall):
     at = 0
-    for ref in (x_ref, dt_ref, log_ref, misc_ref):
-        wide[at : at + ref.shape[0], :] = ref[...]
-        at += ref.shape[0]
+    for ref, size in zip((x_ref, dt_ref, log_ref, taps_ref, dtb_ref, skip_ref), sizes):
+        wide[at : at + size, :] = ref[0:size, :]
+        at += size
     wide[at:, :] = jnp.zeros((wide.shape[0] - at, wide.shape[1]), F32)
     for j in range(tall.shape[0] // 128):
         tall[j * 128 : (j + 1) * 128, :] = wide[:, j * 128 : (j + 1) * 128].T
@@ -641,58 +822,85 @@
         out_ref[b] = jnp.concatenate([tall[b * own : (b + 1) * own, :], tail], axis=0).astype(BF)
 
 
-def pack_grads(x_t, dt_t, log_t, misc, small, own):
+def pack_grads(parts, sizes, small, own):
     blocks, cols = small.shape
-    chans = x_t.shape[1]
+    chans = parts[0].shape[1]
     rows = own + -own % 16
     if own % 8:
-        turned = jnp.concatenate([x_t, dt_t, log_t, misc]).T.reshape(blocks, own, -1)
+        turned = jnp.concatenate([part[:size] for part, size in zip(parts, sizes)]).T.reshape(blocks, own, -1)
         turned = jnp.pad(turned, ((0, 0), (0, 0), (0, cols - turned.shape[2])))
         return jnp.concatenate([turned, small[:, None], jnp.zeros((blocks, rows - own - 1, cols), F32)], axis=1).astype(BF)
     return pl.pallas_call(
-        functools.partial(pack_kernel, own),
+        functools.partial(pack_kernel, own, sizes),
         out_shape=jax.ShapeDtypeStruct((blocks, rows, cols), BF),
         scratch_shapes=[pltpu.VMEM((cols, chans), F32), pltpu.VMEM((chans, cols), F32)],
         compiler_params=pltpu.CompilerParams(vmem_limit_bytes=VM),
         name="pack_small",
-    )(x_t, dt_t, log_t, misc, small)
-
-
-def finish_kernel(own, cuts, pack_ref, exp_ref, proj_ref, up_out, down_out, row_out, proj_out, *col_outs):
-    piece, width = exp_ref.shape[2:]
-    filler = -piece % 128
-
-    down_out[0] = exp_ref[0, 1].astype(F32)
-    tall = exp_ref[0, 0].astype(F32)
-    if filler:
-        tall = jnp.concatenate([tall, jnp.zeros((filler, width), F32)], axis=0)
-    for j in range(width // 128):
-        up_out[0, j * 128 : (j + 1) * 128, :] = tall[:, j * 128 : (j + 1) * 128].T[:, :piece]
+    )(*parts, small)
+
+
+def finish_kernel(own, cuts, pack_ref, up_ref, down_ref, proj_ref, up_out, down_out, row_out, proj_out, *small_outs):
+    up_out[0] = up_ref[0].astype(F32)
+    down_out[0] = down_ref[0].astype(F32)
 
     @pl.when(pl.program_id(0) == 0)
     def _():
         row_out[...] = pack_ref[own : own + 1, :]
         proj_out[...] = sum(proj_ref[k].astype(F32) for k in range(proj_ref.shape[0]))[:own]
-        for (lo, size), out in zip(cuts, col_outs):
-            out[...] = pack_ref[0:own, lo : lo + size]
-
-
-def finish(pack, both, proj, own, cuts):
-    experts, _, piece, width = both.shape
+        tall = pack_ref[...]
+        turned = jnp.concatenate([tall, jnp.zeros((-tall.shape[0] % 128, tall.shape[1]), F32)], axis=0).T
+        for (lo, size, turn), out in zip(cuts, small_outs):
+            out[...] = turned[lo : lo + size, :own] if turn else pack_ref[0:own, lo : lo + size]
+
+
+def finish(pack, up, down, proj, own, cuts):
+    experts, piece, width = up.shape
     if own % 8:
-        return [jnp.swapaxes(both[:, 0].astype(F32), 1, 2), both[:, 1].astype(F32), pack[own : own + 1], jnp.sum(proj[:, :own].astype(F32), axis=0)] + [pack[:own, lo : lo + size] for lo, size in cuts]
+        small = [pack[:own, lo : lo + size].T if turn else pack[:own, lo : lo + size] for lo, size, turn in cuts]
+        return [up.astype(F32), down.astype(F32), pack[own : own + 1], jnp.sum(proj[:, :own].astype(F32), axis=0)] + small
     whole = lambda shape: pl.BlockSpec(shape, lambda e: (0,) * len(shape))
     part = lambda shape: pl.BlockSpec((1,) + shape[1:], lambda e: (e, 0, 0))
-    shapes = [(experts, width, piece), (experts, piece, width), (1, pack.shape[1]), (own, width)] + [(own, size) for _, size in cuts]
+    shapes = [(experts, piece, width)] * 2 + [(1, pack.shape[1]), (own, width)] + [(size, own) if turn else (own, size) for _, size, turn in cuts]
     return pl.pallas_call(
         functools.partial(finish_kernel, own, cuts),
         grid=(experts,),
-        in_specs=[whole(pack.shape), pl.BlockSpec((1,) + both.shape[1:], lambda e: (e, 0, 0, 0)), whole(proj.shape)],
+        in_specs=[whole(pack.shape), part(up.shape), part(up.shape), whole(proj.shape)],
         out_specs=[part(shapes[0]), part(shapes[1])] + [whole(s) for s in shapes[2:]],
         out_shape=[jax.ShapeDtypeStruct(s, F32) for s in shapes],
         compiler_params=pltpu.CompilerParams(vmem_limit_bytes=VM),
         name="finish",
-    )(pack, both, proj)
+    )(pack, up, down, proj)
+
+
+def pack_params_kernel(x_ref, dt_ref, log_ref, taps_ref, bias_ref, dtb_ref, skip_ref, small_ref, out_ref, thin, tall):
+    own, x_cols = x_ref.shape
+    thin[...] = jnp.zeros_like(thin)
+    at = 0
+    for ref in (log_ref, taps_ref, bias_ref, dtb_ref, skip_ref):
+        thin[at : at + ref.shape[0], 0:own] = ref[...].astype(F32)
+        at += ref.shape[0]
+    tall[...] = jnp.zeros_like(tall)
+    at = x_cols + dt_ref.shape[1]
+    tall[0:own, 0:x_cols] = x_ref[...].astype(F32)
+    tall[0:own, x_cols:at] = dt_ref[...].astype(F32)
+    tall[0:own, at : at + thin.shape[0]] = thin[...].T[:own]
+    tall[own : own + 1, 0 : small_ref.shape[1]] = small_ref[...].astype(F32)
+    out_ref[...] = tall[...].astype(BF)
+
+
+def pack_params(w_x, w_dt, log_t, taps_t, bias, dtb, skip, small):
+    own = w_x.shape[0]
+    rows = own + -own % 16
+    if own % 8:
+        wide = jnp.concatenate([w_x, w_dt, log_t.T, taps_t.T, bias.T, dtb.T, skip.T], axis=1)
+        wide = jnp.pad(wide, ((0, -own % 16), (0, 256 - wide.shape[1])))
+        return wide + jnp.pad(small, ((own, -own % 16 - 1), (0, 256 - small.shape[1])))
+    return pl.pallas_call(
+        pack_params_kernel,
+        out_shape=jax.ShapeDtypeStruct((rows, 256), BF),
+        scratch_shapes=[pltpu.VMEM((32, 128), F32), pltpu.VMEM((rows, 256), F32)],
+        name="pack_params",
+    )(w_x, w_dt, log_t, taps_t, bias, dtb, skip, small)
 
 
 def chain_kernel(step, pieces, carry_ref, own_ref, out_ref, inbox, outbox, send, recv):
@@ -947,11 +1155,8 @@
     tok_b = tokens[0]
     seg_plus = segment_ids[0] + 1
 
-    columns = (w_x, w_dt, a_log, conv_w, conv_b[:, None], dt_bias[:, None], d_skip[:, None])
-    packed = jnp.concatenate(columns, axis=1)
     share = small_params.shape[0]
-    packed = jnp.pad(packed, ((0, -own % 16), (0, 256 - packed.shape[1])))
-    packed = packed + jnp.pad(small_params[None], ((own, -own % 16 - 1), (0, 256 - share)))
+    packed = pack_params(w_x, w_dt, a_log.T, conv_w.T, conv_b[None], dt_bias[None], d_skip[None], small_params[None])
     direct = lax.axis_size("dp") == 8 and lax.axis_size("seq") == 4
     up_t = jnp.swapaxes(w_up, 1, 2)
     full_out = lax.all_gather(w_out, both, axis=0, tiled=True)
@@ -967,11 +1172,9 @@
         rim_tok = shift(tok_b[rows - halo :], "seq", 1)
         rim_ids = shift(seg_plus[rows - halo :], "seq", 1)
     full_in = lax.optimization_barrier(all_in.reshape(2 * chans, width))
-    low_t, high_t, small = unpack(all_pack.reshape(devices, -1, 256), own, rank + w_x.shape[1])
+    full_x_t, full_dt_t, high_t, small = unpack(all_pack.reshape(devices, -1, 256), own, w_x.shape[1], rank)
     small, part_up = lax.optimization_barrier((small, part_up))
     full_up = lax.all_gather(part_up, "dp", axis=0).reshape(-1, width)
-    xcols = w_x.shape[1]
-    full_x_t, full_dt_t = low_t[:xcols], low_t[xcols:]
     alog_t, conv_f, bias_row, dtb_row, skip = high_t[:n], high_t[n : n + taps], high_t[n + taps : n + taps + 1], high_t[n + taps + 1 : n + taps + 2], high_t[n + taps + 2 : n + taps + 3]
     flat_small = small[:, :share].reshape(-1)
     gain_one = flat_small[:width]
@@ -995,38 +1198,18 @@
     keep = same[:, taps - 2 : taps - 1]
     normed_ext = (tok_ext * rms_scale(tok_ext) * gain_one).astype(BF)
     normed = normed_ext[halo:]
-    conv_in = dot_nt(normed_ext, full_in[:chans]).astype(BF).astype(F32)
-    z = dot_nt(normed, full_in[chans:])
-    conv_sum = bias_row
-    for k in range(taps):
-        lo = halo - taps + 1 + k
-        conv_sum = conv_sum + conv_f[k : k + 1] * conv_in[lo : lo + rows] * same[:, k : k + 1]
-    values = conv_sum * jax.nn.sigmoid(conv_sum)
-    values_b = values.astype(BF)
-    projected = dot_nt(values_b, full_x_t)
-    low_rank = projected[:, :rank].astype(BF)
-    b_rows = projected[:, rank : rank + n]
-    c_rows = projected[:, rank + n :]
-    pre_dt = dot(low_rank, full_dt_t) + dtb_row
-    dt = jax.nn.softplus(pre_dt)
-    dt_keep = jnp.where(keep > 0, dt, 1e30)
-    dtx = dt * values
-    rates = -jnp.exp(alog_t)
-    rates2 = rates * math.log2(math.e)
-    b_wide = jnp.broadcast_to(b_rows[:, :, None], (rows, n, 128)).reshape(rows * n, 128)
-    c_wide = jnp.broadcast_to(c_rows[:, :, None], (rows, n, 128)).reshape(rows * n, 128)
-    own_state, carry = state_pass(dt_keep, dtx, rates2, b_wide, wide)
+    conv_in, conv_sum, values, z, projected = front(normed_ext, normed, full_in, full_x_t, conv_f, bias_row, same, halo, wide)
+    low_wide, b_wide, c_wide, b_blk, c_blk, pre_dt, dt, dt_keep, dtx, rates, rates2, own_state, carry = steps(projected, keep, values, full_dt_t, dtb_row, alog_t, rank, wide)
     carry, part_down = lax.optimization_barrier((carry, part_down))
     full_down = lax.all_gather(part_down, "dp", axis=0).reshape(-1, width)
     start = chain(carry, own_state, 1, 3)
     go_local, start = lax.optimization_barrier((dot_tn(gather_mat, grad_out_b).astype(BF), start))
     go_slots = swap(go_local.reshape(experts, slots, width))
-    scanned, checks = scan_pass(dt_keep, dtx, rates2, b_wide, block_diag(c_rows).astype(BF), start, wide)
-    scanned, go_slots = lax.optimization_barrier((scanned, go_slots))
+    scanned, checks, gated, first_sum, normed_two = scan_pass(
+        dt_keep, dtx, rates2, b_wide, c_blk, start, values, z, skip, full_out, tok_b, gain_two[None], wide
+    )
+    normed_two, go_slots = lax.optimization_barrier((normed_two, go_slots))
     sig_z = jax.nn.sigmoid(z)
-    gated = ((scanned + skip * values) * (z * sig_z)).astype(BF)
-    first_sum = tok_f + dot(gated, full_out)
-    normed_two = (first_sum * rms_scale(first_sum) * gain_two).astype(BF)
 
     piece = w_up.shape[2]
     router_wide = jnp.pad(router, ((0, 0), (0, 128 - experts)))
@@ -1037,56 +1220,38 @@
     mixed_slots = swap(mixed_back).reshape(-1, width)
     if piece % 16:
         grad_exp = jnp.swapaxes(jnp.swapaxes(grad_exp, 0, 1).reshape(2, -1, piece, width), 0, 1)
-    part_exp = lax.psum_scatter(grad_exp, "dp", scatter_dimension=0, tiled=True)
+    part_exp = lax.psum_scatter(grad_exp.reshape(-1, width), "dp", scatter_dimension=0, tiled=True)
 
     grad_norm_two, grad_gain_two = rms_back(first_sum, gain_two, grad_n2)
     grad_first = grad_out + grad_norm_two
     grad_mixer = grad_first.astype(BF)
-    grad_w_out = dot_tn(gated, grad_mixer)
+    grad_w_out = dot_tn(gated, grad_mixer).astype(BF)
     grad_gated = dot_nt(grad_mixer, full_out)
     silu_z = z * sig_z
     grad_scanned = grad_gated * silu_z
     grad_z = grad_gated * (scanned + skip * values) * (sig_z * (1.0 + z * (1.0 - sig_z)))
     grad_z_b = grad_z.astype(BF)
-    grad_skip = jnp.sum(grad_scanned * values, axis=0)
     grad_start = back_state_pass(dt_keep, grad_scanned, rates2, c_wide, wide)
     nxt = chain(carry, grad_start, -1, 4)
-    ones_blk = block_diag(jnp.ones((STEP, n), F32)).astype(BF)
-    g_dtx, g_dt, g_log, gb_full, gc_full = back_pass(
-        dt, dt_keep, dtx, grad_scanned, rates2, rates, b_wide, c_wide, block_diag(b_rows).astype(BF), ones_blk, checks, nxt, wide
+    nxt, grad_w_out = lax.optimization_barrier((nxt, grad_w_out))
+    grad_vals, g_log, grad_dt_t, grad_dtb, grad_skip, grad_proj = back_pass(
+        dt, dt_keep, dtx, grad_scanned, values, pre_dt, skip, rates2, rates, b_wide, c_wide, b_blk, checks, nxt, low_wide, full_dt_t, rank, wide
     )
-    g_dtx, mixed_slots, part_exp, grad_w_out = lax.optimization_barrier((g_dtx, mixed_slots, part_exp, grad_w_out.astype(BF)))
-    sum_exp = swap(part_exp)
+    grad_vals, mixed_slots, part_exp, grad_w_out = lax.optimization_barrier((grad_vals, mixed_slots, part_exp, grad_w_out))
+    sum_exp = swap(part_exp.reshape(experts, 2, piece, width))
     mixed_out = (first_sum + dot(gather_mat, mixed_slots)).astype(BF)
-    grad_dt = g_dt + g_dtx * values
-    grad_pre_f = grad_dt * jax.nn.sigmoid(pre_dt)
-    grad_dtb = jnp.sum(grad_pre_f, axis=0)
-    grad_pre = grad_pre_f.astype(BF)
-    grad_dt_t = dot_tn(low_rank, grad_pre)
-    grad_proj = jnp.concatenate([dot_nt(grad_pre, full_dt_t), block_undiag(gb_full, n), block_undiag(gc_full, n)], axis=1).astype(BF)
-    grad_x_t = dot_tn(grad_proj, values_b)
-    grad_values = grad_scanned * skip + g_dtx * dt + dot(grad_proj, full_x_t)
-    sig_c = jax.nn.sigmoid(conv_sum)
-    grad_conv_sum = grad_values * (sig_c * (1.0 + conv_sum * (1.0 - sig_c)))
-    grad_bias = jnp.sum(grad_conv_sum, axis=0)
-    grad_taps = []
-    grad_ext = None
-    for k in range(taps):
-        lo = halo - taps + 1 + k
-        masked = grad_conv_sum * same[:, k : k + 1]
-        grad_taps.append(jnp.sum(masked * conv_in[lo : lo + rows], axis=0))
-        term = jnp.pad(masked * conv_f[k : k + 1], ((lo, halo - lo), (0, 0)))
-        grad_ext = term if grad_ext is None else grad_ext + term
-    rim_back = shift(grad_ext[halo - 8 : halo], "seq", -1)
-    grad_conv_in = (grad_ext[halo:] + jnp.pad(rim_back, ((rows - 8, 0), (0, 0)))).astype(BF)
+    grad_conv_b, grad_last, grad_rim, grad_x_t, grad_taps = conv_back(grad_vals, grad_proj, full_x_t, values, conv_sum, conv_in, same, conv_f, halo, wide)
+    grad_last = (grad_last + shift(grad_rim, "seq", -1)).astype(BF)
+    grad_conv_in = jnp.concatenate([grad_conv_b[: rows - 8], grad_last])
     grad_w_in = dot_tn(jnp.concatenate([grad_conv_in, grad_z_b], axis=1), normed).astype(BF)
     grad_normed = dot(grad_conv_in, full_in[:chans]) + dot(grad_z_b, full_in[chans:])
     grad_norm_one, grad_gain_one = rms_back(tok_f, gain_one, grad_normed)
     tokens_grad = (grad_first + grad_norm_one).astype(BF)
 
     grad_small = jnp.concatenate([grad_gain_one, grad_gain_two, grad_router.reshape(-1)])
-    misc = jnp.stack(grad_taps + [grad_bias, grad_dtb, grad_skip, jnp.zeros_like(grad_bias)])
-    grad_packed = pack_grads(grad_x_t, grad_dt_t, g_log, misc, jnp.pad(grad_small.reshape(devices, -1), ((0, 0), (0, 256 - share))), own)
+    grad_packed = pack_grads(
+        (grad_x_t, grad_dt_t, g_log, grad_taps, grad_dtb, grad_skip), (w_x.shape[1], rank, n, taps + 1, 1, 1), jnp.pad(grad_small.reshape(devices, -1), ((0, 0), (0, 256 - share))), own
+    )
     part_out = lax.psum_scatter(grad_w_out, "dp", scatter_dimension=0, tiled=True).reshape(-1, own, width)
     part_out = jnp.pad(part_out, ((0, 0), (0, -own % 16), (0, 0)))
     if direct:
@@ -1099,24 +1264,24 @@
         sum_pack = lax.psum_scatter(grad_packed, both, scatter_dimension=0, tiled=True)[0].astype(F32)
         all_out = swap(part_out)
     cuts, at = [], 0
-    for column in columns:
-        cuts.append((at, column.shape[1]))
-        at += column.shape[1]
-    up_out, down_out, s_row, sum_out, s_x, s_dt, s_log, s_conv, s_bias, s_dtb, s_skip = finish(sum_pack, sum_exp, all_out, own, tuple(cuts))
+    for size, turn in ((w_x.shape[1], False), (rank, False), (n, True), (taps, True), (1, True), (1, True), (1, True)):
+        cuts.append((at, size, turn))
+        at += size
+    up_out, down_out, s_row, sum_out, s_x, s_dt, s_log, s_conv, s_bias, s_dtb, s_skip = finish(sum_pack, sum_exp[:, 0], sum_exp[:, 1], all_out, own, tuple(cuts))
     return (
         mixed_out[None],
         tokens_grad[None],
         s_row[0, :share],
         sum_in,
-        s_conv,
-        s_bias[:, 0],
+        s_conv.T,
+        s_bias[0],
         s_x,
         s_dt,
-        s_dtb[:, 0],
-        s_log,
-        s_skip[:, 0],
+        s_dtb[0],
+        s_log.T,
+        s_skip[0],
         sum_out,
-        up_out,
+        jnp.swapaxes(up_out, 1, 2),
         down_out,
     )
 

time: 546 us -> 524 us (0.960)
  Pallas kernels: 323 us -> 364 us
  matrix products: 71.4 us -> 34 us
  other arithmetic: 25.6 us -> 5.62 us
  local copies, waits for them, and re-layouts: 39.3 us -> 26 us
  waiting for transfers between devices: 27.3 us -> 38.9 us
    pallas_call x4 -> x7, Pallas kernels: 62.6 us -> 99.3 us  [the longest x1 51.2 us: back_pass(): pl.pallas_call(functools.partial(back_kernel, n, rank_cols), grid=(chans...]
    dot_general x8 -> x5, matrix products: 32.2 us -> 15.1 us  [dot(): return jnp.dot(a, b, preferred_element_type=F32)]
    dot_general x5 -> x1, matrix products: 21.5 us -> 6.27 us  [dot_nt(): return lax.dot_general(a, b, NT, preferred_element_type=F32)]
    all_gather x1, waiting for transfers between devices: 1.42 us -> 11.8 us  [shards(): full_down = lax.all_gather(part_down, 'dp', axis=0).reshape(-1, width)]
    unnamed x114 -> x59, local copies, waits for them, and re-layouts: 15.7 us -> 6.36 us
    reduce_sum x3 -> x0, other arithmetic: 5.91 us -> none  [the longest x1 4.91 us: shards(): grad_dtb = jnp.sum(grad_pre_f, axis=0)]
    dot_general x5 -> x3, matrix products: 17.7 us -> 12.6 us  [dot_tn(): return lax.dot_general(a, b, TN, preferred_element_type=F32)]
  transfers between devices with their start and end apart: 11 -> 11, of which waited for: 3 -> 3; matrix products, arithmetic and copies ran while one was open for 22% -> 11% of each run, Pallas kernels for 36% -> 45%
where the time goes in v3:
time: 524 us; the launch traced here: 518 us
  Pallas kernels  364 us (69%)
  waiting for transfers between devices  38.9 us (7%)
  starting transfers between devices  34.3 us (7%)
  matrix products  34 us (6%)
  local copies, waits for them, and re-layouts  26 us (5%)
  between operations  14.6 us (3%)
  other arithmetic  5.62 us (1%)
    pallas_call x1, Pallas kernels, gather_all(): pl.pallas_call(functools.partial(gather_kernel, parts, count), in_specs=[...  84.4 us
    pallas_call x1, Pallas kernels, scatter_all(): pl.pallas_call(functools.partial(scatter_kernel, parts, count), in_specs=...  67.8 us
    pallas_call x1, Pallas kernels, experts_pass(): pl.pallas_call(functools.partial(experts_kernel, block, piece), in_specs=...  57.4 us
    pallas_call x1, Pallas kernels, back_pass(): pl.pallas_call(functools.partial(back_kernel, n, rank_cols), grid=(chans...  51.2 us
    all_to_all x5, starting transfers between devices, swap(): return lax.all_to_all(value, 'seq', 0, 0)  29.2 us
    all_to_all x5, waiting for transfers between devices, swap(): return lax.all_to_all(value, 'seq', 0, 0)  26.3 us
    pallas_call x1, Pallas kernels, scan_pass(): pl.pallas_call(functools.partial(scan_kernel, n), grid=(chans // wide,),...  24.7 us
    pallas_call x1, Pallas kernels, steps(): pl.pallas_call(functools.partial(steps_kernel, n, rank_cols), grid=(chans...  18.4 us
  transfers between devices with their start and end apart: 11, of which 3 were waited for; matrix products, arithmetic and copies ran while one was open for 11% of the time, Pallas kernels for 45%

profile of v3, /device:TPU:9, one launch (start us, length us, event | category | flops | bytes accessed | tf_op | source)
XLA Modules:
  0.0 517.8 jit_solution(8722555942400428191)
XLA Ops:
  12.2 84.4 %gather_all.1 = (bf16[4,2,4,144,1152]{4,3,2,1,0:T(8,128)(2,1)}, bf16[4,2,4,80,256]{4,3,2,1,0:T(8,128)(2,1)}, bf16[4,96,1152]{2,1,0:T(8,128)(2,1)}, bf16[16,1152]{1,0:T(8,128)(2,1)}, s32[16,128]{1,0:T(8,128)}) custom-call(bf16[144,1152]{1,0:T(8,128)(2,1)} %in_ref.1, bf16[80,256]{1,0:T(8,128)(2,1)} %pack_params.1.rest_ref, bf16[4,96,1152]{2,1,0:T(8,128)(2,1)} %bitcast.79, ...), custom_call_target="tpu_custom_call" | custom-call | bytes 200000000 | tf_op jit(solution)/shard_map/gather_all/pallas_call | solution.py:615
  96.6 3.0 unpack_small.1
  99.6 8.1 %all-to-all-start = ((bf16[4,96,1152]{2,1,0:T(8,128)(2,1)}), bf16[4,96,1152]{2,1,0:T(8,128)(2,1)S(1)}, u32[]{:S(2)}, u32[]{:S(2)}) async-start(bf16[4,96,1152]{2,1,0:T(8,128)(2,1)} %param.31), calls=%async_computation | async-start | bytes 1769472 | tf_op jit(solution)/shard_map/all_to_all | solution.py:1137
  116.7 12.0 %front.1 = (f32[272,2304]{1,0:T(8,128)}, f32[256,2304]{1,0:T(8,128)}, f32[256,2304]{1,0:T(8,128)}, f32[256,2304]{1,0:T(8,128)}, f32[256,128]{1,0:T(8,128)}) custom-call(bf16[272,1152]{1,0:T(8,128)(2,1)} %copy-done.4, bf16[256,1152]{1,0:T(8,128)(2,1)} %slice.119.normed_ref, bf16[4608,1152]{1,0:T(8,128)(2,1)} %bitcast.66, bf16[4608,1152]{1,0:T(8,128)(2,1)} %bitcast.67, ...), custom_call_target="tpu_custom_call" | custom-call | flops 2717908992 | bytes 20054016 | tf_op jit(solution)/shard_map/front/pallas_call | solution.py:78
  129.4 18.4 %steps.1 = (bf16[256,128]{1,0:T(8,128)(2,1)}, f32[4096,128]{1,0:T(8,128)}, f32[4096,128]{1,0:T(8,128)}, bf16[256,256]{1,0:T(8,128)(2,1)}, bf16[256,256]{1,0:T(8,...) custom-call(f32[256,128]{1,0:T(8,128)} %get-tuple-element.104.proj_r, ...), custom_call_target="tpu_custom_call" | custom-call | flops 94371840 | bytes 14155776 | tf_op jit(solution)/shard_map/steps/pallas_call | solution.py:138
  149.3 1.7 convolution_convert_fusion.2
  151.0 5.9 %chain.2.start_ref = f32[16,2304]{1,0:T(8,128)} custom-call(f32[16,2304]{1,0:T(8,128)} %get-tuple-element.114.carry_ref, f32[16,2304]{1,0:T(8,128)} %get-tuple-element.115.own_ref), custom_call_target="tpu_custom_call" | custom-call | tf_op jit(solution)/shard_map/chain/pallas_call | solution.py:954
  156.9 6.6 %all-to-all-start.1 = ((bf16[4,128,1152]{2,1,0:T(8,128)(2,1)}), bf16[4,128,1152]{2,1,0:T(8,128)(2,1)S(1)}, u32[]{:S(2)}, u32[]{:S(2)}) async-start(bf16[4,128,1152]{2,1,0:T(8,128)(2,1)} %bitcast.15), calls=%async_computation.1 | async-start | bytes 2359296 | tf_op jit(solution)/shard_map/all_to_all | solution.py:1137
  166.2 24.7 %scan_pass.1 = (f32[256,2304]{1,0:T(8,128)}, f32[256,2304]{1,0:T(8,128)}, bf16[256,2304]{1,0:T(8,128)(2,1)}, f32[256,1152]{1,0:T(8,128)}, bf16[256,1152]{1,0:T(8,128)(2,1)}) custom-call(f32[256,2304]{1,0:T(8,128)} %get-tuple-element.107.dte_ref, f32[256,2304]{1,0:T(8,128)} %get-tuple-element.108.dtx_ref, f32[16,2304]{1,0:T(8,128)} %get-tuple-element.109.rate_ref, ...), custom_call_target="tpu_custom_call" | custom-call | flops 94371840 | bytes 7077888 | tf_op jit(solution)/shard_map/scan_pass/pallas_call | solution.py:198
  190.9 11.8 %all-gather.10.cloned.1.call-done = bf16[32,96,1152]{2,1,0:T(8,128)(2,1)} async-done(((bf16[4,96,1152]{2,1,0:T(8,128)(2,1)}), bf16[32,96,1152]{2,1,0:T(8,128)(2,1)}) %all-gather.10.cloned.1.call-update) | async-done | bytes 7077904 | tf_op jit(solution)/shard_map/all_gather | solution.py:1204
  202.7 57.4 %experts.1 = (bf16[4,64,1152]{2,1,0:T(8,128)(2,1)}, bf16[4,64,1152]{2,1,0:T(8,128)(2,1)}, bf16[4,128,1152]{2,1,0:T(8,128)(2,1)}, f32[1152,128]{1,0:T(8,128)}, bf16[32,2,96,1152]{3,2,1,0:T(8,128)(2,1)}) custom-call(bf16[256,512]{1,0:T(8,128)(2,1)} %fusion.35.pick_ref, bf16[256,1152]{1,0:T(8,128)(2,1)} %get-tuple-element.122.n2_ref, ...), custom_call_target="tpu_custom_call" | custom-call | flops 21743271936 | bytes 100000000 | tf_op jit(solution)/shard_map/experts/pallas_call | solution.py:1092
  260.1 3.6 all-to-all-start.2
  263.9 12.6 %all-to-all-done.2 = bf16[4,64,1152]{2,1,0:T(8,128)(2,1)S(1)} async-done(((bf16[4,64,1152]{2,1,0:T(8,128)(2,1)}), bf16[4,64,1152]{2,1,0:T(8,128)(2,1)S(1)}, u32[]{:S(2)}, u32[]{:S(2)}) %all-to-all-start.2) | async-done | bytes 589856 | tf_op jit(solution)/shard_map/all_to_all | solution.py:1137
  276.5 6.2 %all-to-all-start.3 = ((bf16[4,128,1152]{2,1,0:T(8,128)(2,1)}), bf16[4,128,1152]{2,1,0:T(8,128)(2,1)}, u32[]{:S(2)}, u32[]{:S(2)}) async-start(bf16[4,128,1152]{2,1,0:T(8,128)(2,1)} %get-tuple-element.137), calls=%async_computation.3 | async-start | bytes 2359296 | tf_op jit(solution)/shard_map/all_to_all | solution.py:1137
  286.4 6.3 %multiply_convert_fusion = (bf16[256,2304]{1,0:T(8,128)(2,1)}, f32[256,2304]{1,0:T(8,128)}) fusion(f32[256,2304]{1,0:T(8,128)} %get-tuple-element.117.z_ref, f32[256,2304]{1,0:T(8,128)} %get-tuple-element.148, f32[256,2304]{1,0:T(8,128)S(1)} %copy-done.3, f32[2304]{0:T(1024)S(1)} %get-tuple-element.182, bf16[2304,1152]{1,0:T(8,128)(2,1)S(1)} %copy-done.25, ...), kind=kOutput, calls=%fused_computation.16 | convolution fusion | flops 1367506944 | bytes 17114112 | tf_op jit(solution)/shard_map/dot_general | solution.py:1112
  292.7 9.6 %shard_map.263.own_ref = f32[16,2304]{1,0:T(8,128)} custom-call(f32[256,2304]{1,0:T(8,128)} %get-tuple-element.107.dte_ref, f32[256,2304]{1,0:T(8,128)} %get-tuple-element.179.gs_ref, f32[16,2304]{1,0:T(8,128)} %get-tuple-element.109.rate_ref, f32[4096,128]{1,0:T(8,128)} %get-tuple-element.130.c_ref), custom_call_target="tpu_custom_call" | custom-call | flops 75497472 | bytes 4718592 | tf_op jit(solution)/shard_map/pallas_call | solution.py:236
  302.3 10.6 %chain.3.next_ref = f32[16,2304]{1,0:T(8,128)} custom-call(f32[16,2304]{1,0:T(8,128)} %get-tuple-element.114.carry_ref, f32[16,2304]{1,0:T(8,128)} %shard_map.263.own_ref), custom_call_target="tpu_custom_call" | custom-call | tf_op jit(solution)/shard_map/chain/pallas_call | solution.py:954
  312.9 4.2 convolution_convert_fusion.1
  317.1 51.2 %back_pass.1 = (f32[256,2304]{1,0:T(8,128)}, f32[16,2304]{1,0:T(8,128)}, f32[128,2304]{1,0:T(8,128)}, f32[1,2304]{1,0:T(1,128)}, f32[1,2304]{1,0:T(1,128)}, /*index=5*/bf16[256,128]{1,0:T(8,128)(2,1)}) custom-call(f32[256,2304]{1,0:T(8,128)} %get-tuple-element.119.dt_ref, f32[256,2304]{1,0:T(8,128)} %get-tuple-element.107.dte_ref, ...), custom_call_target="tpu_custom_call" | custom-call | flops 245366784 | bytes 14155776 | tf_op jit(solution)/shard_map/back_pass/pallas_call | solution.py:337
  371.0 5.6 %fusion = f32[256,1152]{1,0:T(8,128)} fusion(bf16[256,2304]{1,0:T(8,128)(2,1)} %get-tuple-element.178, bf16[4608,1152]{1,0:T(8,128)(2,1)} %bitcast.68), kind=kOutput, calls=%fused_computation.2 | convolution fusion | flops 1358954496 | bytes 7667712 | tf_op jit(solution)/shard_map/dot_general | solution.py:1108
  377.6 9.9 %conv_back.1 = (bf16[256,2304]{1,0:T(8,128)(2,1)}, f32[8,2304]{1,0:T(8,128)}, f32[8,2304]{1,0:T(8,128)}, f32[128,2304]{1,0:T(8,128)}, f32[8,2304]{1,0:T(8,128)}) custom-call(f32[256,2304]{1,0:T(8,128)} %get-tuple-element.141.gval_ref, bf16[256,128]{1,0:T(8,128)(2,1)} %get-tuple-element.142.proj_ref, bf16[128,2304]{1,0:T(8,128)(2,1)} %get-tuple-element.101.xt_ref, ...), custom_call_target="tpu_custom_call" | custom-call | flops 35389440 | bytes 11796480 | tf_op jit(solution)/shard_map/conv_back/pallas_call | solution.py:391
  387.6 4.1 collective-permute-start
  391.7 4.7 all-to-all-start.4
  396.4 2.7 fusion.8
  400.9 5.3 %fusion.24 = (f32[1152]{0:T(1024)S(1)}, f32[256]{0:T(256)S(1)}, f32[256,1152]{1,0:T(8,128)}) fusion(f32[256]{0:T(256)S(1)} %copy-done.23, bf16[1,256,1152]{2,1,0:T(8,128)(2,1)S(1)} %copy-done.1, f32[1152]{0:T(1024)S(1)} %get-tuple-element.187, f32[256,1152]{1,0:T(8,128)S(1)} %copy-done.28, bf16[4608,1152]{1,0:T(8,128)(2,1)} %bitcast.69, ...), kind=kOutput, calls=%fused_computation.35 | convolution fusion | flops 1363671680 | bytes 9448448 | tf_op jit(solution)/shard_map/dot_general | solution.py:1108
  407.0 3.2 pack_small.1
  412.2 6.7 %convolution_convert_fusion = bf16[4608,1152]{1,0:T(8,128)(2,1)} fusion(bf16[256,2304]{1,0:T(8,128)(2,1)S(1)} %copy-done.27, bf16[8,2304]{1,0:T(8,128)(2,1)S(1)} %add_convert_fusion, bf16[248,2304]{1,0:T(8,128)(2,1)S(1)} %copy-done.12, bf16[272,1152]{1,0:T(8,128)(2,1)S(1)} %copy-done.5), kind=kOutput, calls=%fused_computation | convolution fusion | flops 2730295296 | bytes 13565952 | tf_op jit(solution)/shard_map/dot_general | solution.py:1116
  418.9 13.7 %all-to-all-done.4 = bf16[4,2,96,1152]{3,2,1,0:T(8,128)(2,1)} async-done(((bf16[4,2,96,1152]{3,2,1,0:T(8,128)(2,1)}), bf16[4,2,96,1152]{3,2,1,0:T(8,128)(2,1)}, u32[]{:S(2)}, u32[]{:S(2)}) %all-to-all-start.4) | async-done | bytes 1769504 | tf_op jit(solution)/shard_map/all_to_all | solution.py:1137
  432.6 2.8 slice_bitcast_fusion
  435.5 2.0 pad.29.proj_ref
  437.5 67.8 %scatter_all.1 = (f32[144,1152]{1,0:T(8,128)}, f32[80,256]{1,0:T(8,128)}, bf16[4,80,1152]{2,1,0:T(8,128)(2,1)}) custom-call(bf16[4,2,4,144,1152]{4,3,2,1,0:T(8,128)(2,1)} %bitcast.75, bf16[4,2,4,80,256]{4,3,2,1,0:T(8,128)(2,1)} %bitcast.76, bf16[4,80,1152]{2,1,0:T(8,128)(2,1)} %pad.29.proj_ref), custom_call_target="tpu_custom_call" | custom-call | bytes 200000000 | tf_op jit(solution)/shard_map/scatter_all/pallas_call | solution.py:767
  505.3 4.8 finish.1
  (134 shorter events, 31.6 us)
Async XLA Ops:
  7.2 159.0 %all-gather.6.cloned.1.call-start = ((), (), s32[]{:S(2)}) async-start(), calls=%async_computation.7 | async-start | bytes 5474304 | tf_op jit(solution)/shard_map/all_gather | solution.py:1162
  7.9 183.0 %all-gather.8.cloned.1.call-start = ((), (), s32[]{:S(2)}) async-start(), calls=%async_computation.10 | async-start | bytes 7962624 | tf_op jit(solution)/shard_map/all_gather | solution.py:1177
  99.6 11.8 %copy-start.18 = (f32[32,256]{1,0:T(8,128)S(1)}, f32[32,256]{1,0:T(8,128)}, u32[]{:S(2)}) copy-start(f32[32,256]{1,0:T(8,128)} %get-tuple-element.98) | copy-start | bytes 98308
  99.6 11.9 %copy-start = (bf16[1,256,1152]{2,1,0:T(8,128)(2,1)S(1)}, bf16[1,256,1152]{2,1,0:T(8,128)(2,1)}, u32[]{:S(2)}) copy-start(bf16[1,256,1152]{2,1,0:T(8,128)(2,1)} %param.16) | copy-start | bytes 1769476
  99.6 11.9 %copy-start.16 = (bf16[16,1152]{1,0:T(8,128)(2,1)S(1)}, bf16[16,1152]{1,0:T(8,128)(2,1)}, u32[]{:S(2)}) copy-start(bf16[16,1152]{1,0:T(8,128)(2,1)} %get-tuple-element.94) | copy-start | bytes 110596
  99.6 48.3 %all-to-all-start = ((bf16[4,96,1152]{2,1,0:T(8,128)(2,1)}), bf16[4,96,1152]{2,1,0:T(8,128)(2,1)S(1)}, u32[]{:S(2)}, u32[]{:S(2)}) async-start(bf16[4,96,1152]{2,1,0:T(8,128)(2,1)} %param.31), calls=%async_computation | async-start | bytes 1769472 | tf_op jit(solution)/shard_map/all_to_all | solution.py:1137
  107.7 95.0 %all-gather.10.cloned.1.call-start = ((), (), s32[]{:S(2)}) async-start(), calls=%async_computation.11 | async-start | bytes 7962624 | tf_op jit(solution)/shard_map/all_gather | solution.py:1204
  112.0 4.7 copy-start.4
  129.4 19.4 %copy-start.24 = (s32[1,256,1]{1,2,0:T(1,128)S(1)}, s32[1,256,1]{1,2,0:T(1,128)}, u32[]{:S(2)}) copy-start(s32[1,256,1]{1,2,0:T(1,128)} %param.18) | copy-start | bytes 3076
  156.9 34.0 %all-to-all-start.1 = ((bf16[4,128,1152]{2,1,0:T(8,128)(2,1)}), bf16[4,128,1152]{2,1,0:T(8,128)(2,1)S(1)}, u32[]{:S(2)}, u32[]{:S(2)}) async-start(bf16[4,128,1152]{2,1,0:T(8,128)(2,1)} %bitcast.15), calls=%async_computation.1 | async-start | bytes 2359296 | tf_op jit(solution)/shard_map/all_to_all | solution.py:1137
  163.5 204.8 %reduce-scatter.3.cloned.1.call-start = ((), (), s32[]{:S(2)}) async-start(), calls=%async_computation.8 | async-start | bytes 15925248 | tf_op jit(solution)/shard_map/reduce_scatter | solution.py:1223
  190.9 11.8 %copy-start.10 = (bf16[4,128,1152]{2,1,0:T(8,128)(2,1)}, bf16[4,128,1152]{2,1,0:T(8,128)(2,1)S(1)}, u32[]{:S(2)}) copy-start(bf16[4,128,1152]{2,1,0:T(8,128)(2,1)S(1)} %all-to-all-done.1.go_ref) | copy-start | bytes 3538948
  260.1 3.6 copy-start.2
  260.1 16.4 %all-to-all-start.2 = ((bf16[4,64,1152]{2,1,0:T(8,128)(2,1)}), bf16[4,64,1152]{2,1,0:T(8,128)(2,1)S(1)}, u32[]{:S(2)}, u32[]{:S(2)}) async-start(bf16[4,64,1152]{2,1,0:T(8,128)(2,1)} %get-tuple-element.127), calls=%async_computation.2 | async-start | bytes 1179648 | tf_op jit(solution)/shard_map/all_to_all | solution.py:1137
  263.9 19.0 %copy-start.26 = (bf16[4,64,1152]{2,1,0:T(8,128)(2,1)S(1)}, bf16[4,64,1152]{2,1,0:T(8,128)(2,1)}, u32[]{:S(2)}) copy-start(bf16[4,64,1152]{2,1,0:T(8,128)(2,1)} %get-tuple-element.126) | copy-start | bytes 1769476
  276.5 91.7 %all-to-all-start.3 = ((bf16[4,128,1152]{2,1,0:T(8,128)(2,1)}), bf16[4,128,1152]{2,1,0:T(8,128)(2,1)}, u32[]{:S(2)}, u32[]{:S(2)}) async-start(bf16[4,128,1152]{2,1,0:T(8,128)(2,1)} %get-tuple-element.137), calls=%async_computation.3 | async-start | bytes 2359296 | tf_op jit(solution)/shard_map/all_to_all | solution.py:1137
  282.7 152.8 %reduce-scatter.5.cloned.1.call-start = ((), (), s32[]{:S(2)}) async-start(), calls=%async_computation.9 | async-start | bytes 5971968 | tf_op jit(solution)/shard_map/reduce_scatter | solution.py:1255
  282.9 2.5 copy-start.25
  284.2 2.2 copy-start.3
  292.7 20.2 %copy-start.7 = (bf16[256,2304]{1,0:T(8,128)(2,1)S(1)}, bf16[256,2304]{1,0:T(8,128)(2,1)}, u32[]{:S(2)}) copy-start(bf16[256,2304]{1,0:T(8,128)(2,1)} %get-tuple-element.133) | copy-start | bytes 3538948
  368.3 1.8 copy-start.15
  387.6 11.7 %collective-permute-start = (f32[8,2304]{1,0:T(8,128)}, f32[8,2304]{1,0:T(8,128)S(1)}, u32[]{:S(2)}, u32[]{:S(2)}) collective-permute-start(f32[8,2304]{1,0:T(8,128)} %get-tuple-element.147), channel_id=1, source_target_pairs={{1,0},{2,1},{3,2},{5,4},{6,5},{7,6},{9,8},{10,9},{11,10},{13,12},{... | collective-permute-start | bytes 221192 | tf_op jit(solution)/shard_map/ppermute | solution.py:1122
  391.7 40.9 %all-to-all-start.4 = ((bf16[4,2,96,1152]{3,2,1,0:T(8,128)(2,1)}), bf16[4,2,96,1152]{3,2,1,0:T(8,128)(2,1)}, u32[]{:S(2)}, u32[]{:S(2)}) async-start(bf16[4,2,96,1152]{3,2,1,0:T(8,128)(2,1)} %bitcast.77), calls=%async_computation.5 | async-start | bytes 3538944 | tf_op jit(solution)/shard_map/all_to_all | solution.py:1137
  396.4 2.8 copy-start.13
  399.1 1.8 copy-start.28
  399.2 7.0 %copy-start.11 = (bf16[248,2304]{1,0:T(8,128)(2,1)}, bf16[248,2304]{1,0:T(8,128)(2,1)S(1)}, u32[]{:S(2)}) copy-start(bf16[248,2304]{1,0:T(8,128)(2,1)S(1)} %slice.110) | copy-start | bytes 3428356
  400.9 5.3 %copy-start.17 = (f32[4608]{0:T(1024)S(1)}, f32[4608]{0:T(1024)}, u32[]{:S(2)}) copy-start(f32[4608]{0:T(1024)} %reshape.193) | copy-start | bytes 55300
  400.9 5.3 %copy-start.21 = (f32[1152]{0:T(1024)S(1)}, f32[1152]{0:T(1024)}, u32[]{:S(2)}) copy-start(f32[1152]{0:T(1024)} %get-tuple-element.174) | copy-start | bytes 13828
  407.0 3.2 copy-start.9
  407.0 3.2 copy-start.22
  410.2 2.0 copy-start.27
  505.3 4.8 copy-start.14
  (8 other events, 9.2 us)
Sparse Core Ops, SparseCore 0:
  10.9 85.8 all-gather.5
  99.7 52.0 all-gather.7
  153.7 48.9 all-gather.9
  260.2 98.8 reduce-scatter.2
  368.5 57.9 reduce-scatter.4

commit v4 on v3

--- a/solution.py
+++ b/solution.py
@@ -13,6 +13,7 @@
 STEP = 16
 VM = 56 * 1024 * 1024
 MESH = pl.DeviceIdType.MESH
+SMALL = pl.CostEstimate(flops=0, bytes_accessed=0, transcendentals=0)
 NT = (((1,), (1,)), ((), ()))
 TN = (((0,), (0,)), ((), ()))
 
@@ -45,47 +46,55 @@
         state_ref[:, c] = state[j]
         carry_ref[:, c] = jnp.exp2(jnp.broadcast_to(summed[:, c], (n, 128)) * rates[j])
 
-def front_kernel(halo, ext_ref, normed_ref, wc_ref, wz_ref, xt_ref, taps_ref, bias_ref, same_ref, conv_ref, sum_ref, values_ref, z_ref, proj_ref):
+def front_kernel(rim_ref, tok_ref, gain_ref, wc_ref, wz_ref, xt_ref, taps_ref, bias_ref, same_ref, normed_ref, conv_ref, sum_ref, values_ref, z_ref, proj_ref, ext):
     rows, wide = sum_ref.shape
+    halo = rim_ref.shape[0]
     taps = taps_ref.shape[0]
-    conv_ref[...] = lax.dot_general(ext_ref[...], wc_ref[...], NT, preferred_element_type=F32).astype(BF).astype(F32)
-    z_ref[...] = lax.dot_general(normed_ref[...], wz_ref[...], NT, preferred_element_type=F32)
+
+    @pl.when(pl.program_id(0) == 0)
+    def _():
+        for ref, lo in ((rim_ref, 0), (tok_ref, halo)):
+            tok = ref[...].astype(F32)
+            scale = lax.rsqrt(jnp.mean(tok * tok, axis=1, keepdims=True) + EPS)
+            ext[lo : lo + ref.shape[0], :] = (tok * scale * gain_ref[...]).astype(BF)
+        normed_ref[...] = ext[halo:, :]
+        proj_ref[...] = jnp.zeros_like(proj_ref)
+
+    conv_ref[...] = lax.dot_general(ext[...], wc_ref[...], NT, preferred_element_type=F32).astype(BF).astype(F32)
+    z_ref[...] = lax.dot_general(ext[halo:, :], wz_ref[...], NT, preferred_element_type=F32)
+    same = [jnp.broadcast_to(same_ref[:, k : k + 1], (rows, 128)) for k in range(taps)]
     for j in range(wide // 128):
         c = slice(j * 128, (j + 1) * 128)
         total = jnp.broadcast_to(bias_ref[:, c], (rows, 128))
         for k in range(taps):
             lo = halo - taps + 1 + k
-            total = total + taps_ref[k : k + 1, c] * conv_ref[lo : lo + rows, c] * same_ref[k]
+            total = total + taps_ref[k : k + 1, c] * conv_ref[lo : lo + rows, c] * same[k]
         sum_ref[:, c] = total
         values_ref[:, c] = total * jax.nn.sigmoid(total)
-
-    @pl.when(pl.program_id(0) == 0)
-    def _():
-        proj_ref[...] = jnp.zeros_like(proj_ref)
-
     proj_ref[...] += lax.dot_general(values_ref[...].astype(BF), xt_ref[...], NT, preferred_element_type=F32)
 
 
-def front(normed_ext, normed, full_in, x_t, conv_taps, bias, same, halo, wide):
-    rows, width = normed.shape
+def front(rim, tok, gain, full_in, x_t, conv_taps, bias, same, wide):
+    rows, width = tok.shape
+    halo = rim.shape[0]
     chans = full_in.shape[0] // 2
     taps = conv_taps.shape[0]
-    wide_same = jnp.broadcast_to(same.T[:, :, None], (taps, rows, 128))
     col = lambda r: pl.BlockSpec((r, wide), lambda g: (0, g))
-    whole = lambda a: pl.BlockSpec(a.shape, lambda g: (0,) * len(a.shape))
+    whole = lambda a: pl.BlockSpec(a.shape, lambda g: (0, 0))
     steps = chans // wide
     f32 = lambda r: jax.ShapeDtypeStruct((r, chans), F32)
     return pl.pallas_call(
-        functools.partial(front_kernel, halo),
+        front_kernel,
         grid=(steps,),
-        in_specs=[whole(normed_ext), whole(normed), pl.BlockSpec((wide, width), lambda g: (g, 0)), pl.BlockSpec((wide, width), lambda g: (g + steps, 0)),
-                  col(128), col(taps), col(1), whole(wide_same)],
-        out_specs=[col(rows + halo), col(rows), col(rows), col(rows), pl.BlockSpec((rows, 128), lambda g: (0, 0))],
-        out_shape=[f32(rows + halo), f32(rows), f32(rows), f32(rows), jax.ShapeDtypeStruct((rows, 128), F32)],
+        in_specs=[whole(rim), whole(tok), whole(gain), pl.BlockSpec((wide, width), lambda g: (g, 0)), pl.BlockSpec((wide, width), lambda g: (g + steps, 0)),
+                  col(128), col(taps), col(1), whole(same)],
+        out_specs=[whole(tok), col(rows + halo), col(rows), col(rows), col(rows), pl.BlockSpec((rows, 128), lambda g: (0, 0))],
+        out_shape=[jax.ShapeDtypeStruct((rows, width), BF), f32(rows + halo), f32(rows), f32(rows), f32(rows), jax.ShapeDtypeStruct((rows, 128), F32)],
+        scratch_shapes=[pltpu.VMEM((rows + halo, width), BF)],
         compiler_params=pltpu.CompilerParams(vmem_limit_bytes=VM),
         cost_estimate=pl.CostEstimate(flops=4*rows*chans*width, bytes_accessed=4*chans*width + 16*rows*chans, transcendentals=rows*chans),
         name="front",
-    )(normed_ext, normed, full_in, full_in, x_t, conv_taps, bias, wide_same)
+    )(rim, tok, gain, full_in, full_in, x_t, conv_taps, bias, same)
 
 
 def steps_kernel(n, rank_cols, proj_ref, keep_ref, values_ref, dtt_ref, dtb_ref, alog_ref,
@@ -117,20 +126,21 @@
     pre_ref[...] = pre
     dt_ref[...] = dt
     dtx_ref[...] = dt * values_ref[...]
+    taps = keep_ref.shape[1]
+    keep = jnp.broadcast_to(keep_ref[:, taps - 2 : taps - 1], (rows, 128))
     for j in range(wide // 128):
         c = slice(j * 128, (j + 1) * 128)
-        dte_ref[:, c] = jnp.where(keep_ref[...] > 0, dt[:, c], 1e30)
+        dte_ref[:, c] = jnp.where(keep > 0, dt[:, c], 1e30)
     rate = -jnp.exp(alog_ref[...])
     rate_ref[...] = rate
     rate2_ref[...] = rate * math.log2(math.e)
     state_kernel(n, dte_ref, dtx_ref, rate2_ref, bw_ref, state_ref, carry_ref)
 
 
-def steps(proj, keep, values, dt_t, dtb, alog_t, rank_cols, wide):
+def steps(proj, same, values, dt_t, dtb, alog_t, rank_cols, wide):
     rows, chans = values.shape
     n = alog_t.shape[0]
     groups = STEP * n
-    wide_keep = jnp.broadcast_to(keep, (rows, 128))
     col = lambda r: pl.BlockSpec((r, wide), lambda g: (0, g))
     fixed = lambda *s: pl.BlockSpec(s, lambda g: (0, 0))
     f32 = lambda *s: jax.ShapeDtypeStruct(s, F32)
@@ -138,17 +148,17 @@
     return pl.pallas_call(
         functools.partial(steps_kernel, n, rank_cols),
         grid=(chans // wide,),
-        in_specs=[fixed(rows, 128), fixed(rows, 128), col(rows), col(128), col(1), col(n)],
+        in_specs=[fixed(rows, 128), fixed(*same.shape), col(rows), col(128), col(1), col(n)],
         out_specs=[fixed(rows, 128), fixed(rows * n, 128), fixed(rows * n, 128), fixed(rows, groups), fixed(rows, groups)] + [col(rows)] * 4 + [col(n)] * 4,
         out_shape=[bf(rows, 128), f32(rows * n, 128), f32(rows * n, 128), bf(rows, groups), bf(rows, groups)] + [f32(rows, chans)] * 4 + [f32(n, chans)] * 4,
         compiler_params=pltpu.CompilerParams(vmem_limit_bytes=VM),
         cost_estimate=pl.CostEstimate(flops=10*rows*chans*n, bytes_accessed=24*rows*chans, transcendentals=rows*chans*n),
         name="steps",
-    )(proj, wide_keep, values, dt_t, dtb, alog_t)
-
-
-def scan_kernel(n, dte_ref, dtx_ref, rate_ref, b_ref, cblk_ref, start_ref, values_ref, z_ref, skip_ref, out_ref, tok_ref, gain_ref,
-                y_ref, check_ref, gated_ref, first_ref, normed_ref, hs):
+    )(proj, same, values, dt_t, dtb, alog_t)
+
+
+def scan_kernel(n, dte_ref, dtx_ref, rate_ref, b_ref, cblk_ref, start_ref, values_ref, z_ref, skip_ref, out_ref, tok_ref, gain_ref, pick_ref,
+                y_ref, check_ref, gated_ref, first_ref, normed_ref, sent_ref, hs):
     rows, wide = dte_ref.shape
     tiles = wide // 128
     rates = [rate_ref[:, j*128:(j+1)*128] for j in range(tiles)]
@@ -187,9 +197,10 @@
         first = first_ref[...]
         scale = lax.rsqrt(jnp.mean(first * first, axis=1, keepdims=True) + EPS)
         normed_ref[...] = (first * scale * gain_ref[...]).astype(BF)
-
-
-def scan_pass(dte, dtx, rates2, b_wide, c_blk, start, values, z, skip, full_out, tok, gain, wide):
+        sent_ref[...] = lax.dot_general(pick_ref[...], normed_ref[...], TN, preferred_element_type=F32).astype(BF)
+
+
+def scan_pass(dte, dtx, rates2, b_wide, c_blk, start, values, z, skip, full_out, tok, gain, pick, wide):
     rows, chans = dte.shape
     n = rates2.shape[0]
     width = tok.shape[1]
@@ -198,15 +209,15 @@
     return pl.pallas_call(
         functools.partial(scan_kernel, n),
         grid=(chans // wide,),
-        in_specs=[col(rows), col(rows), col(n), whole(b_wide), whole(c_blk), col(n), col(rows), col(rows), col(1), pl.BlockSpec((wide, width), lambda g: (g, 0)), whole(tok), whole(gain)],
-        out_specs=[col(rows), col(rows // STEP * n), col(rows), whole(tok), whole(tok)],
+        in_specs=[col(rows), col(rows), col(n), whole(b_wide), whole(c_blk), col(n), col(rows), col(rows), col(1), pl.BlockSpec((wide, width), lambda g: (g, 0)), whole(tok), whole(gain), whole(pick)],
+        out_specs=[col(rows), col(rows // STEP * n), col(rows), whole(tok), whole(tok), pl.BlockSpec((pick.shape[1], width), lambda g: (0, 0))],
         out_shape=[jax.ShapeDtypeStruct((rows, chans), F32), jax.ShapeDtypeStruct((rows // STEP * n, chans), F32), jax.ShapeDtypeStruct((rows, chans), BF),
-                   jax.ShapeDtypeStruct((rows, width), F32), jax.ShapeDtypeStruct((rows, width), BF)],
+                   jax.ShapeDtypeStruct((rows, width), F32), jax.ShapeDtypeStruct((rows, width), BF), jax.ShapeDtypeStruct((pick.shape[1], width), BF)],
         scratch_shapes=[pltpu.VMEM((STEP * n, wide), BF)],
         compiler_params=pltpu.CompilerParams(vmem_limit_bytes=VM),
         cost_estimate=pl.CostEstimate(flops=10*rows*chans*n, bytes_accessed=12*rows*chans, transcendentals=rows*chans*n),
         name="scan_pass",
-    )(dte, dtx, rates2, b_wide, c_blk, start, values, z, skip, full_out, tok, gain)
+    )(dte, dtx, rates2, b_wide, c_blk, start, values, z, skip, full_out, tok, gain, pick)
 
 
 def back_state_kernel(n, dte_ref, gs_ref, rate_ref, c_ref, out_ref):
@@ -230,21 +241,48 @@
     for j in range(tiles):
         out_ref[:, j*128:(j+1)*128] = state[j]
 
-def back_state_pass(dte, gs, rates2, c_wide, wide):
+def back_front_kernel(n, order, steps, grad_ref, out_ref, z_ref, y_ref, values_ref, skip_ref, gated_ref, dte_ref, rate_ref, c_ref, gs_ref, gz_ref, gwo_ref, state_ref):
+    grad = grad_ref[...]
+    gated = lax.dot_general(grad, out_ref[...], NT, preferred_element_type=F32)
+    z = z_ref[...]
+    sig = jax.nn.sigmoid(z)
+    gs_ref[...] = gated * (z * sig)
+    gz_ref[...] = (gated * (y_ref[...] + skip_ref[...] * values_ref[...]) * (sig * (1.0 + z * (1.0 - sig)))).astype(BF)
+    grad_out = lax.dot_general(gated_ref[...], grad, TN, preferred_element_type=F32).astype(BF)
+    if order is None:
+        gwo_ref[...] = grad_out
+    else:
+        per = len(order) // steps
+        size = grad_out.shape[0] // per
+        for g in range(steps):
+
+            @pl.when(pl.program_id(0) == g)
+            def _():
+                for to, share in enumerate(order[g * per : (g + 1) * per]):
+                    at = (share - g * per) * size
+                    gwo_ref[to * size : (to + 1) * size, :] = grad_out[at : at + size]
+
+    back_state_kernel(n, dte_ref, gs_ref, rate_ref, c_ref, state_ref)
+
+
+def back_front(grad, full_out, z, scanned, values, skip, gated, dte, rates2, c_wide, wide, order=None):
     rows, chans = dte.shape
+    width = grad.shape[1]
     n = rates2.shape[0]
+    col = lambda r: pl.BlockSpec((r, wide), lambda g: (0, g))
+    whole = lambda a: pl.BlockSpec(a.shape, lambda g: (0, 0))
+    flat = pl.BlockSpec((wide, width), lambda g: (g, 0))
     return pl.pallas_call(
-        functools.partial(back_state_kernel, n),
+        functools.partial(back_front_kernel, n, order, chans // wide),
         grid=(chans // wide,),
-        in_specs=[pl.BlockSpec((rows, wide), lambda g: (0, g)),
-                  pl.BlockSpec((rows, wide), lambda g: (0, g)),
-                  pl.BlockSpec((n, wide), lambda g: (0, g)),
-                  pl.BlockSpec(c_wide.shape, lambda g: (0, 0))],
-        out_specs=pl.BlockSpec((n, wide), lambda g: (0, g)),
-        out_shape=jax.ShapeDtypeStruct((n, chans), F32),
+        in_specs=[whole(grad), flat, col(rows), col(rows), col(rows), col(1), col(rows), col(rows), col(n), whole(c_wide)],
+        out_specs=[col(rows), col(rows), flat, col(n)],
+        out_shape=[jax.ShapeDtypeStruct((rows, chans), F32), jax.ShapeDtypeStruct((rows, chans), BF), jax.ShapeDtypeStruct((chans, width), BF), jax.ShapeDtypeStruct((n, chans), F32)],
         compiler_params=pltpu.CompilerParams(vmem_limit_bytes=VM),
         cost_estimate=pl.CostEstimate(flops=8*rows*chans*n, bytes_accessed=8*rows*chans, transcendentals=rows*chans*n),
-    )(dte, gs, rates2, c_wide)
+        name="back_front",
+    )(grad, full_out, z, scanned, values, skip, gated, dte, rates2, c_wide)
+
 
 def back_kernel(n, rank_cols, dt_ref, dte_ref, dtx_ref, gs_ref, values_ref, pre_ref, skip_ref, rate_ref, rawrate_ref, b_ref, c_ref, bblk_ref, check_ref, next_ref, low_ref, wdt_ref,
                 gval_ref, glog_ref, gwdt_ref, gdtb_ref, gskip_ref, proj_ref, us, decs, hs, ls, ps, gdtx, gdt, gb, gc, rank):
@@ -349,7 +387,7 @@
     )(dt, dte, dtx, gs, values, pre, skip, rates2, rates, b_wide, c_wide, b_blk, check, nxt, low, wdt)
 
 
-def conv_back_kernel(halo, gval_ref, proj_ref, xt_ref, values_ref, sum_ref, ext_ref, same_ref, later_ref, taps_ref,
+def conv_back_kernel(halo, gval_ref, proj_ref, xt_ref, values_ref, sum_ref, ext_ref, same_ref, taps_ref,
                      gconv_ref, last_ref, rim_ref, gxt_ref, gtaps_ref, pad):
     rows, wide = gval_ref.shape
     taps = taps_ref.shape[0]
@@ -361,18 +399,21 @@
     pad[0:rows, :] = grad_values * (sig * (1.0 + sums * (1.0 - sig)))
     pad[rows:, :] = jnp.zeros((pad.shape[0] - rows, wide), F32)
     row = lax.broadcasted_iota(jnp.int32, (8, 128), 0)
+    same = [jnp.broadcast_to(same_ref[:, k : k + 1], (rows, 128)) for k in range(taps)]
+    rowed = lax.broadcasted_iota(jnp.int32, (rows, 128), 0)
+    later = [jnp.where(rowed < rows - (taps - 1 - k), pltpu.roll(same[k], (rows - (taps - 1 - k)) % rows, 0), 0.0) for k in range(taps)]
     for j in range(wide // 128):
         c = slice(j * 128, (j + 1) * 128)
         grads = pad[0:rows, c]
-        sums_of = [jnp.sum(grads * same_ref[k] * ext_ref[halo - taps + 1 + k : halo - taps + 1 + k + rows, c], axis=0, keepdims=True) for k in range(taps)]
+        sums_of = [jnp.sum(grads * same[k] * ext_ref[halo - taps + 1 + k : halo - taps + 1 + k + rows, c], axis=0, keepdims=True) for k in range(taps)]
         sums_of.append(jnp.sum(grads, axis=0, keepdims=True))
         total = jnp.zeros((rows, 128), F32)
         rim = jnp.zeros((8, 128), F32)
         for k in range(taps):
             weight = taps_ref[k : k + 1, c]
-            total = total + pad[taps - 1 - k : taps - 1 - k + rows, c] * later_ref[k] * weight
+            total = total + pad[taps - 1 - k : taps - 1 - k + rows, c] * later[k] * weight
             if k < taps - 1:
-                moved = pltpu.roll(grads[0:8] * same_ref[k, 0:8, :], 8 - taps + 1 + k, 0)
+                moved = pltpu.roll(grads[0:8] * same[k][0:8], 8 - taps + 1 + k, 0)
                 rim = rim + jnp.where(row >= 8 - taps + 1 + k, moved, 0.0) * weight
         gconv_ref[:, c] = total.astype(BF)
         last_ref[:, c] = total[rows - 8 :]
@@ -383,22 +424,20 @@
 def conv_back(gval, proj, x_t, values, sums, ext, same, conv_taps, halo, wide):
     rows, chans = gval.shape
     taps = conv_taps.shape[0]
-    later = jnp.stack([jnp.pad(same[taps - 1 - k :, k], (0, taps - 1 - k)) for k in range(taps)])
-    cover = lambda a: jnp.broadcast_to(a[:, :, None], (taps, rows, 128))
     col = lambda r: pl.BlockSpec((r, wide), lambda g: (0, g))
-    mask = pl.BlockSpec((taps, rows, 128), lambda g: (0, 0, 0))
+    mask = pl.BlockSpec(same.shape, lambda g: (0, 0))
     f32 = lambda r: jax.ShapeDtypeStruct((r, chans), F32)
     return pl.pallas_call(
         functools.partial(conv_back_kernel, halo),
         grid=(chans // wide,),
-        in_specs=[col(rows), pl.BlockSpec(proj.shape, lambda g: (0, 0)), col(x_t.shape[0]), col(rows), col(rows), col(ext.shape[0]), mask, mask, col(taps)],
+        in_specs=[col(rows), pl.BlockSpec(proj.shape, lambda g: (0, 0)), col(x_t.shape[0]), col(rows), col(rows), col(ext.shape[0]), mask, col(taps)],
         out_specs=[col(rows), col(8), col(8), col(x_t.shape[0]), col(8)],
         out_shape=[jax.ShapeDtypeStruct((rows, chans), BF), f32(8), f32(8), f32(x_t.shape[0]), f32(8)],
         scratch_shapes=[pltpu.VMEM((rows + 8, wide), F32)],
         compiler_params=pltpu.CompilerParams(vmem_limit_bytes=VM),
         cost_estimate=pl.CostEstimate(flops=60*rows*chans, bytes_accessed=20*rows*chans, transcendentals=rows*chans),
         name="conv_back",
-    )(gval, proj, x_t, values, sums, ext, cover(same.T), cover(later), conv_taps)
+    )(gval, proj, x_t, values, sums, ext, same, conv_taps)
 
 
 def flip(value, bit):
@@ -625,7 +664,7 @@
     )(w_in, rest, up, tok, ids)
 
 
-def scatter_kernel(parts, count, in_ref, rest_ref, proj_ref, oin_ref, orest_ref, oproj_ref, mine_a, mine_b, sib_a, sib_b, far_a, far_b, near_a, near_b, zgot_a, zgot_b, final_a, final_b,
+def scatter_kernel(parts, count, in_ref, rest_ref, proj_ref, down_ref, oin_ref, orest_ref, oproj_ref, odown_ref, mine_a, mine_b, sib_a, sib_b, far_a, far_b, near_a, near_b, zgot_a, zgot_b, final_a, final_b,
                    load_sem, sib_send, sib_recv, two_send, two_recv, one_send, one_recv, z_send, z_recv, end_send, end_recv, end_local,
                    swap_local, swap_send, swap_recv):
     dp, z = lax.axis_index("dp"), lax.axis_index("seq")
@@ -636,7 +675,7 @@
     peers = [(dp, lax.rem(z + j, count)) for j in range(1, count)]
     greet([sibling, (flip(dp, 4), z), (flip(dp, 2), z)] + peers)
 
-    swap = ZSwap(((proj_ref, oproj_ref),), swap_local, swap_send, swap_recv, count)
+    swap = ZSwap(((proj_ref, oproj_ref), (down_ref, odown_ref)), swap_local, swap_send, swap_recv, count)
 
     def role(which, first_bit, second_bit):
         chunks, other = parts[which], parts[1 - which]
@@ -753,7 +792,7 @@
     swap.wait()
 
 
-def scatter_all(g_in, g_rest, proj, cut, collective_id):
+def scatter_all(g_in, g_rest, proj, down, cut, collective_id):
     count = g_in.shape[2]
     rows_in, rows_rest = g_in.shape[3], g_rest.shape[3]
     parts = (((0, 0, cut),), ((0, cut, rows_in - cut), (1, 0, rows_rest)))
@@ -766,19 +805,20 @@
 
     return pl.pallas_call(
         functools.partial(scatter_kernel, parts, count),
-        in_specs=[pl.BlockSpec(memory_space=pl.ANY)] * 3,
-        out_specs=[pl.BlockSpec(memory_space=pl.ANY)] * 3,
-        out_shape=[jax.ShapeDtypeStruct(g_in.shape[3:], F32), jax.ShapeDtypeStruct(g_rest.shape[3:], F32), jax.ShapeDtypeStruct(proj.shape, proj.dtype)],
+        in_specs=[pl.BlockSpec(memory_space=pl.ANY)] * 4,
+        out_specs=[pl.BlockSpec(memory_space=pl.ANY)] * 4,
+        out_shape=[jax.ShapeDtypeStruct(g_in.shape[3:], F32), jax.ShapeDtypeStruct(g_rest.shape[3:], F32), jax.ShapeDtypeStruct(proj.shape, proj.dtype), jax.ShapeDtypeStruct(down.shape, down.dtype)],
         scratch_shapes=bufs(places) + bufs(places) + bufs(2 * count) + bufs(count) + bufs(count - 1) + bufs(0, F32)
         + [sems(places, 2), sems(places, 2), sems(places, 2), sems(2 * count, 2), sems(2 * count, 2), sems(count, 2), sems(count, 2),
-           sems(count - 1, 2), sems(count - 1, 2), sems(2, 2), sems(2, 2), sems(2), sems(1), sems(1, count - 1), sems(1, count - 1)],
+           sems(count - 1, 2), sems(count - 1, 2), sems(2, 2), sems(2, 2), sems(2), sems(2), sems(2, count - 1), sems(2, count - 1)],
         compiler_params=pltpu.CompilerParams(collective_id=collective_id, has_side_effects=True, vmem_limit_bytes=VM),
         cost_estimate=pl.CostEstimate(flops=0, bytes_accessed=200_000_000, transcendentals=0),
         name="scatter_all",
-    )(g_in, g_rest, proj)
-
-
-def unpack_kernel(own, x_cols, dt_cols, pack_ref, xt_ref, dtt_ref, high_ref, small_ref, tall):
+    )(g_in, g_rest, proj, down)
+
+
+def unpack_kernel(own, cuts, pack_ref, small_ref, *refs):
+    outs, tall = refs[:-1], refs[-1]
     for b in range(pack_ref.shape[0]):
         block = pack_ref[b].astype(F32)
         tall[b * own : (b + 1) * own, :] = block[:own]
@@ -786,21 +826,29 @@
     for j in range(tall.shape[0] // 128):
         c = slice(j * 128, (j + 1) * 128)
         turned = tall[c, :].T
-        for ref, lo, size in ((xt_ref, 0, x_cols), (dtt_ref, x_cols, dt_cols)):
-            ref[:, c] = jnp.concatenate([turned[lo : lo + size], jnp.zeros((ref.shape[0] - size, 128), F32)], axis=0).astype(BF)
-        high_ref[:, c] = turned[x_cols + dt_cols :]
-
-
-def unpack(pack, own, x_cols, dt_cols):
+        for ref, (lo, size) in zip(outs, cuts):
+            part = turned[lo : lo + size]
+            if ref.shape[0] > size:
+                part = jnp.concatenate([part, jnp.zeros((ref.shape[0] - size, 128), F32)], axis=0)
+            ref[:, c] = part.astype(ref.dtype)
+
+
+def unpack(pack, own, sizes):
     blocks, _, cols = pack.shape
     chans = blocks * own
+    cuts, at = [], 0
+    for size in sizes:
+        cuts.append((at, size))
+        at += size
+    rows = [128, 128] + list(sizes[2:])
+    kinds = [BF, BF] + [F32] * (len(sizes) - 2)
     if own % 8:
         turned = pack[:, :own].reshape(chans, cols).T
-        grown = lambda a: jnp.pad(a, ((0, 128 - a.shape[0]), (0, 0)))
-        return grown(turned[:x_cols]), grown(turned[x_cols : x_cols + dt_cols]), turned[x_cols + dt_cols :].astype(F32), pack[:, own].astype(F32)
+        parts = [jnp.pad(turned[lo : lo + size], ((0, r - size), (0, 0))).astype(kind) for (lo, size), r, kind in zip(cuts, rows, kinds)]
+        return [pack[:, own].astype(F32)] + parts
     return pl.pallas_call(
-        functools.partial(unpack_kernel, own, x_cols, dt_cols),
-        out_shape=[jax.ShapeDtypeStruct((128, chans), BF)] * 2 + [jax.ShapeDtypeStruct((cols - x_cols - dt_cols, chans), F32), jax.ShapeDtypeStruct((blocks, cols), F32)],
+        functools.partial(unpack_kernel, own, tuple(cuts)),
+        out_shape=[jax.ShapeDtypeStruct((blocks, cols), F32)] + [jax.ShapeDtypeStruct((r, chans), kind) for r, kind in zip(rows, kinds)],
         scratch_shapes=[pltpu.VMEM((chans, cols), F32)],
         compiler_params=pltpu.CompilerParams(vmem_limit_bytes=VM),
         name="unpack_small",
@@ -962,7 +1010,7 @@
     )(carry, own)
 
 
-def experts_kernel(block, piece, pick_ref, n2_ref, go_ref, router_ref, up_hbm, down_hbm, back_ref, late_ref, mixed_ref, grouter_ref, gexp_hbm,
+def experts_kernel(block, piece, pick_ref, n2_ref, early_ref, go_ref, router_ref, up_hbm, down_hbm, back_ref, late_ref, mixed_ref, grouter_ref, gexp_hbm,
                    up, down, gup, gdown, outbox, inbox, ret, total, disp, load_sem, store_sem, own_sem, out_send, out_recv, back_own, back_send, back_recv):
     dp, z = lax.axis_index("dp"), lax.axis_index("seq")
     count = lax.axis_size("seq")
@@ -984,14 +1032,14 @@
             made.append(pltpu.make_async_copy(gdown.at[at], gexp_hbm.at[to, 1], store_sem.at[to, 1]))
         return made
 
-    def send(half, j):
-        return pltpu.make_async_remote_copy(outbox.at[half, peers[j]], inbox.at[half, z], out_send.at[half, j], out_recv.at[half, j], device_id=(dp, peers[j]), device_id_type=MESH)
-
-    def came(half, j):
-        return pltpu.make_async_remote_copy(outbox.at[half, z], inbox.at[half, lax.rem(z + count - 1 - j, count)], out_send.at[half, j], out_recv.at[half, j], device_id=(dp, z), device_id_type=MESH)
-
-    def kept(half):
-        return pltpu.make_async_copy(outbox.at[half, z], inbox.at[half, z], own_sem.at[half])
+    def send(j):
+        return pltpu.make_async_remote_copy(outbox.at[peers[j]], inbox.at[z], out_send.at[j], out_recv.at[j], device_id=(dp, peers[j]), device_id_type=MESH)
+
+    def came(j):
+        return pltpu.make_async_remote_copy(outbox.at[z], inbox.at[lax.rem(z + count - 1 - j, count)], out_send.at[j], out_recv.at[j], device_id=(dp, z), device_id_type=MESH)
+
+    def kept():
+        return pltpu.make_async_copy(outbox.at[z], inbox.at[z], own_sem.at[0])
 
     def give(half, j):
         return pltpu.make_async_remote_copy(ret.at[half, peers[j]], back_ref.at[z], back_send.at[half, j], back_recv.at[half, j], device_id=(dp, peers[j]), device_id_type=MESH)
@@ -1003,22 +1051,22 @@
         return pltpu.make_async_copy(ret.at[half, z], back_ref.at[z], back_own.at[half])
 
     greet([(dp, peer) for peer in peers])
-    for half in range(2):
-        picked = lax.dot_general(pick_ref[:, half * rows : (half + 1) * rows], n2_ref[...], TN, preferred_element_type=F32)
-        outbox[half] = picked.astype(BF).reshape(count, each, width)
-        for j in range(count - 1):
-            send(half, j).start()
-        kept(half).start()
+    picked = lax.dot_general(pick_ref[...], n2_ref[...], TN, preferred_element_type=F32)
+    outbox[...] = picked.astype(BF).reshape(count, each, width)
+    for j in range(count - 1):
+        send(j).start()
+    kept().start()
     for b in range(blocks):
         for copy in loads(b):
             copy.start()
     lanes = lax.broadcasted_iota(jnp.int32, (rows, router_ref.shape[1]), 1)
     mine = (lanes == z).astype(F32)
     for half in range(2):
-        kept(half).wait()
-        for j in range(count - 1):
-            came(half, j).wait_recv()
-        slots = inbox[half].reshape(rows, width)
+        if half:
+            kept().wait()
+            for j in range(count - 1):
+                came(j).wait_recv()
+        slots = (inbox if half else early_ref)[...].reshape(rows, width)
         go = go_ref[:, half * each : (half + 1) * each, :].reshape(rows, width).astype(F32)
         logits = jnp.where(lanes < count, jnp.dot(slots, router_ref[...], preferred_element_type=F32), -1e30)
         powers = jnp.exp(logits - jnp.max(logits, axis=1, keepdims=True))
@@ -1075,13 +1123,12 @@
             copy.wait()
     give_own(0).wait()
     for j in range(count - 1):
-        send(0, j).wait_send()
-        send(1, j).wait_send()
+        send(j).wait_send()
         give(0, j).wait_send()
         got(0, j).wait_recv()
 
 
-def experts_pass(pick, n2, go, router, up, down, block, piece, collective_id):
+def experts_pass(pick, n2, early, go, router, up, down, block, piece, collective_id):
     count, slots, width = go.shape
     units = up.shape[0]
     rows = count * slots // 2
@@ -1091,17 +1138,17 @@
     blocks = units // block
     return pl.pallas_call(
         functools.partial(experts_kernel, block, piece),
-        in_specs=[vmem] * 4 + [hbm] * 2,
+        in_specs=[vmem] * 5 + [hbm] * 2,
         out_specs=[hbm, vmem, vmem, vmem, hbm],
         out_shape=[jax.ShapeDtypeStruct((count, slots // 2, width), BF)] * 2 + [jax.ShapeDtypeStruct((count, slots, width), BF), jax.ShapeDtypeStruct(router.shape, F32),
                    jax.ShapeDtypeStruct((units // piece, 2, piece, width), BF)],
         scratch_shapes=[pltpu.VMEM(up.shape, BF)] * 4
-        + [pltpu.VMEM((2, count, slots // 2, width), BF)] * 2 + [pltpu.VMEM((1, count, slots // 2, width), BF)] + [pltpu.VMEM((rows, width), F32)] * 2
-        + [sems(blocks, 2), sems(units // piece, 2), sems(2), sems(2, count - 1), sems(2, count - 1), sems(1), sems(1, count - 1), sems(1, count - 1)],
+        + [pltpu.VMEM((count, slots // 2, width), BF)] * 2 + [pltpu.VMEM((1, count, slots // 2, width), BF)] + [pltpu.VMEM((rows, width), F32)] * 2
+        + [sems(blocks, 2), sems(units // piece, 2), sems(1), sems(count - 1), sems(count - 1), sems(1), sems(1, count - 1), sems(1, count - 1)],
         compiler_params=pltpu.CompilerParams(collective_id=collective_id, has_side_effects=True, vmem_limit_bytes=VM),
         cost_estimate=pl.CostEstimate(flops=24 * rows * units * width, bytes_accessed=100_000_000, transcendentals=4 * rows * units),
         name="experts",
-    )(pick, n2, go, router, up, down)
+    )(pick, n2, early, go, router, up, down)
 
 
 def dot(a, b):
@@ -1158,6 +1205,7 @@
     share = small_params.shape[0]
     packed = pack_params(w_x, w_dt, a_log.T, conv_w.T, conv_b[None], dt_bias[None], d_skip[None], small_params[None])
     direct = lax.axis_size("dp") == 8 and lax.axis_size("seq") == 4
+    ring = [[r ^ (r >> 1) for r in range(8)]] if direct else None
     up_t = jnp.swapaxes(w_up, 1, 2)
     full_out = lax.all_gather(w_out, both, axis=0, tiled=True)
     if direct:
@@ -1172,10 +1220,9 @@
         rim_tok = shift(tok_b[rows - halo :], "seq", 1)
         rim_ids = shift(seg_plus[rows - halo :], "seq", 1)
     full_in = lax.optimization_barrier(all_in.reshape(2 * chans, width))
-    full_x_t, full_dt_t, high_t, small = unpack(all_pack.reshape(devices, -1, 256), own, w_x.shape[1], rank)
+    small, full_x_t, full_dt_t, alog_t, conv_f, bias_row, dtb_row, skip = unpack(all_pack.reshape(devices, -1, 256), own, (w_x.shape[1], rank, n, taps, 1, 1, 1))
     small, part_up = lax.optimization_barrier((small, part_up))
-    full_up = lax.all_gather(part_up, "dp", axis=0).reshape(-1, width)
-    alog_t, conv_f, bias_row, dtb_row, skip = high_t[:n], high_t[n : n + taps], high_t[n + taps : n + taps + 1], high_t[n + taps + 1 : n + taps + 2], high_t[n + taps + 2 : n + taps + 3]
+    full_up = lax.all_gather(part_up, "dp", axis=0, axis_index_groups=ring).reshape(-1, width)
     flat_small = small[:, :share].reshape(-1)
     gain_one = flat_small[:width]
     gain_two = flat_small[width : 2 * width]
@@ -1191,54 +1238,45 @@
     pick = (pick_of[:, None] == jnp.arange(experts * slots)[None, :]).astype(BF)
     grad_out_b = cotangent[0]
     grad_out = grad_out_b.astype(F32)
-    tok_ext = jnp.concatenate([rim_tok, tok_b]).astype(F32)
     tok_f = tok_b.astype(F32)
     ids_ext = jnp.concatenate([rim_ids, seg_plus])
     same = jnp.stack([ids_ext[halo - taps + 1 + k : halo - taps + 1 + k + rows] == seg_plus for k in range(taps)], axis=1).astype(F32)
-    keep = same[:, taps - 2 : taps - 1]
-    normed_ext = (tok_ext * rms_scale(tok_ext) * gain_one).astype(BF)
-    normed = normed_ext[halo:]
-    conv_in, conv_sum, values, z, projected = front(normed_ext, normed, full_in, full_x_t, conv_f, bias_row, same, halo, wide)
-    low_wide, b_wide, c_wide, b_blk, c_blk, pre_dt, dt, dt_keep, dtx, rates, rates2, own_state, carry = steps(projected, keep, values, full_dt_t, dtb_row, alog_t, rank, wide)
+    normed, conv_in, conv_sum, values, z, projected = front(rim_tok, tok_b, gain_one[None], full_in, full_x_t, conv_f, bias_row, same, wide)
+    low_wide, b_wide, c_wide, b_blk, c_blk, pre_dt, dt, dt_keep, dtx, rates, rates2, own_state, carry = steps(projected, same, values, full_dt_t, dtb_row, alog_t, rank, wide)
     carry, part_down = lax.optimization_barrier((carry, part_down))
-    full_down = lax.all_gather(part_down, "dp", axis=0).reshape(-1, width)
+    full_down = lax.all_gather(part_down, "dp", axis=0, axis_index_groups=ring).reshape(-1, width)
     start = chain(carry, own_state, 1, 3)
     go_local, start = lax.optimization_barrier((dot_tn(gather_mat, grad_out_b).astype(BF), start))
     go_slots = swap(go_local.reshape(experts, slots, width))
-    scanned, checks, gated, first_sum, normed_two = scan_pass(
-        dt_keep, dtx, rates2, b_wide, c_blk, start, values, z, skip, full_out, tok_b, gain_two[None], wide
+    scanned, checks, gated, first_sum, normed_two, sent = scan_pass(
+        dt_keep, dtx, rates2, b_wide, c_blk, start, values, z, skip, full_out, tok_b, gain_two[None], pick[:, : experts * half], wide
     )
-    normed_two, go_slots = lax.optimization_barrier((normed_two, go_slots))
-    sig_z = jax.nn.sigmoid(z)
+    sent, go_slots = lax.optimization_barrier((sent, go_slots))
+    early = swap(sent.reshape(experts, half, width))
 
     piece = w_up.shape[2]
     router_wide = jnp.pad(router, ((0, 0), (0, 128 - experts)))
-    back_n2, late_n2, mixed_back, grad_router, grad_exp = experts_pass(pick, normed_two, go_slots, router_wide, full_up, full_down, 768, piece if piece % 16 == 0 else 768, 5)
+    back_n2, late_n2, mixed_back, grad_router, grad_exp = experts_pass(pick[:, experts * half :], normed_two, early, go_slots, router_wide, full_up, full_down, 768, piece if piece % 16 == 0 else 768, 5)
     grad_router = grad_router[:, :experts]
     late_n2 = swap(late_n2)
     grad_n2 = dot(pick, jnp.concatenate([back_n2.reshape(-1, width), late_n2.reshape(-1, width)]))
     mixed_slots = swap(mixed_back).reshape(-1, width)
     if piece % 16:
         grad_exp = jnp.swapaxes(jnp.swapaxes(grad_exp, 0, 1).reshape(2, -1, piece, width), 0, 1)
-    part_exp = lax.psum_scatter(grad_exp.reshape(-1, width), "dp", scatter_dimension=0, tiled=True)
+    part_exp = lax.psum_scatter(grad_exp.reshape(-1, width), "dp", scatter_dimension=0, tiled=True, axis_index_groups=ring)
 
     grad_norm_two, grad_gain_two = rms_back(first_sum, gain_two, grad_n2)
     grad_first = grad_out + grad_norm_two
     grad_mixer = grad_first.astype(BF)
-    grad_w_out = dot_tn(gated, grad_mixer).astype(BF)
-    grad_gated = dot_nt(grad_mixer, full_out)
-    silu_z = z * sig_z
-    grad_scanned = grad_gated * silu_z
-    grad_z = grad_gated * (scanned + skip * values) * (sig_z * (1.0 + z * (1.0 - sig_z)))
-    grad_z_b = grad_z.astype(BF)
-    grad_start = back_state_pass(dt_keep, grad_scanned, rates2, c_wide, wide)
+    grad_scanned, grad_z_b, grad_w_out, grad_start = back_front(grad_mixer, full_out, z, scanned, values, skip, gated, dt_keep, rates2, c_wide, chans // 2, ring[0] if direct else None)
     nxt = chain(carry, grad_start, -1, 4)
-    nxt, grad_w_out = lax.optimization_barrier((nxt, grad_w_out))
     grad_vals, g_log, grad_dt_t, grad_dtb, grad_skip, grad_proj = back_pass(
         dt, dt_keep, dtx, grad_scanned, values, pre_dt, skip, rates2, rates, b_wide, c_wide, b_blk, checks, nxt, low_wide, full_dt_t, rank, wide
     )
     grad_vals, mixed_slots, part_exp, grad_w_out = lax.optimization_barrier((grad_vals, mixed_slots, part_exp, grad_w_out))
-    sum_exp = swap(part_exp.reshape(experts, 2, piece, width))
+    part_exp = part_exp.reshape(experts, 2, piece, width)
+    part_down = part_exp[:, 1]
+    sum_up = swap(part_exp[:, 0])
     mixed_out = (first_sum + dot(gather_mat, mixed_slots)).astype(BF)
     grad_conv_b, grad_last, grad_rim, grad_x_t, grad_taps = conv_back(grad_vals, grad_proj, full_x_t, values, conv_sum, conv_in, same, conv_f, halo, wide)
     grad_last = (grad_last + shift(grad_rim, "seq", -1)).astype(BF)
@@ -1252,22 +1290,22 @@
     grad_packed = pack_grads(
         (grad_x_t, grad_dt_t, g_log, grad_taps, grad_dtb, grad_skip), (w_x.shape[1], rank, n, taps + 1, 1, 1), jnp.pad(grad_small.reshape(devices, -1), ((0, 0), (0, 256 - share))), own
     )
-    part_out = lax.psum_scatter(grad_w_out, "dp", scatter_dimension=0, tiled=True).reshape(-1, own, width)
+    part_out = lax.psum_scatter(grad_w_out, "dp", scatter_dimension=0, tiled=True, axis_index_groups=ring).reshape(-1, own, width)
     part_out = jnp.pad(part_out, ((0, 0), (0, -own % 16), (0, 0)))
     if direct:
-        grad_packed, sum_exp = lax.optimization_barrier((grad_packed, sum_exp))
-        sum_in, sum_pack, all_out = scatter_all(
-            grad_w_in.reshape(4, 2, 4, 2 * own, width), grad_packed.reshape((4, 2, 4) + grad_packed.shape[1:]), part_out, 80, 2
+        grad_packed, sum_up = lax.optimization_barrier((grad_packed, sum_up))
+        sum_in, sum_pack, all_out, sum_down = scatter_all(
+            grad_w_in.reshape(4, 2, 4, 2 * own, width), grad_packed.reshape((4, 2, 4) + grad_packed.shape[1:]), part_out, part_down, 80, 2
         )
     else:
         sum_in = lax.psum_scatter(grad_w_in, both, scatter_dimension=0, tiled=True).astype(F32)
         sum_pack = lax.psum_scatter(grad_packed, both, scatter_dimension=0, tiled=True)[0].astype(F32)
-        all_out = swap(part_out)
+        all_out, sum_down = swap(part_out), swap(part_down)
     cuts, at = [], 0
     for size, turn in ((w_x.shape[1], False), (rank, False), (n, True), (taps, True), (1, True), (1, True), (1, True)):
         cuts.append((at, size, turn))
         at += size
-    up_out, down_out, s_row, sum_out, s_x, s_dt, s_log, s_conv, s_bias, s_dtb, s_skip = finish(sum_pack, sum_exp[:, 0], sum_exp[:, 1], all_out, own, tuple(cuts))
+    up_out, down_out, s_row, sum_out, s_x, s_dt, s_log, s_conv, s_bias, s_dtb, s_skip = finish(sum_pack, sum_up, sum_down, all_out, own, tuple(cuts))
     return (
         mixed_out[None],
         tokens_grad[None],

time: 524 us -> 490 us (0.935)
  waiting for transfers between devices: 38.9 us -> 11 us
  blocking collectives: 0 us -> 16.4 us
  matrix products: 34 us -> 22.7 us
  local copies, waits for them, and re-layouts: 26 us -> 18.4 us
    pallas_call x1, Pallas kernels: 57.4 us -> 39.1 us  [experts_pass(): pl.pallas_call(functools.partial(experts_kernel, block, piece), in_specs=...]
    all_to_all x0 -> x1, blocking collectives: none -> 16.4 us  [swap(): return lax.all_to_all(value, 'seq', 0, 0)]
    all_to_all x5, waiting for transfers between devices: 26.3 us -> 10.2 us  [swap(): return lax.all_to_all(value, 'seq', 0, 0)]
    all_gather x2, waiting for transfers between devices: 11.8 us -> 0.01 us  [the longest x1 0.01 us: shards(): lax.all_gather(part_up, 'dp', axis=0, axis_index_groups=ring)]
    pallas_call x1, Pallas kernels: 67.8 us -> 77.7 us  [scatter_all(): pl.pallas_call(functools.partial(scatter_kernel, parts, count), in_specs=...]
    pallas_call x3, Pallas kernels: 24.6 us -> 33.1 us  [the longest x1 18.1 us: back_front(): pl.pallas_call(functools.partial(back_front_kernel, n, order, chans // wi...]
    dot_general x1 -> x0, matrix products: 6.27 us -> none  [dot_nt(): return lax.dot_general(a, b, NT, preferred_element_type=F32)]
    dot_general x3 -> x2, matrix products: 12.6 us -> 8.43 us  [dot_tn(): return lax.dot_general(a, b, TN, preferred_element_type=F32)]
  transfers between devices with their start and end apart: 11 -> 11, of which waited for: 3 -> 1; matrix products, arithmetic and copies ran while one was open for 11% -> 7% of each run, Pallas kernels for 45% -> 50%
where the time goes in v4:
time: 490 us; the launch traced here: 486 us
  Pallas kernels  363 us (74%)
  starting transfers between devices  34.1 us (7%)
  matrix products  22.7 us (5%)
  local copies, waits for them, and re-layouts  18.4 us (4%)
  blocking collectives  16.4 us (3%)
  between operations  14.5 us (3%)
  waiting for transfers between devices  11 us (2%)
  other arithmetic  5.17 us (1%)
    pallas_call x1, Pallas kernels, gather_all(): pl.pallas_call(functools.partial(gather_kernel, parts, count), in_specs=[...  84.4 us
    pallas_call x1, Pallas kernels, scatter_all(): pl.pallas_call(functools.partial(scatter_kernel, parts, count), in_specs=...  77.7 us
    pallas_call x1, Pallas kernels, back_pass(): pl.pallas_call(functools.partial(back_kernel, n, rank_cols), grid=(chans...  51.4 us
    pallas_call x1, Pallas kernels, experts_pass(): pl.pallas_call(functools.partial(experts_kernel, block, piece), in_specs=...  39.1 us
    all_to_all x5, starting transfers between devices, swap(): return lax.all_to_all(value, 'seq', 0, 0)  29.6 us
    pallas_call x1, Pallas kernels, scan_pass(): pl.pallas_call(functools.partial(scan_kernel, n), grid=(chans // wide,),...  25.4 us
    pallas_call x1, Pallas kernels, steps(): pl.pallas_call(functools.partial(steps_kernel, n, rank_cols), grid=(chans...  18.4 us
    pallas_call x1, Pallas kernels, back_front(): pl.pallas_call(functools.partial(back_front_kernel, n, order, chans // wi...  18.1 us
  transfers between devices with their start and end apart: 11, of which 1 were waited for; matrix products, arithmetic and copies ran while one was open for 7% of the time, Pallas kernels for 50%

profile of v4, /device:TPU:9, one launch (start us, length us, event | category | flops | bytes accessed | tf_op | source)
XLA Modules:
  0.0 485.7 jit_solution(3650017242467427428)
XLA Ops:
  8.0 1.2 broadcast_in_dim.25.small_ref
  9.2 1.6 pack_params.1.rest_ref
  12.2 84.4 %gather_all.1 = (bf16[4,2,4,144,1152]{4,3,2,1,0:T(8,128)(2,1)}, bf16[4,2,4,80,256]{4,3,2,1,0:T(8,128)(2,1)}, bf16[4,96,1152]{2,1,0:T(8,128)(2,1)}, bf16[16,1152]{1,0:T(8,128)(2,1)}, s32[16,128]{1,0:T(8,128)}) custom-call(bf16[144,1152]{1,0:T(8,128)(2,1)} %in_ref.1, bf16[80,256]{1,0:T(8,128)(2,1)} %pack_params.1.rest_ref, bf16[4,96,1152]{2,1,0:T(8,128)(2,1)} %bitcast.72, ...), custom_call_target="tpu_custom_call" | custom-call | bytes 200000000 | tf_op jit(solution)/shard_map/gather_all/pallas_call | solution.py:654
  96.6 2.8 unpack_small.1
  99.4 8.0 %all-to-all-start = ((bf16[4,96,1152]{2,1,0:T(8,128)(2,1)}), bf16[4,96,1152]{2,1,0:T(8,128)(2,1)S(1)}, u32[]{:S(2)}, u32[]{:S(2)}) async-start(bf16[4,96,1152]{2,1,0:T(8,128)(2,1)} %param.31), calls=%async_computation | async-start | bytes 1769472 | tf_op jit(solution)/shard_map/all_to_all | solution.py:1184
  110.0 12.3 %front.1 = (bf16[256,1152]{1,0:T(8,128)(2,1)}, f32[272,2304]{1,0:T(8,128)}, f32[256,2304]{1,0:T(8,128)}, f32[256,2304]{1,0:T(8,128)}, f32[256,2304]{1,0:T(8,128)}, /*index=5*/f32[256,128]{1,0:T(8,128)}) custom-call(bf16[16,1152]{1,0:T(8,128)(2,1)} %get-tuple-element.103.rim_ref, bf16[256,1152]{1,0:T(8,128)(2,1)} %bitcast.65, ...), custom_call_target="tpu_custom_call" | custom-call | flops 2717908992 | bytes 20054016 | tf_op jit(solution)/shard_map/front/pallas_call | solution.py:86
  122.3 18.4 %steps.1 = (bf16[256,128]{1,0:T(8,128)(2,1)}, f32[4096,128]{1,0:T(8,128)}, f32[4096,128]{1,0:T(8,128)}, bf16[256,256]{1,0:T(8,128)(2,1)}, bf16[256,256]{1,0:T(8,...) custom-call(f32[256,128]{1,0:T(8,128)} %get-tuple-element.114.proj_r, ...), custom_call_target="tpu_custom_call" | custom-call | flops 94371840 | bytes 14155776 | tf_op jit(solution)/shard_map/steps/pallas_call | solution.py:148
  142.0 1.7 convolution_convert_fusion.1
  143.7 5.9 %chain.2.start_ref = f32[16,2304]{1,0:T(8,128)} custom-call(f32[16,2304]{1,0:T(8,128)} %get-tuple-element.126.carry_ref, f32[16,2304]{1,0:T(8,128)} %get-tuple-element.127.own_ref), custom_call_target="tpu_custom_call" | custom-call | tf_op jit(solution)/shard_map/chain/pallas_call | solution.py:1002
  149.6 6.6 %all-to-all-start.1 = ((bf16[4,128,1152]{2,1,0:T(8,128)(2,1)}), bf16[4,128,1152]{2,1,0:T(8,128)(2,1)S(1)}, u32[]{:S(2)}, u32[]{:S(2)}) async-start(bf16[4,128,1152]{2,1,0:T(8,128)(2,1)} %bitcast.13), calls=%async_computation.1 | async-start | bytes 2359296 | tf_op jit(solution)/shard_map/all_to_all | solution.py:1184
  157.6 25.4 %scan_pass.1 = (f32[256,2304]{1,0:T(8,128)}, f32[256,2304]{1,0:T(8,128)}, bf16[256,2304]{1,0:T(8,128)(2,1)}, f32[256,1152]{1,0:T(8,128)}, bf16[256,1152]{1,0:T(8,128)(2,1)}, /*index=5*/bf16[256,1152]{1,0:T(8,128)(2,1)}) custom-call(f32[256,2304]{1,0:T(8,128)} %get-tuple-element.119.dte_ref, f32[256,2304]{1,0:T(8,128)} %get-tuple-element.120.dtx_ref, ...), custom_call_target="tpu_custom_call" | custom-call | flops 94371840 | bytes 7077888 | tf_op jit(solution)/shard_map/scan_pass/pallas_call | solution.py:209
  183.1 4.5 all-to-all-start.2
  188.9 10.2 %all-to-all-done.2.early_ref = bf16[4,64,1152]{2,1,0:T(8,128)(2,1)S(1)} async-done(((bf16[4,64,1152]{2,1,0:T(8,128)(2,1)}), bf16[4,64,1152]{2,1,0:T(8,128)(2,1)S(1)}, u32[]{:S(2)}, u32[]{:S(2)}) %all-to-all-start.2) | async-done | bytes 589856 | tf_op jit(solution)/shard_map/all_to_all | solution.py:1184
  200.0 39.1 %experts.1 = (bf16[4,64,1152]{2,1,0:T(8,128)(2,1)}, bf16[4,64,1152]{2,1,0:T(8,128)(2,1)}, bf16[4,128,1152]{2,1,0:T(8,128)(2,1)}, f32[1152,128]{1,0:T(8,128)}, bf16[32,2,96,1152]{3,2,1,0:T(8,128)(2,1)}) custom-call(bf16[256,256]{1,0:T(8,128)(2,1)} %get-tuple-element.200.pick_ref, bf16[256,1152]{1,0:T(8,128)(2,1)} %get-tuple-element.133.n2_ref, ...), custom_call_target="tpu_custom_call" | custom-call | flops 21743271936 | bytes 100000000 | tf_op jit(solution)/shard_map/experts/pallas_call | solution.py:1139
  240.1 16.4 %all_to_all.30 = bf16[4,64,1152]{2,1,0:T(8,128)(2,1)S(1)} all-to-all(bf16[4,64,1152]{2,1,0:T(8,128)(2,1)S(1)} %copy-done.12), channel_id=1, replica_groups=mesh['dp'=8,'seq'=4] {'seq'}, dimensions={0} | all-to-all | bytes 1179648 | tf_op jit(solution)/shard_map/all_to_all | solution.py:1184
  256.5 6.0 %all-to-all-start.4 = ((bf16[4,128,1152]{2,1,0:T(8,128)(2,1)}), bf16[4,128,1152]{2,1,0:T(8,128)(2,1)}, u32[]{:S(2)}, u32[]{:S(2)}) async-start(bf16[4,128,1152]{2,1,0:T(8,128)(2,1)} %get-tuple-element.153), calls=%async_computation.4 | async-start | bytes 2359296 | tf_op jit(solution)/shard_map/all_to_all | solution.py:1184
  263.6 1.3 multiply_reduce_fusion
  266.1 18.1 %back_front.1 = (f32[256,2304]{1,0:T(8,128)}, bf16[256,2304]{1,0:T(8,128)(2,1)}, bf16[2304,1152]{1,0:T(8,128)(2,1)}, f32[16,2304]{1,0:T(8,128)}) custom-call(bf16[256,1152]{1,0:T(8,128)(2,1)} %get-tuple-element.196.grad_ref, bf16[2304,1152]{1,0:T(8,128)(2,1)} %all-gather.6.cloned.1.call-done.out_ref, f32[256,2304]{1,0:T(8,128)} %get-tuple-element.129.z_ref, ...), custom_call_target="tpu_custom_call" | custom-call | flops 75497472 | bytes 4718592 | tf_op jit(solution)/shard_map/back_front/pallas_call | solution.py:275
  284.1 9.1 %chain.3.next_ref = f32[16,2304]{1,0:T(8,128)} custom-call(f32[16,2304]{1,0:T(8,128)} %get-tuple-element.126.carry_ref, f32[16,2304]{1,0:T(8,128)} %get-tuple-element.150.own_ref), custom_call_target="tpu_custom_call" | custom-call | tf_op jit(solution)/shard_map/chain/pallas_call | solution.py:1002
  293.3 51.4 %back_pass.1 = (f32[256,2304]{1,0:T(8,128)}, f32[16,2304]{1,0:T(8,128)}, f32[128,2304]{1,0:T(8,128)}, f32[1,2304]{1,0:T(1,128)}, f32[1,2304]{1,0:T(1,128)}, /*index=5*/bf16[256,128]{1,0:T(8,128)(2,1)}) custom-call(f32[256,2304]{1,0:T(8,128)} %get-tuple-element.132.dt_ref, f32[256,2304]{1,0:T(8,128)} %get-tuple-element.119.dte_ref, ...), custom_call_target="tpu_custom_call" | custom-call | flops 245366784 | bytes 14155776 | tf_op jit(solution)/shard_map/back_pass/pallas_call | solution.py:375
  347.4 5.6 %fusion = f32[256,1152]{1,0:T(8,128)} fusion(bf16[256,2304]{1,0:T(8,128)(2,1)} %get-tuple-element.164, bf16[4608,1152]{1,0:T(8,128)(2,1)} %bitcast.62), kind=kOutput, calls=%fused_computation.1 | convolution fusion | flops 1358954496 | bytes 7667712 | tf_op jit(solution)/shard_map/dot_general | solution.py:1155
  353.0 9.5 %conv_back.1 = (bf16[256,2304]{1,0:T(8,128)(2,1)}, f32[8,2304]{1,0:T(8,128)}, f32[8,2304]{1,0:T(8,128)}, f32[128,2304]{1,0:T(8,128)}, f32[8,2304]{1,0:T(8,128)}) custom-call(f32[256,2304]{1,0:T(8,128)} %get-tuple-element.157.gval_ref, bf16[256,128]{1,0:T(8,128)(2,1)} %get-tuple-element.158.proj_ref, bf16[128,2304]{1,0:T(8,128)(2,1)} %get-tuple-element.110.xt_ref, ...), custom_call_target="tpu_custom_call" | custom-call | flops 35389440 | bytes 11796480 | tf_op jit(solution)/shard_map/conv_back/pallas_call | solution.py:430
  362.5 3.6 collective-permute-start
  366.1 1.3 slice_bitcast_fusion
  367.4 4.5 all-to-all-start.5
  371.9 2.8 fusion.8
  376.4 4.5 fusion.21
  381.7 3.1 pack_small.1
  386.8 6.7 %convolution_convert_fusion = bf16[4608,1152]{1,0:T(8,128)(2,1)} fusion(bf16[256,1152]{1,0:T(8,128)(2,1)S(1)} %copy-done.21, bf16[256,2304]{1,0:T(8,128)(2,1)S(1)} %copy-done.20, bf16[8,2304]{1,0:T(8,128)(2,1)S(1)} %add_convert_fusion, bf16[248,2304]{1,0:T(8,128)(2,1)S(1)} %copy-done.7), kind=kOutput, calls=%fused_computation | convolution fusion | flops 2730295296 | bytes 13565952 | tf_op jit(solution)/shard_map/dot_general | solution.py:1163
  393.5 2.0 pad.14.proj_ref
  395.5 77.7 %scatter_all.1 = (f32[144,1152]{1,0:T(8,128)}, f32[80,256]{1,0:T(8,128)}, bf16[4,80,1152]{2,1,0:T(8,128)(2,1)}, bf16[4,96,1152]{2,1,0:T(8,128)(2,1)}) custom-call(bf16[4,2,4,144,1152]{4,3,2,1,0:T(8,128)(2,1)} %bitcast.68, bf16[4,2,4,80,256]{4,3,2,1,0:T(8,128)(2,1)} %bitcast.69, bf16[4,80,1152]{2,1,0:T(8,128)(2,1)} %pad.14.proj_ref, ...), custom_call_target="tpu_custom_call" | custom-call | bytes 200000000 | tf_op jit(solution)/shard_map/scatter_all/pallas_call | solution.py:806
  473.2 4.8 finish.1
  (108 shorter events, 21.0 us)
Async XLA Ops:
  7.2 150.5 %all-gather.6.cloned.1.call-start = ((), (), s32[]{:S(2)}) async-start(), calls=%async_computation.8 | async-start | bytes 5474304 | tf_op jit(solution)/shard_map/all_gather | solution.py:1210
  7.9 191.2 %all-gather.8.cloned.1.call-start = ((), (), s32[]{:S(2)}) async-start(), calls=%async_computation.11 | async-start | bytes 7962624 | tf_op jit(solution)/shard_map/all_gather | solution.py:1225
  99.4 8.6 %copy-start.16 = (s32[16,128]{1,0:T(8,128)S(1)}, s32[16,128]{1,0:T(8,128)}, u32[]{:S(2)}) copy-start(s32[16,128]{1,0:T(8,128)} %get-tuple-element.113) | copy-start | bytes 24580
  99.4 9.9 %copy-start.14 = (f32[32,256]{1,0:T(8,128)S(1)}, f32[32,256]{1,0:T(8,128)}, u32[]{:S(2)}) copy-start(f32[32,256]{1,0:T(8,128)} %get-tuple-element.107) | copy-start | bytes 98308
  99.4 41.3 %all-to-all-start = ((bf16[4,96,1152]{2,1,0:T(8,128)(2,1)}), bf16[4,96,1152]{2,1,0:T(8,128)(2,1)S(1)}, u32[]{:S(2)}, u32[]{:S(2)}) async-start(bf16[4,96,1152]{2,1,0:T(8,128)(2,1)} %param.31), calls=%async_computation | async-start | bytes 1769472 | tf_op jit(solution)/shard_map/all_to_all | solution.py:1184
  107.4 91.7 %all-gather.10.cloned.1.call-start = ((), (), s32[]{:S(2)}) async-start(), calls=%async_computation.12 | async-start | bytes 7962624 | tf_op jit(solution)/shard_map/all_gather | solution.py:1247
  122.3 19.3 %copy-start.19 = (s32[1,256,1]{1,2,0:T(1,128)S(1)}, s32[1,256,1]{1,2,0:T(1,128)}, u32[]{:S(2)}) copy-start(s32[1,256,1]{1,2,0:T(1,128)} %param.18) | copy-start | bytes 3076
  140.6 1.4 copy-start.3
  140.7 0.9 copy-start.2
  149.6 33.4 %all-to-all-start.1 = ((bf16[4,128,1152]{2,1,0:T(8,128)(2,1)}), bf16[4,128,1152]{2,1,0:T(8,128)(2,1)S(1)}, u32[]{:S(2)}, u32[]{:S(2)}) async-start(bf16[4,128,1152]{2,1,0:T(8,128)(2,1)} %bitcast.13), calls=%async_computation.1 | async-start | bytes 2359296 | tf_op jit(solution)/shard_map/all_to_all | solution.py:1184
  183.1 5.9 %copy-start.5 = (bf16[4,128,1152]{2,1,0:T(8,128)(2,1)}, bf16[4,128,1152]{2,1,0:T(8,128)(2,1)S(1)}, u32[]{:S(2)}) copy-start(bf16[4,128,1152]{2,1,0:T(8,128)(2,1)S(1)} %all-to-all-done.1.go_ref) | copy-start | bytes 3538948
  183.1 16.1 %all-to-all-start.2 = ((bf16[4,64,1152]{2,1,0:T(8,128)(2,1)}), bf16[4,64,1152]{2,1,0:T(8,128)(2,1)S(1)}, u32[]{:S(2)}, u32[]{:S(2)}) async-start(bf16[4,64,1152]{2,1,0:T(8,128)(2,1)} %bitcast.75), calls=%async_computation.2 | async-start | bytes 1179648 | tf_op jit(solution)/shard_map/all_to_all | solution.py:1184
  187.6 157.1 %reduce-scatter.3.cloned.1.call-start = ((), (), s32[]{:S(2)}) async-start(), calls=%async_computation.9 | async-start | bytes 15925248 | tf_op jit(solution)/shard_map/reduce_scatter | solution.py:1266
  239.0 1.1 copy-start.12
  256.5 6.2 %copy-start.1 = (f32[256,1152]{1,0:T(8,128)S(1)}, f32[256,1152]{1,0:T(8,128)}, u32[]{:S(2)}) copy-start(f32[256,1152]{1,0:T(8,128)} %get-tuple-element.131) | copy-start | bytes 3538948
  256.5 88.2 %all-to-all-start.4 = ((bf16[4,128,1152]{2,1,0:T(8,128)(2,1)}), bf16[4,128,1152]{2,1,0:T(8,128)(2,1)}, u32[]{:S(2)}, u32[]{:S(2)}) async-start(bf16[4,128,1152]{2,1,0:T(8,128)(2,1)} %get-tuple-element.153), calls=%async_computation.4 | async-start | bytes 2359296 | tf_op jit(solution)/shard_map/all_to_all | solution.py:1184
  262.5 1.1 copy-start.22
  262.5 131.0 %reduce-scatter.5.cloned.1.call-start = ((), (), s32[]{:S(2)}) async-start(), calls=%async_computation.10 | async-start | bytes 5971968 | tf_op jit(solution)/shard_map/reduce_scatter | solution.py:1293
  344.7 1.1 copy-start
  344.7 1.8 copy-start.10
  353.0 13.1 %copy-start.4 = (bf16[768,1152]{1,0:T(8,128)(2,1)S(1)}, bf16[768,1152]{1,0:T(8,128)(2,1)}, u32[]{:S(2)}) copy-start(bf16[768,1152]{1,0:T(8,128)(2,1)} %reduce-scatter.3.cloned.1.call-done) | copy-start | bytes 5308420
  362.5 12.3 %collective-permute-start = (f32[8,2304]{1,0:T(8,128)}, f32[8,2304]{1,0:T(8,128)S(1)}, u32[]{:S(2)}, u32[]{:S(2)}) collective-permute-start(f32[8,2304]{1,0:T(8,128)} %get-tuple-element.163), channel_id=1, source_target_pairs={{1,0},{2,1},{3,2},{5,4},{6,5},{7,6},{9,8},{10,9},{11,10},{13,12},{... | collective-permute-start | bytes 221192 | tf_op jit(solution)/shard_map/ppermute | solution.py:1169
  367.4 26.1 %all-to-all-start.5 = ((bf16[4,96,1152]{2,1,0:T(8,128)(2,1)}), bf16[4,96,1152]{2,1,0:T(8,128)(2,1)}, u32[]{:S(2)}, u32[]{:S(2)}) async-start(bf16[4,96,1152]{2,1,0:T(8,128)(2,1)} %get-tuple-element.199), calls=%async_computation.6 | async-start | bytes 1769472 | tf_op jit(solution)/shard_map/all_to_all | solution.py:1184
  371.9 2.8 copy-start.8
  374.7 1.8 copy-start.23
  374.7 6.2 %copy-start.6 = (bf16[248,2304]{1,0:T(8,128)(2,1)}, bf16[248,2304]{1,0:T(8,128)(2,1)S(1)}, u32[]{:S(2)}) copy-start(bf16[248,2304]{1,0:T(8,128)(2,1)S(1)} %slice.74) | copy-start | bytes 3428356
  376.4 4.5 copy-start.13
  376.4 4.5 copy-start.17
  384.8 1.3 copy-start.7
  384.8 1.8 copy-start.20
  384.8 2.0 copy-start.21
  473.2 4.8 copy-start.9
  (3 other events, 2.6 us)
Sparse Core Ops, SparseCore 0:
  10.9 85.8 all-gather.5
  99.5 45.4 all-gather.7
  146.6 42.2 all-gather.9
  239.2 78.5 reduce-scatter.2
  344.8 37.0 reduce-scatter.4

commit v5 on v4

--- a/solution.py
+++ b/solution.py
@@ -18,8 +18,8 @@
 TN = (((0,), (0,)), ((), ()))
 
 
-def rowb(block, i, n):
-    return jnp.broadcast_to(block[i:i+1, :], (n, block.shape[1]))
+def rowr(ref, at, i, c, n):
+    return jnp.broadcast_to(ref.at[pl.ds(at, STEP), c][i : i + 1, :], (n, 128))
 
 def state_kernel(n, dte_ref, dtx_ref, rate_ref, b_ref, state_ref, carry_ref):
     rows, wide = dte_ref.shape
@@ -35,8 +35,8 @@
             bs = b_ref[pl.ds((at + i) * n, n), :]
             for j in range(tiles):
                 c = slice(j*128, (j+1)*128)
-                decay = jnp.exp2(rowb(dte[:, c], i, n) * rates[j])
-                state[j] = decay * state[j] + bs * rowb(dtx[:, c], i, n)
+                decay = jnp.exp2(rowr(dte_ref, at, i, c, n) * rates[j])
+                state[j] = decay * state[j] + bs * rowr(dtx_ref, at, i, c, n)
         return tuple(state), total + dte
     zero = tuple(jnp.zeros((n, 128), F32) for _ in range(tiles))
     state, total = lax.fori_loop(0, rows // STEP, block, (zero, jnp.zeros((STEP, wide), F32)))
@@ -115,11 +115,13 @@
         for i, (wide_ref, blk_ref) in enumerate(((bw_ref, bblk_ref), (cw_ref, cblk_ref))):
             pick = (from_col == to_col + rank_cols + i * n).astype(F32)
             tiled = jnp.where(own, jnp.dot(proj, pick, precision=lax.Precision.HIGHEST, preferred_element_type=F32), 0.0)
-            blk_ref[...] = tiled.astype(BF)
-            ones = jnp.ones((STEP, 128), F32)
+            high = tiled.astype(BF)
+            low = (tiled - high.astype(F32)).astype(BF)
+            blk_ref[...] = high
+            ones = jnp.ones((STEP, 128), BF)
             for k in range(rows // STEP):
-                block = tiled[k * STEP : (k + 1) * STEP, :]
-                wide_ref[k * groups : (k + 1) * groups, :] = lax.dot_general(block, ones, TN, precision=lax.Precision.HIGHEST, preferred_element_type=F32)
+                at = slice(k * STEP, (k + 1) * STEP)
+                wide_ref[k * groups : (k + 1) * groups, :] = lax.dot_general(high[at], ones, TN, preferred_element_type=F32) + lax.dot_general(low[at], ones, TN, preferred_element_type=F32)
 
     pre = jnp.dot(low_ref[...], dtt_ref[...], preferred_element_type=F32) + dtb_ref[...]
     dt = jax.nn.softplus(pre)
@@ -175,8 +177,8 @@
             bs = b_ref[pl.ds((at + i) * n, n), :]
             for j in range(tiles):
                 c = slice(j*128, (j+1)*128)
-                decay = jnp.exp2(rowb(dte[:, c], i, n) * rates[j])
-                state[j] = decay * state[j] + bs * rowb(dtx[:, c], i, n)
+                decay = jnp.exp2(rowr(dte_ref, at, i, c, n) * rates[j])
+                state[j] = decay * state[j] + bs * rowr(dtx_ref, at, i, c, n)
                 hs[i*n:(i+1)*n, c] = state[j].astype(BF)
         y_ref[pl.ds(at, STEP), :] = jnp.dot(cblk_ref[pl.ds(at, STEP), :], hs[...], preferred_element_type=F32)
         return tuple(state)
@@ -233,8 +235,8 @@
             cs = c_ref[pl.ds((at + i) * n, n), :]
             for j in range(tiles):
                 c = slice(j*128, (j+1)*128)
-                decay = jnp.exp2(rowb(dte[:, c], i, n) * rates[j])
-                state[j] = decay * (state[j] + cs * rowb(gs[:, c], i, n))
+                decay = jnp.exp2(rowr(dte_ref, at, i, c, n) * rates[j])
+                state[j] = decay * (state[j] + cs * rowr(gs_ref, at, i, c, n))
         return tuple(state)
     zero = tuple(jnp.zeros((n, 128), F32) for _ in range(tiles))
     state = lax.fori_loop(0, rows // STEP, block, zero)
@@ -310,9 +312,9 @@
             bs = b_ref[pl.ds((at + i) * n, n), :]
             for j in range(tiles):
                 c = slice(j*128, (j+1)*128)
-                decay = jnp.exp2(rowb(dte[:, c], i, n) * rates[j])
+                decay = jnp.exp2(rowr(dte_ref, at, i, c, n) * rates[j])
                 kept = decay * state[j]
-                state[j] = kept + bs * rowb(dtx[:, c], i, n)
+                state[j] = kept + bs * rowr(dtx_ref, at, i, c, n)
                 decs[i*n:(i+1)*n, c] = decay
                 us[i*n:(i+1)*n, c] = kept
                 hs[i*n:(i+1)*n, c] = state[j].astype(BF)
@@ -324,10 +326,10 @@
             cs = c_ref[pl.ds((at + i) * n, n), :]
             for j in range(tiles):
                 c = slice(j*128, (j+1)*128)
-                adj = later[j] + cs * rowb(gs[:, c], i, n)
+                adj = later[j] + cs * rowr(gs_ref, at, i, c, n)
                 part = adj * us[i*n:(i+1)*n, c] * rawrate_ref[:, c]
                 later[j] = adj * decs[i*n:(i+1)*n, c]
-                logs[j] = logs[j] + part * rowb(dt[:, c], i, n)
+                logs[j] = logs[j] + part * rowr(dt_ref, at, i, c, n)
                 ls[i*n:(i+1)*n, c] = adj.astype(BF)
                 ps[i*n:(i+1)*n, c] = part.astype(BF)
         for j in range(tiles):
@@ -387,10 +389,15 @@
     )(dt, dte, dtx, gs, values, pre, skip, rates2, rates, b_wide, c_wide, b_blk, check, nxt, low, wdt)
 
 
-def conv_back_kernel(halo, gval_ref, proj_ref, xt_ref, values_ref, sum_ref, ext_ref, same_ref, taps_ref,
-                     gconv_ref, last_ref, rim_ref, gxt_ref, gtaps_ref, pad):
+def conv_back_kernel(halo, gval_ref, proj_ref, xt_ref, values_ref, sum_ref, ext_ref, same_ref, taps_ref, place_ref, slots_ref, first_ref,
+                     mixed_ref, gconv_ref, last_ref, rim_ref, gxt_ref, gtaps_ref, pad):
     rows, wide = gval_ref.shape
     taps = taps_ref.shape[0]
+
+    @pl.when(pl.program_id(0) == 0)
+    def _():
+        mixed_ref[...] = (first_ref[...] + jnp.dot(place_ref[...], slots_ref[...], preferred_element_type=F32)).astype(BF)
+
     proj = proj_ref[...]
     grad_values = gval_ref[...] + jnp.dot(proj, xt_ref[...], preferred_element_type=F32)
     gxt_ref[...] = lax.dot_general(proj, values_ref[...].astype(BF), TN, preferred_element_type=F32)
@@ -421,23 +428,98 @@
         gtaps_ref[:, c] = jnp.concatenate(sums_of + [jnp.zeros((8 - len(sums_of), 128), F32)], axis=0)
 
 
-def conv_back(gval, proj, x_t, values, sums, ext, same, conv_taps, halo, wide):
+def conv_back(gval, proj, x_t, values, sums, ext, same, conv_taps, place, slots, first, halo, wide):
     rows, chans = gval.shape
     taps = conv_taps.shape[0]
     col = lambda r: pl.BlockSpec((r, wide), lambda g: (0, g))
-    mask = pl.BlockSpec(same.shape, lambda g: (0, 0))
+    fixed = lambda a: pl.BlockSpec(a.shape, lambda g: (0, 0))
+    mask = fixed(same)
     f32 = lambda r: jax.ShapeDtypeStruct((r, chans), F32)
     return pl.pallas_call(
         functools.partial(conv_back_kernel, halo),
         grid=(chans // wide,),
-        in_specs=[col(rows), pl.BlockSpec(proj.shape, lambda g: (0, 0)), col(x_t.shape[0]), col(rows), col(rows), col(ext.shape[0]), mask, col(taps)],
-        out_specs=[col(rows), col(8), col(8), col(x_t.shape[0]), col(8)],
-        out_shape=[jax.ShapeDtypeStruct((rows, chans), BF), f32(8), f32(8), f32(x_t.shape[0]), f32(8)],
+        in_specs=[col(rows), pl.BlockSpec(proj.shape, lambda g: (0, 0)), col(x_t.shape[0]), col(rows), col(rows), col(ext.shape[0]), mask, col(taps), fixed(place), fixed(slots), fixed(first)],
+        out_specs=[fixed(first), col(rows), col(8), col(8), col(x_t.shape[0]), col(8)],
+        out_shape=[jax.ShapeDtypeStruct(first.shape, BF), jax.ShapeDtypeStruct((rows, chans), BF), f32(8), f32(8), f32(x_t.shape[0]), f32(8)],
         scratch_shapes=[pltpu.VMEM((rows + 8, wide), F32)],
         compiler_params=pltpu.CompilerParams(vmem_limit_bytes=VM),
         cost_estimate=pl.CostEstimate(flops=60*rows*chans, bytes_accessed=20*rows*chans, transcendentals=rows*chans),
         name="conv_back",
-    )(gval, proj, x_t, values, sums, ext, same, conv_taps)
+    )(gval, proj, x_t, values, sums, ext, same, conv_taps, place, slots, first)
+
+
+def tail_gate_kernel(gz_ref, normed_ref, win_ref, gwin_ref, total_ref):
+    @pl.when(pl.program_id(0) == 0)
+    def _():
+        total_ref[...] = jnp.zeros_like(total_ref)
+
+    grad = gz_ref[...]
+    gwin_ref[...] = lax.dot_general(grad, normed_ref[...], TN, preferred_element_type=F32).astype(BF)
+    total_ref[...] += jnp.dot(grad, win_ref[...], preferred_element_type=F32)
+
+
+def tail_gate(grad_z, normed, full_in, wide):
+    rows, width = normed.shape
+    chans = grad_z.shape[1]
+    steps = chans // wide
+    whole = pl.BlockSpec((rows, width), lambda g: (0, 0))
+    weights = pl.BlockSpec((wide, width), lambda g: (g + steps, 0))
+    return pl.pallas_call(
+        tail_gate_kernel,
+        grid=(steps,),
+        in_specs=[pl.BlockSpec((rows, wide), lambda g: (0, g)), whole, weights],
+        out_specs=[weights, whole],
+        out_shape=[jax.ShapeDtypeStruct((2 * chans, width), BF), jax.ShapeDtypeStruct((rows, width), F32)],
+        compiler_params=pltpu.CompilerParams(vmem_limit_bytes=VM),
+        cost_estimate=pl.CostEstimate(flops=4*rows*chans*width, bytes_accessed=4*chans*width, transcendentals=0),
+        name="tail_gate",
+    )(grad_z, normed, full_in)
+
+
+def tail_kernel(conv_ref, last_ref, rim_ref, normed_ref, win_ref, tok_ref, gain_ref, first_ref, before_ref, _, gwin_ref, gtok_ref, ggain_ref, total, mixed):
+    step = pl.program_id(0)
+    rows = tok_ref.shape[0]
+
+    @pl.when(step == 0)
+    def _():
+        total[...] = before_ref[...]
+
+    mixed[0 : rows - 16, :] = conv_ref[0 : rows - 16, :]
+    kept = conv_ref[rows - 16 : rows, :].astype(F32)
+    mixed[rows - 16 : rows, :] = jnp.concatenate([kept[0:8], last_ref[...] + rim_ref[...]], axis=0).astype(BF)
+    grad = mixed[...]
+    gwin_ref[...] = lax.dot_general(grad, normed_ref[...], TN, preferred_element_type=F32).astype(BF)
+    total[...] += jnp.dot(grad, win_ref[...], preferred_element_type=F32)
+
+    @pl.when(step == pl.num_programs(0) - 1)
+    def _():
+        tok = tok_ref[...].astype(F32)
+        grad_normed = total[...]
+        scale = lax.rsqrt(jnp.mean(tok * tok, axis=1, keepdims=True) + EPS)
+        scaled = grad_normed * gain_ref[...]
+        ggain_ref[...] = jnp.sum(grad_normed * (tok * scale), axis=0, keepdims=True)
+        back = scale * scaled - tok * (scale * scale * scale) * jnp.mean(tok * scaled, axis=1, keepdims=True)
+        gtok_ref[...] = (first_ref[...] + back).astype(BF)
+
+
+def tail(grad_conv, last, rim, normed, full_in, tok, gain, grad_first, before, gwin, wide):
+    rows, width = tok.shape
+    chans = grad_conv.shape[1]
+    whole = lambda a: pl.BlockSpec(a.shape, lambda g: (0, 0))
+    col = lambda r: pl.BlockSpec((r, wide), lambda g: (0, g))
+    weights = pl.BlockSpec((wide, width), lambda g: (g, 0))
+    return pl.pallas_call(
+        tail_kernel,
+        grid=(chans // wide,),
+        in_specs=[col(rows), col(8), col(8), whole(normed), weights, whole(tok), whole(gain), whole(grad_first), whole(before), pl.BlockSpec(memory_space=pl.ANY)],
+        out_specs=[weights, whole(tok), whole(gain)],
+        out_shape=[jax.ShapeDtypeStruct(gwin.shape, BF), jax.ShapeDtypeStruct(tok.shape, BF), jax.ShapeDtypeStruct(gain.shape, F32)],
+        input_output_aliases={9: 0},
+        scratch_shapes=[pltpu.VMEM((rows, width), F32), pltpu.VMEM((rows, wide), BF)],
+        compiler_params=pltpu.CompilerParams(vmem_limit_bytes=VM),
+        cost_estimate=pl.CostEstimate(flops=4*rows*chans*width, bytes_accessed=4*chans*width, transcendentals=0),
+        name="tail",
+    )(grad_conv, last, rim, normed, full_in, tok, gain, grad_first, before, gwin)
 
 
 def flip(value, bit):
@@ -1277,16 +1359,15 @@
     part_exp = part_exp.reshape(experts, 2, piece, width)
     part_down = part_exp[:, 1]
     sum_up = swap(part_exp[:, 0])
-    mixed_out = (first_sum + dot(gather_mat, mixed_slots)).astype(BF)
-    grad_conv_b, grad_last, grad_rim, grad_x_t, grad_taps = conv_back(grad_vals, grad_proj, full_x_t, values, conv_sum, conv_in, same, conv_f, halo, wide)
-    grad_last = (grad_last + shift(grad_rim, "seq", -1)).astype(BF)
-    grad_conv_in = jnp.concatenate([grad_conv_b[: rows - 8], grad_last])
-    grad_w_in = dot_tn(jnp.concatenate([grad_conv_in, grad_z_b], axis=1), normed).astype(BF)
-    grad_normed = dot(grad_conv_in, full_in[:chans]) + dot(grad_z_b, full_in[chans:])
-    grad_norm_one, grad_gain_one = rms_back(tok_f, gain_one, grad_normed)
-    tokens_grad = (grad_first + grad_norm_one).astype(BF)
-
-    grad_small = jnp.concatenate([grad_gain_one, grad_gain_two, grad_router.reshape(-1)])
+    mixed_out, grad_conv_b, grad_last, grad_rim, grad_x_t, grad_taps = conv_back(
+        grad_vals, grad_proj, full_x_t, values, conv_sum, conv_in, same, conv_f, gather_mat, mixed_slots, first_sum, halo, wide
+    )
+    grad_z_b, grad_rim = lax.optimization_barrier((grad_z_b, grad_rim))
+    grad_w_in, gate_part = tail_gate(grad_z_b, normed, full_in, wide)
+    grad_w_in, tokens_grad, grad_gain_one = tail(
+        grad_conv_b, grad_last, shift(grad_rim, "seq", -1), normed, full_in, tok_b, gain_one[None], grad_first, gate_part, grad_w_in, wide
+    )
+    grad_small = jnp.concatenate([grad_gain_one[0], grad_gain_two, grad_router.reshape(-1)])
     grad_packed = pack_grads(
         (grad_x_t, grad_dt_t, g_log, grad_taps, grad_dtb, grad_skip), (w_x.shape[1], rank, n, taps + 1, 1, 1), jnp.pad(grad_small.reshape(devices, -1), ((0, 0), (0, 256 - share))), own
     )

time: 490 us -> 490 us (level)
  matrix products: 22.7 us -> 3.2 us
  Pallas kernels: 363 us -> 380 us
    pallas_call x0 -> x2, Pallas kernels: none -> 17.5 us  [the longest x1 9.92 us: tail(): pl.pallas_call(tail_kernel, grid=(chans // wide,), in_specs=[col(rows), c...]
    dot_general x5 -> x2, matrix products: 14.3 us -> 1.49 us  [dot(): return jnp.dot(a, b, preferred_element_type=F32)]
    dot_general x2 -> x1, matrix products: 8.43 us -> 1.71 us  [dot_tn(): return lax.dot_general(a, b, TN, preferred_element_type=F32)]
  transfers between devices with their start and end apart: 11 -> 11, of which waited for: 1 -> 1; matrix products, arithmetic and copies ran while one was open for 7% -> 3% of each run, Pallas kernels for 50% -> 54%
where the time goes in v5:
time: 490 us; the launch traced here: 481 us
  Pallas kernels  380 us (78%)
  starting transfers between devices  32.8 us (7%)
  local copies, waits for them, and re-layouts  17.3 us (4%)
  blocking collectives  16.4 us (3%)
  between operations  14.6 us (3%)
  waiting for transfers between devices  11.4 us (2%)
  other arithmetic  5.15 us (1%)
    pallas_call x1, Pallas kernels, gather_all(): pl.pallas_call(functools.partial(gather_kernel, parts, count), in_specs=[...  84.4 us
    pallas_call x1, Pallas kernels, scatter_all(): pl.pallas_call(functools.partial(scatter_kernel, parts, count), in_specs=...  78.4 us
    pallas_call x1, Pallas kernels, back_pass(): pl.pallas_call(functools.partial(back_kernel, n, rank_cols), grid=(chans...  51.2 us
    pallas_call x1, Pallas kernels, experts_pass(): pl.pallas_call(functools.partial(experts_kernel, block, piece), in_specs=...  39.1 us
    all_to_all x5, starting transfers between devices, swap(): return lax.all_to_all(value, 'seq', 0, 0)  30.3 us
    pallas_call x1, Pallas kernels, scan_pass(): pl.pallas_call(functools.partial(scan_kernel, n), grid=(chans // wide,),...  25.3 us
    pallas_call x1, Pallas kernels, back_front(): pl.pallas_call(functools.partial(back_front_kernel, n, order, chans // wi...  18.1 us
    all_to_all x1, blocking collectives, swap(): return lax.all_to_all(value, 'seq', 0, 0)  16.4 us
  transfers between devices with their start and end apart: 11, of which 1 were waited for; matrix products, arithmetic and copies ran while one was open for 3% of the time, Pallas kernels for 54%

profile of v5, /device:TPU:9, one launch (start us, length us, event | category | flops | bytes accessed | tf_op | source)
XLA Modules:
  0.0 481.0 jit_solution(6063161434652011747)
XLA Ops:
  8.0 1.2 broadcast_in_dim.48.small_ref
  9.2 1.6 pack_params.1.rest_ref
  12.2 84.4 %gather_all.1 = (bf16[4,2,4,144,1152]{4,3,2,1,0:T(8,128)(2,1)}, bf16[4,2,4,80,256]{4,3,2,1,0:T(8,128)(2,1)}, bf16[4,96,1152]{2,1,0:T(8,128)(2,1)}, bf16[16,1152]{1,0:T(8,128)(2,1)}, s32[16,128]{1,0:T(8,128)}) custom-call(bf16[144,1152]{1,0:T(8,128)(2,1)} %in_ref.1, bf16[80,256]{1,0:T(8,128)(2,1)} %pack_params.1.rest_ref, bf16[4,96,1152]{2,1,0:T(8,128)(2,1)} %bitcast.65, ...), custom_call_target="tpu_custom_call" | custom-call | bytes 200000000 | tf_op jit(solution)/shard_map/gather_all/pallas_call | solution.py:736
  96.6 2.8 unpack_small.1
  99.4 8.0 %all-to-all-start = ((bf16[4,96,1152]{2,1,0:T(8,128)(2,1)}), bf16[4,96,1152]{2,1,0:T(8,128)(2,1)S(1)}, u32[]{:S(2)}, u32[]{:S(2)}) async-start(bf16[4,96,1152]{2,1,0:T(8,128)(2,1)} %param.31), calls=%async_computation | async-start | bytes 1769472 | tf_op jit(solution)/shard_map/all_to_all | solution.py:1266
  109.4 12.5 %front.1 = (bf16[256,1152]{1,0:T(8,128)(2,1)}, f32[272,2304]{1,0:T(8,128)}, f32[256,2304]{1,0:T(8,128)}, f32[256,2304]{1,0:T(8,128)}, f32[256,2304]{1,0:T(8,128)}, /*index=5*/f32[256,128]{1,0:T(8,128)}) custom-call(bf16[16,1152]{1,0:T(8,128)(2,1)} %get-tuple-element.111.rim_ref, bf16[256,1152]{1,0:T(8,128)(2,1)} %bitcast.58, ...), custom_call_target="tpu_custom_call" | custom-call | flops 2717908992 | bytes 20054016 | tf_op jit(solution)/shard_map/front/pallas_call | solution.py:86
  121.9 16.2 %steps.1 = (bf16[256,128]{1,0:T(8,128)(2,1)}, f32[4096,128]{1,0:T(8,128)}, f32[4096,128]{1,0:T(8,128)}, bf16[256,256]{1,0:T(8,128)(2,1)}, bf16[256,256]{1,0:T(8,...) custom-call(f32[256,128]{1,0:T(8,128)} %get-tuple-element.122.proj_r, ...), custom_call_target="tpu_custom_call" | custom-call | flops 94371840 | bytes 14155776 | tf_op jit(solution)/shard_map/steps/pallas_call | solution.py:150
  139.5 1.7 convolution_convert_fusion
  141.2 5.9 %chain.2.start_ref = f32[16,2304]{1,0:T(8,128)} custom-call(f32[16,2304]{1,0:T(8,128)} %get-tuple-element.135.carry_ref, f32[16,2304]{1,0:T(8,128)} %get-tuple-element.136.own_ref), custom_call_target="tpu_custom_call" | custom-call | tf_op jit(solution)/shard_map/chain/pallas_call | solution.py:1084
  147.1 6.8 %all-to-all-start.1 = ((bf16[4,128,1152]{2,1,0:T(8,128)(2,1)}), bf16[4,128,1152]{2,1,0:T(8,128)(2,1)S(1)}, u32[]{:S(2)}, u32[]{:S(2)}) async-start(bf16[4,128,1152]{2,1,0:T(8,128)(2,1)} %bitcast.13), calls=%async_computation.1 | async-start | bytes 2359296 | tf_op jit(solution)/shard_map/all_to_all | solution.py:1266
  155.3 25.3 %scan_pass.1 = (f32[256,2304]{1,0:T(8,128)}, f32[256,2304]{1,0:T(8,128)}, bf16[256,2304]{1,0:T(8,128)(2,1)}, f32[256,1152]{1,0:T(8,128)}, bf16[256,1152]{1,0:T(8,128)(2,1)}, /*index=5*/bf16[256,1152]{1,0:T(8,128)(2,1)}) custom-call(f32[256,2304]{1,0:T(8,128)} %get-tuple-element.128.dte_ref, f32[256,2304]{1,0:T(8,128)} %get-tuple-element.129.dtx_ref, ...), custom_call_target="tpu_custom_call" | custom-call | flops 94371840 | bytes 7077888 | tf_op jit(solution)/shard_map/scan_pass/pallas_call | solution.py:211
  180.6 4.6 all-to-all-start.2
  186.4 10.6 %all-to-all-done.2.early_ref = bf16[4,64,1152]{2,1,0:T(8,128)(2,1)S(1)} async-done(((bf16[4,64,1152]{2,1,0:T(8,128)(2,1)}), bf16[4,64,1152]{2,1,0:T(8,128)(2,1)S(1)}, u32[]{:S(2)}, u32[]{:S(2)}) %all-to-all-start.2) | async-done | bytes 589856 | tf_op jit(solution)/shard_map/all_to_all | solution.py:1266
  197.7 39.1 %experts.1 = (bf16[4,64,1152]{2,1,0:T(8,128)(2,1)}, bf16[4,64,1152]{2,1,0:T(8,128)(2,1)}, bf16[4,128,1152]{2,1,0:T(8,128)(2,1)}, f32[1152,128]{1,0:T(8,128)}, bf16[32,2,96,1152]{3,2,1,0:T(8,128)(2,1)}) custom-call(bf16[256,256]{1,0:T(8,128)(2,1)} %get-tuple-element.215.pick_ref, bf16[256,1152]{1,0:T(8,128)(2,1)} %get-tuple-element.141.n2_ref, ...), custom_call_target="tpu_custom_call" | custom-call | flops 21743271936 | bytes 100000000 | tf_op jit(solution)/shard_map/experts/pallas_call | solution.py:1221
  236.9 1.0 copy-done.10
  237.9 16.4 %all_to_all.30 = bf16[4,64,1152]{2,1,0:T(8,128)(2,1)S(1)} all-to-all(bf16[4,64,1152]{2,1,0:T(8,128)(2,1)S(1)} %copy-done.10), channel_id=1, replica_groups=mesh['dp'=8,'seq'=4] {'seq'}, dimensions={0} | all-to-all | bytes 1179648 | tf_op jit(solution)/shard_map/all_to_all | solution.py:1266
  254.3 5.2 %all-to-all-start.4 = ((bf16[4,128,1152]{2,1,0:T(8,128)(2,1)}), bf16[4,128,1152]{2,1,0:T(8,128)(2,1)S(1)}, u32[]{:S(2)}, u32[]{:S(2)}) async-start(bf16[4,128,1152]{2,1,0:T(8,128)(2,1)} %get-tuple-element.161), calls=%async_computation.4 | async-start | bytes 2359296 | tf_op jit(solution)/shard_map/all_to_all | solution.py:1266
  260.8 1.3 multiply_reduce_fusion
  262.1 1.6 fusion.14
  263.7 18.1 %back_front.1 = (f32[256,2304]{1,0:T(8,128)}, bf16[256,2304]{1,0:T(8,128)(2,1)}, bf16[2304,1152]{1,0:T(8,128)(2,1)}, f32[16,2304]{1,0:T(8,128)}) custom-call(bf16[256,1152]{1,0:T(8,128)(2,1)} %get-tuple-element.210.grad_ref, bf16[2304,1152]{1,0:T(8,128)(2,1)} %all-gather.6.cloned.1.call-done.out_ref, f32[256,2304]{1,0:T(8,128)} %get-tuple-element.138.z_ref, ...), custom_call_target="tpu_custom_call" | custom-call | flops 75497472 | bytes 4718592 | tf_op jit(solution)/shard_map/back_front/pallas_call | solution.py:277
  281.8 9.1 %chain.3.next_ref = f32[16,2304]{1,0:T(8,128)} custom-call(f32[16,2304]{1,0:T(8,128)} %get-tuple-element.135.carry_ref, f32[16,2304]{1,0:T(8,128)} %get-tuple-element.158.own_ref), custom_call_target="tpu_custom_call" | custom-call | tf_op jit(solution)/shard_map/chain/pallas_call | solution.py:1084
  290.9 51.2 %back_pass.1 = (f32[256,2304]{1,0:T(8,128)}, f32[16,2304]{1,0:T(8,128)}, f32[128,2304]{1,0:T(8,128)}, f32[1,2304]{1,0:T(1,128)}, f32[1,2304]{1,0:T(1,128)}, /*index=5*/bf16[256,128]{1,0:T(8,128)(2,1)}) custom-call(f32[256,2304]{1,0:T(8,128)} %get-tuple-element.127.dt_ref, f32[256,2304]{1,0:T(8,128)} %get-tuple-element.128.dte_ref, ...), custom_call_target="tpu_custom_call" | custom-call | flops 245366784 | bytes 14155776 | tf_op jit(solution)/shard_map/back_pass/pallas_call | solution.py:377
  344.1 1.4 slice_bitcast_fusion
  345.5 5.7 %all-to-all-start.5 = ((bf16[4,96,1152]{2,1,0:T(8,128)(2,1)}), bf16[4,96,1152]{2,1,0:T(8,128)(2,1)S(1)}, u32[]{:S(2)}, u32[]{:S(2)}) async-start(bf16[4,96,1152]{2,1,0:T(8,128)(2,1)} %get-tuple-element.213), calls=%async_computation.6 | async-start | bytes 1769472 | tf_op jit(solution)/shard_map/all_to_all | solution.py:1266
  352.3 10.3 %conv_back.1 = (bf16[256,1152]{1,0:T(8,128)(2,1)}, bf16[256,2304]{1,0:T(8,128)(2,1)}, f32[8,2304]{1,0:T(8,128)}, f32[8,2304]{1,0:T(8,128)}, f32[128,2304]{1,0:T(8,128)}, /*index=5*/f32[8,2304]{1,0:T(8,128)}) custom-call(f32[256,2304]{1,0:T(8,128)} %get-tuple-element.164.gval_ref, bf16[256,128]{1,0:T(8,128)(2,1)} %get-tuple-element.165.proj_ref, ...), custom_call_target="tpu_custom_call" | custom-call | flops 35389440 | bytes 11796480 | tf_op jit(solution)/shard_map/conv_back/pallas_call | solution.py:438
  362.6 2.2 collective-permute-start
  364.9 7.6 %tail_gate.1 = (bf16[4608,1152]{1,0:T(8,128)(2,1)}, f32[256,1152]{1,0:T(8,128)}) custom-call(bf16[256,2304]{1,0:T(8,128)(2,1)} %get-tuple-element.176.gz_ref, bf16[256,1152]{1,0:T(8,128)(2,1)} %get-tuple-element.175.normed_ref, bf16[4608,1152]{1,0:T(8,128)(2,1)} %bitcast.53), custom_call_target="tpu_custom_call" | custom-call | flops 2717908992 | bytes 10616832 | tf_op jit(solution)/shard_map/tail_gate/pallas_call | solution.py:467
  373.1 9.9 %tail.1 = (bf16[4608,1152]{1,0:T(8,128)(2,1)}, bf16[256,1152]{1,0:T(8,128)(2,1)}, f32[1,1152]{1,0:T(1,128)}) custom-call(bf16[256,2304]{1,0:T(8,128)(2,1)} %get-tuple-element.170.conv_ref, f32[8,2304]{1,0:T(8,128)} %get-tuple-element.171.last_ref, f32[8,2304]{1,0:T(8,128)} %copy-done.11, ...), custom_call_target="tpu_custom_call", output_to_operand_aliasing={{0}: (9, {})} | custom-call | flops 2717908992 | bytes 10616832 | tf_op jit(solution)/shard_map/tail/pallas_call | solution.py:511
  384.4 3.1 pack_small.1
  387.6 2.3 pad.14.proj_ref
  389.9 78.4 %scatter_all.1 = (f32[144,1152]{1,0:T(8,128)}, f32[80,256]{1,0:T(8,128)}, bf16[4,80,1152]{2,1,0:T(8,128)(2,1)}, bf16[4,96,1152]{2,1,0:T(8,128)(2,1)}) custom-call(bf16[4,2,4,144,1152]{4,3,2,1,0:T(8,128)(2,1)} %bitcast.55, bf16[4,2,4,80,256]{4,3,2,1,0:T(8,128)(2,1)} %bitcast.61, bf16[4,80,1152]{2,1,0:T(8,128)(2,1)} %pad.14.proj_ref, ...), custom_call_target="tpu_custom_call" | custom-call | bytes 200000000 | tf_op jit(solution)/shard_map/scatter_all/pallas_call | solution.py:888
  468.3 4.8 finish.1
  (88 shorter events, 16.2 us)
Async XLA Ops:
  7.2 148.1 %all-gather.6.cloned.1.call-start = ((), (), s32[]{:S(2)}) async-start(), calls=%async_computation.8 | async-start | bytes 5474304 | tf_op jit(solution)/shard_map/all_gather | solution.py:1292
  7.9 189.0 %all-gather.8.cloned.1.call-start = ((), (), s32[]{:S(2)}) async-start(), calls=%async_computation.11 | async-start | bytes 7962624 | tf_op jit(solution)/shard_map/all_gather | solution.py:1307
  99.4 8.0 %copy-start.13 = (s32[16,128]{1,0:T(8,128)S(1)}, s32[16,128]{1,0:T(8,128)}, u32[]{:S(2)}) copy-start(s32[16,128]{1,0:T(8,128)} %get-tuple-element.121) | copy-start | bytes 24580
  99.4 9.3 %copy-start.12 = (f32[32,256]{1,0:T(8,128)S(1)}, f32[32,256]{1,0:T(8,128)}, u32[]{:S(2)}) copy-start(f32[32,256]{1,0:T(8,128)} %get-tuple-element.115) | copy-start | bytes 98308
  99.4 38.7 %all-to-all-start = ((bf16[4,96,1152]{2,1,0:T(8,128)(2,1)}), bf16[4,96,1152]{2,1,0:T(8,128)(2,1)S(1)}, u32[]{:S(2)}, u32[]{:S(2)}) async-start(bf16[4,96,1152]{2,1,0:T(8,128)(2,1)} %param.31), calls=%async_computation | async-start | bytes 1769472 | tf_op jit(solution)/shard_map/all_to_all | solution.py:1266
  107.4 89.5 %all-gather.10.cloned.1.call-start = ((), (), s32[]{:S(2)}) async-start(), calls=%async_computation.12 | async-start | bytes 7962624 | tf_op jit(solution)/shard_map/all_gather | solution.py:1329
  121.9 17.1 %copy-start.15 = (s32[1,256,1]{1,2,0:T(1,128)S(1)}, s32[1,256,1]{1,2,0:T(1,128)}, u32[]{:S(2)}) copy-start(s32[1,256,1]{1,2,0:T(1,128)} %param.18) | copy-start | bytes 3076
  138.1 1.4 copy-start.4
  138.1 0.9 copy-start.2
  147.1 33.5 %all-to-all-start.1 = ((bf16[4,128,1152]{2,1,0:T(8,128)(2,1)}), bf16[4,128,1152]{2,1,0:T(8,128)(2,1)S(1)}, u32[]{:S(2)}, u32[]{:S(2)}) async-start(bf16[4,128,1152]{2,1,0:T(8,128)(2,1)} %bitcast.13), calls=%async_computation.1 | async-start | bytes 2359296 | tf_op jit(solution)/shard_map/all_to_all | solution.py:1266
  180.6 5.7 %copy-start.6 = (bf16[4,128,1152]{2,1,0:T(8,128)(2,1)}, bf16[4,128,1152]{2,1,0:T(8,128)(2,1)S(1)}, u32[]{:S(2)}) copy-start(bf16[4,128,1152]{2,1,0:T(8,128)(2,1)S(1)} %all-to-all-done.1.go_ref) | copy-start | bytes 3538948
  180.6 16.3 %all-to-all-start.2 = ((bf16[4,64,1152]{2,1,0:T(8,128)(2,1)}), bf16[4,64,1152]{2,1,0:T(8,128)(2,1)S(1)}, u32[]{:S(2)}, u32[]{:S(2)}) async-start(bf16[4,64,1152]{2,1,0:T(8,128)(2,1)} %bitcast.68), calls=%async_computation.2 | async-start | bytes 1179648 | tf_op jit(solution)/shard_map/all_to_all | solution.py:1266
  185.2 157.0 %reduce-scatter.3.cloned.1.call-start = ((), (), s32[]{:S(2)}) async-start(), calls=%async_computation.9 | async-start | bytes 15925248 | tf_op jit(solution)/shard_map/reduce_scatter | solution.py:1348
  196.9 0.8 copy-start.9
  236.8 1.1 copy-start.10
  254.3 5.5 %copy-start = (f32[256,1152]{1,0:T(8,128)S(1)}, f32[256,1152]{1,0:T(8,128)}, u32[]{:S(2)}) copy-start(f32[256,1152]{1,0:T(8,128)} %get-tuple-element.140.first_ref) | copy-start | bytes 3538948
  254.3 87.9 %all-to-all-start.4 = ((bf16[4,128,1152]{2,1,0:T(8,128)(2,1)}), bf16[4,128,1152]{2,1,0:T(8,128)(2,1)S(1)}, u32[]{:S(2)}, u32[]{:S(2)}) async-start(bf16[4,128,1152]{2,1,0:T(8,128)(2,1)} %get-tuple-element.161), calls=%async_computation.4 | async-start | bytes 2359296 | tf_op jit(solution)/shard_map/all_to_all | solution.py:1266
  259.5 128.1 %reduce-scatter.5.cloned.1.call-start = ((), (), s32[]{:S(2)}) async-start(), calls=%async_computation.10 | async-start | bytes 5971968 | tf_op jit(solution)/shard_map/reduce_scatter | solution.py:1374
  259.7 1.1 copy-start.16
  342.2 1.0 copy-start.1
  342.2 1.9 copy-start.5
  345.5 6.6 %copy-start.8 = (f32[1152,128]{1,0:T(8,128)S(1)}, f32[1152,128]{1,0:T(8,128)}, u32[]{:S(2)}) copy-start(f32[1152,128]{1,0:T(8,128)} %get-tuple-element.188) | copy-start | bytes 1769476
  345.5 42.1 %all-to-all-start.5 = ((bf16[4,96,1152]{2,1,0:T(8,128)(2,1)}), bf16[4,96,1152]{2,1,0:T(8,128)(2,1)S(1)}, u32[]{:S(2)}, u32[]{:S(2)}) async-start(bf16[4,96,1152]{2,1,0:T(8,128)(2,1)} %get-tuple-element.213), calls=%async_computation.6 | async-start | bytes 1769472 | tf_op jit(solution)/shard_map/all_to_all | solution.py:1266
  362.6 9.8 %collective-permute-start = (f32[8,2304]{1,0:T(8,128)}, f32[8,2304]{1,0:T(8,128)S(1)}, u32[]{:S(2)}, u32[]{:S(2)}) collective-permute-start(f32[8,2304]{1,0:T(8,128)} %get-tuple-element.174), channel_id=1, source_target_pairs={{1,0},{2,1},{3,2},{5,4},{6,5},{7,6},{9,8},{10,9},{11,10},{13,12},{... | collective-permute-start | bytes 221192 | tf_op jit(solution)/shard_map/ppermute | solution.py:1251
  372.4 0.6 copy-start.11
  373.1 10.6 %copy-start.14 = (f32[1152]{0:T(1024)S(1)}, f32[1152]{0:T(1024)}, u32[]{:S(2)}) copy-start(f32[1152]{0:T(1024)} %get-tuple-element.208) | copy-start | bytes 13828
  387.6 80.8 %copy-start.3 = (bf16[4,96,1152]{2,1,0:T(8,128)(2,1)}, bf16[4,96,1152]{2,1,0:T(8,128)(2,1)S(1)}, u32[]{:S(2)}) copy-start(bf16[4,96,1152]{2,1,0:T(8,128)(2,1)S(1)} %all-to-all-done.5.up_ref) | copy-start | bytes 2654212
  468.3 4.8 copy-start.7
Sparse Core Ops, SparseCore 0:
  10.9 85.8 all-gather.5
  99.5 45.4 all-gather.7
  146.6 42.2 all-gather.9
  237.0 78.3 reduce-scatter.2
  342.4 37.0 reduce-scatter.4

commit v6 on v5

--- a/solution.py
+++ b/solution.py
@@ -937,7 +937,7 @@
     )(pack)
 
 
-def pack_kernel(own, sizes, x_ref, dt_ref, log_ref, taps_ref, dtb_ref, skip_ref, small_ref, out_ref, wide, tall):
+def pack_kernel(own, sizes, x_ref, dt_ref, log_ref, taps_ref, dtb_ref, skip_ref, small_ref, part_ref, out_ref, grown_ref, wide, tall):
     at = 0
     for ref, size in zip((x_ref, dt_ref, log_ref, taps_ref, dtb_ref, skip_ref), sizes):
         wide[at : at + size, :] = ref[0:size, :]
@@ -950,23 +950,26 @@
     for b in range(out_ref.shape[0]):
         tail = jnp.where(first, jnp.broadcast_to(small_ref[b : b + 1, :], (8, cols)), 0.0)
         out_ref[b] = jnp.concatenate([tall[b * own : (b + 1) * own, :], tail], axis=0).astype(BF)
-
-
-def pack_grads(parts, sizes, small, own):
+    for z in range(part_ref.shape[0]):
+        rows = part_ref[z].astype(F32)
+        grown_ref[z] = jnp.concatenate([rows, jnp.zeros((grown_ref.shape[1] - own, rows.shape[1]), F32)], axis=0).astype(BF)
+
+
+def pack_grads(parts, sizes, small, part_out, own):
     blocks, cols = small.shape
     chans = parts[0].shape[1]
     rows = own + -own % 16
     if own % 8:
         turned = jnp.concatenate([part[:size] for part, size in zip(parts, sizes)]).T.reshape(blocks, own, -1)
         turned = jnp.pad(turned, ((0, 0), (0, 0), (0, cols - turned.shape[2])))
-        return jnp.concatenate([turned, small[:, None], jnp.zeros((blocks, rows - own - 1, cols), F32)], axis=1).astype(BF)
+        return jnp.concatenate([turned, small[:, None], jnp.zeros((blocks, rows - own - 1, cols), F32)], axis=1).astype(BF), jnp.pad(part_out, ((0, 0), (0, rows - own), (0, 0)))
     return pl.pallas_call(
         functools.partial(pack_kernel, own, sizes),
-        out_shape=jax.ShapeDtypeStruct((blocks, rows, cols), BF),
+        out_shape=[jax.ShapeDtypeStruct((blocks, rows, cols), BF), jax.ShapeDtypeStruct((part_out.shape[0], rows, part_out.shape[2]), BF)],
         scratch_shapes=[pltpu.VMEM((cols, chans), F32), pltpu.VMEM((chans, cols), F32)],
         compiler_params=pltpu.CompilerParams(vmem_limit_bytes=VM),
         name="pack_small",
-    )(*parts, small)
+    )(*parts, small, part_out)
 
 
 def finish_kernel(own, cuts, pack_ref, up_ref, down_ref, proj_ref, up_out, down_out, row_out, proj_out, *small_outs):
@@ -1368,11 +1371,10 @@
         grad_conv_b, grad_last, shift(grad_rim, "seq", -1), normed, full_in, tok_b, gain_one[None], grad_first, gate_part, grad_w_in, wide
     )
     grad_small = jnp.concatenate([grad_gain_one[0], grad_gain_two, grad_router.reshape(-1)])
-    grad_packed = pack_grads(
-        (grad_x_t, grad_dt_t, g_log, grad_taps, grad_dtb, grad_skip), (w_x.shape[1], rank, n, taps + 1, 1, 1), jnp.pad(grad_small.reshape(devices, -1), ((0, 0), (0, 256 - share))), own
+    part_out = lax.psum_scatter(grad_w_out, "dp", scatter_dimension=0, tiled=True, axis_index_groups=ring).reshape(-1, own, width)
+    grad_packed, part_out = pack_grads(
+        (grad_x_t, grad_dt_t, g_log, grad_taps, grad_dtb, grad_skip), (w_x.shape[1], rank, n, taps + 1, 1, 1), jnp.pad(grad_small.reshape(devices, -1), ((0, 0), (0, 256 - share))), part_out, own
     )
-    part_out = lax.psum_scatter(grad_w_out, "dp", scatter_dimension=0, tiled=True, axis_index_groups=ring).reshape(-1, own, width)
-    part_out = jnp.pad(part_out, ((0, 0), (0, -own % 16), (0, 0)))
     if direct:
         grad_packed, sum_up = lax.optimization_barrier((grad_packed, sum_up))
         sum_in, sum_pack, all_out, sum_down = scatter_all(

time: 490 us -> 488 us (level)
  no operation moved by 1% of the time
where the time goes in v6:
time: 488 us; the launch traced here: 479 us
  Pallas kernels  381 us (78%)
  starting transfers between devices  32.8 us (7%)
  blocking collectives  16.4 us (3%)
  local copies, waits for them, and re-layouts  15 us (3%)
  between operations  14.6 us (3%)
  waiting for transfers between devices  11.3 us (2%)
  other arithmetic  5.15 us (1%)
    pallas_call x1, Pallas kernels, gather_all(): pl.pallas_call(functools.partial(gather_kernel, parts, count), in_specs=[...  84.4 us
    pallas_call x1, Pallas kernels, scatter_all(): pl.pallas_call(functools.partial(scatter_kernel, parts, count), in_specs=...  78.5 us
    pallas_call x1, Pallas kernels, back_pass(): pl.pallas_call(functools.partial(back_kernel, n, rank_cols), grid=(chans...  51.3 us
    pallas_call x1, Pallas kernels, experts_pass(): pl.pallas_call(functools.partial(experts_kernel, block, piece), in_specs=...  39.1 us
    all_to_all x5, starting transfers between devices, swap(): return lax.all_to_all(value, 'seq', 0, 0)  30.3 us
    pallas_call x1, Pallas kernels, scan_pass(): pl.pallas_call(functools.partial(scan_kernel, n), grid=(chans // wide,),...  25.3 us
    pallas_call x1, Pallas kernels, back_front(): pl.pallas_call(functools.partial(back_front_kernel, n, order, chans // wi...  18.1 us
    all_to_all x1, blocking collectives, swap(): return lax.all_to_all(value, 'seq', 0, 0)  16.4 us
  transfers between devices with their start and end apart: 11, of which 1 were waited for; matrix products, arithmetic and copies ran while one was open for 3% of the time, Pallas kernels for 54%

profile of v6, /device:TPU:9, one launch (start us, length us, event | category | flops | bytes accessed | tf_op | source)
XLA Modules:
  0.0 479.2 jit_solution(3427946604114071882)
XLA Ops:
  8.0 1.2 broadcast_in_dim.48.small_ref
  9.2 1.6 pack_params.1.rest_ref
  12.2 84.4 %gather_all.1 = (bf16[4,2,4,144,1152]{4,3,2,1,0:T(8,128)(2,1)}, bf16[4,2,4,80,256]{4,3,2,1,0:T(8,128)(2,1)}, bf16[4,96,1152]{2,1,0:T(8,128)(2,1)}, bf16[16,1152]{1,0:T(8,128)(2,1)}, s32[16,128]{1,0:T(8,128)}) custom-call(bf16[144,1152]{1,0:T(8,128)(2,1)} %in_ref.1, bf16[80,256]{1,0:T(8,128)(2,1)} %pack_params.1.rest_ref, bf16[4,96,1152]{2,1,0:T(8,128)(2,1)} %bitcast.65, ...), custom_call_target="tpu_custom_call" | custom-call | bytes 200000000 | tf_op jit(solution)/shard_map/gather_all/pallas_call | solution.py:736
  96.6 2.8 unpack_small.1
  99.4 8.0 %all-to-all-start = ((bf16[4,96,1152]{2,1,0:T(8,128)(2,1)}), bf16[4,96,1152]{2,1,0:T(8,128)(2,1)S(1)}, u32[]{:S(2)}, u32[]{:S(2)}) async-start(bf16[4,96,1152]{2,1,0:T(8,128)(2,1)} %param.31), calls=%async_computation | async-start | bytes 1769472 | tf_op jit(solution)/shard_map/all_to_all | solution.py:1269
  109.4 12.5 %front.1 = (bf16[256,1152]{1,0:T(8,128)(2,1)}, f32[272,2304]{1,0:T(8,128)}, f32[256,2304]{1,0:T(8,128)}, f32[256,2304]{1,0:T(8,128)}, f32[256,2304]{1,0:T(8,128)}, /*index=5*/f32[256,128]{1,0:T(8,128)}) custom-call(bf16[16,1152]{1,0:T(8,128)(2,1)} %get-tuple-element.113.rim_ref, bf16[256,1152]{1,0:T(8,128)(2,1)} %bitcast.58, ...), custom_call_target="tpu_custom_call" | custom-call | flops 2717908992 | bytes 20054016 | tf_op jit(solution)/shard_map/front/pallas_call | solution.py:86
  122.0 16.2 %steps.1 = (bf16[256,128]{1,0:T(8,128)(2,1)}, f32[4096,128]{1,0:T(8,128)}, f32[4096,128]{1,0:T(8,128)}, bf16[256,256]{1,0:T(8,128)(2,1)}, bf16[256,256]{1,0:T(8,...) custom-call(f32[256,128]{1,0:T(8,128)} %get-tuple-element.124.proj_r, ...), custom_call_target="tpu_custom_call" | custom-call | flops 94371840 | bytes 14155776 | tf_op jit(solution)/shard_map/steps/pallas_call | solution.py:150
  139.5 1.7 convolution_convert_fusion
  141.2 5.9 %chain.2.start_ref = f32[16,2304]{1,0:T(8,128)} custom-call(f32[16,2304]{1,0:T(8,128)} %get-tuple-element.137.carry_ref, f32[16,2304]{1,0:T(8,128)} %get-tuple-element.138.own_ref), custom_call_target="tpu_custom_call" | custom-call | tf_op jit(solution)/shard_map/chain/pallas_call | solution.py:1087
  147.1 6.8 %all-to-all-start.1 = ((bf16[4,128,1152]{2,1,0:T(8,128)(2,1)}), bf16[4,128,1152]{2,1,0:T(8,128)(2,1)S(1)}, u32[]{:S(2)}, u32[]{:S(2)}) async-start(bf16[4,128,1152]{2,1,0:T(8,128)(2,1)} %bitcast.13), calls=%async_computation.1 | async-start | bytes 2359296 | tf_op jit(solution)/shard_map/all_to_all | solution.py:1269
  155.3 25.3 %scan_pass.1 = (f32[256,2304]{1,0:T(8,128)}, f32[256,2304]{1,0:T(8,128)}, bf16[256,2304]{1,0:T(8,128)(2,1)}, f32[256,1152]{1,0:T(8,128)}, bf16[256,1152]{1,0:T(8,128)(2,1)}, /*index=5*/bf16[256,1152]{1,0:T(8,128)(2,1)}) custom-call(f32[256,2304]{1,0:T(8,128)} %get-tuple-element.130.dte_ref, f32[256,2304]{1,0:T(8,128)} %get-tuple-element.131.dtx_ref, ...), custom_call_target="tpu_custom_call" | custom-call | flops 94371840 | bytes 7077888 | tf_op jit(solution)/shard_map/scan_pass/pallas_call | solution.py:211
  180.6 4.6 all-to-all-start.2
  186.4 10.6 %all-to-all-done.2.early_ref = bf16[4,64,1152]{2,1,0:T(8,128)(2,1)S(1)} async-done(((bf16[4,64,1152]{2,1,0:T(8,128)(2,1)}), bf16[4,64,1152]{2,1,0:T(8,128)(2,1)S(1)}, u32[]{:S(2)}, u32[]{:S(2)}) %all-to-all-start.2) | async-done | bytes 589856 | tf_op jit(solution)/shard_map/all_to_all | solution.py:1269
  197.7 39.1 %experts.1 = (bf16[4,64,1152]{2,1,0:T(8,128)(2,1)}, bf16[4,64,1152]{2,1,0:T(8,128)(2,1)}, bf16[4,128,1152]{2,1,0:T(8,128)(2,1)}, f32[1152,128]{1,0:T(8,128)}, bf16[32,2,96,1152]{3,2,1,0:T(8,128)(2,1)}) custom-call(bf16[256,256]{1,0:T(8,128)(2,1)} %get-tuple-element.219.pick_ref, bf16[256,1152]{1,0:T(8,128)(2,1)} %get-tuple-element.143.n2_ref, ...), custom_call_target="tpu_custom_call" | custom-call | flops 21743271936 | bytes 100000000 | tf_op jit(solution)/shard_map/experts/pallas_call | solution.py:1224
  236.9 1.0 copy-done.10
  237.9 16.4 %all_to_all.30 = bf16[4,64,1152]{2,1,0:T(8,128)(2,1)S(1)} all-to-all(bf16[4,64,1152]{2,1,0:T(8,128)(2,1)S(1)} %copy-done.10), channel_id=1, replica_groups=mesh['dp'=8,'seq'=4] {'seq'}, dimensions={0} | all-to-all | bytes 1179648 | tf_op jit(solution)/shard_map/all_to_all | solution.py:1269
  254.3 5.2 %all-to-all-start.4 = ((bf16[4,128,1152]{2,1,0:T(8,128)(2,1)}), bf16[4,128,1152]{2,1,0:T(8,128)(2,1)S(1)}, u32[]{:S(2)}, u32[]{:S(2)}) async-start(bf16[4,128,1152]{2,1,0:T(8,128)(2,1)} %get-tuple-element.163), calls=%async_computation.4 | async-start | bytes 2359296 | tf_op jit(solution)/shard_map/all_to_all | solution.py:1269
  260.8 1.3 multiply_reduce_fusion
  262.1 1.6 fusion.14
  263.7 18.1 %back_front.1 = (f32[256,2304]{1,0:T(8,128)}, bf16[256,2304]{1,0:T(8,128)(2,1)}, bf16[2304,1152]{1,0:T(8,128)(2,1)}, f32[16,2304]{1,0:T(8,128)}) custom-call(bf16[256,1152]{1,0:T(8,128)(2,1)} %get-tuple-element.214.grad_ref, bf16[2304,1152]{1,0:T(8,128)(2,1)} %all-gather.6.cloned.1.call-done.out_ref, f32[256,2304]{1,0:T(8,128)} %get-tuple-element.140.z_ref, ...), custom_call_target="tpu_custom_call" | custom-call | flops 75497472 | bytes 4718592 | tf_op jit(solution)/shard_map/back_front/pallas_call | solution.py:277
  281.8 9.1 %chain.3.next_ref = f32[16,2304]{1,0:T(8,128)} custom-call(f32[16,2304]{1,0:T(8,128)} %get-tuple-element.137.carry_ref, f32[16,2304]{1,0:T(8,128)} %get-tuple-element.160.own_ref), custom_call_target="tpu_custom_call" | custom-call | tf_op jit(solution)/shard_map/chain/pallas_call | solution.py:1087
  290.9 51.3 %back_pass.1 = (f32[256,2304]{1,0:T(8,128)}, f32[16,2304]{1,0:T(8,128)}, f32[128,2304]{1,0:T(8,128)}, f32[1,2304]{1,0:T(1,128)}, f32[1,2304]{1,0:T(1,128)}, /*index=5*/bf16[256,128]{1,0:T(8,128)(2,1)}) custom-call(f32[256,2304]{1,0:T(8,128)} %get-tuple-element.129.dt_ref, f32[256,2304]{1,0:T(8,128)} %get-tuple-element.130.dte_ref, ...), custom_call_target="tpu_custom_call" | custom-call | flops 245366784 | bytes 14155776 | tf_op jit(solution)/shard_map/back_pass/pallas_call | solution.py:377
  342.3 0.9 copy-done.1
  344.1 1.4 slice_bitcast_fusion
  345.5 5.7 %all-to-all-start.5 = ((bf16[4,96,1152]{2,1,0:T(8,128)(2,1)}), bf16[4,96,1152]{2,1,0:T(8,128)(2,1)S(1)}, u32[]{:S(2)}, u32[]{:S(2)}) async-start(bf16[4,96,1152]{2,1,0:T(8,128)(2,1)} %get-tuple-element.217), calls=%async_computation.7 | async-start | bytes 1769472 | tf_op jit(solution)/shard_map/all_to_all | solution.py:1269
  352.4 10.3 %conv_back.1 = (bf16[256,1152]{1,0:T(8,128)(2,1)}, bf16[256,2304]{1,0:T(8,128)(2,1)}, f32[8,2304]{1,0:T(8,128)}, f32[8,2304]{1,0:T(8,128)}, f32[128,2304]{1,0:T(8,128)}, /*index=5*/f32[8,2304]{1,0:T(8,128)}) custom-call(f32[256,2304]{1,0:T(8,128)} %get-tuple-element.166.gval_ref, bf16[256,128]{1,0:T(8,128)(2,1)} %get-tuple-element.167.proj_ref, ...), custom_call_target="tpu_custom_call" | custom-call | flops 35389440 | bytes 11796480 | tf_op jit(solution)/shard_map/conv_back/pallas_call | solution.py:438
  362.7 2.2 collective-permute-start
  364.9 7.6 %tail_gate.1 = (bf16[4608,1152]{1,0:T(8,128)(2,1)}, f32[256,1152]{1,0:T(8,128)}) custom-call(bf16[256,2304]{1,0:T(8,128)(2,1)} %get-tuple-element.178.gz_ref, bf16[256,1152]{1,0:T(8,128)(2,1)} %get-tuple-element.177.normed_ref, bf16[4608,1152]{1,0:T(8,128)(2,1)} %bitcast.53), custom_call_target="tpu_custom_call" | custom-call | flops 2717908992 | bytes 10616832 | tf_op jit(solution)/shard_map/tail_gate/pallas_call | solution.py:467
  373.1 9.9 %tail.1 = (bf16[4608,1152]{1,0:T(8,128)(2,1)}, bf16[256,1152]{1,0:T(8,128)(2,1)}, f32[1,1152]{1,0:T(1,128)}) custom-call(bf16[256,2304]{1,0:T(8,128)(2,1)} %get-tuple-element.172.conv_ref, f32[8,2304]{1,0:T(8,128)} %get-tuple-element.173.last_ref, f32[8,2304]{1,0:T(8,128)} %copy-done.11, ...), custom_call_target="tpu_custom_call", output_to_operand_aliasing={{0}: (9, {})} | custom-call | flops 2717908992 | bytes 10616832 | tf_op jit(solution)/shard_map/tail/pallas_call | solution.py:511
  384.5 3.6 pack_small.1
  388.1 78.5 %scatter_all.1 = (f32[144,1152]{1,0:T(8,128)}, f32[80,256]{1,0:T(8,128)}, bf16[4,80,1152]{2,1,0:T(8,128)(2,1)}, bf16[4,96,1152]{2,1,0:T(8,128)(2,1)}) custom-call(bf16[4,2,4,144,1152]{4,3,2,1,0:T(8,128)(2,1)} %bitcast.55, bf16[4,2,4,80,256]{4,3,2,1,0:T(8,128)(2,1)} %bitcast.63, bf16[4,80,1152]{2,1,0:T(8,128)(2,1)} %get-tuple-element.195.proj_ref, ...), custom_call_target="tpu_custom_call" | custom-call | bytes 200000000 | tf_op jit(solution)/shard_map/scatter_all/pallas_call | solution.py:888
  466.6 4.8 finish.1
  (87 shorter events, 15.2 us)
Async XLA Ops:
  7.2 148.1 %all-gather.6.cloned.1.call-start = ((), (), s32[]{:S(2)}) async-start(), calls=%async_computation.8 | async-start | bytes 5474304 | tf_op jit(solution)/shard_map/all_gather | solution.py:1295
  7.9 189.0 %all-gather.8.cloned.1.call-start = ((), (), s32[]{:S(2)}) async-start(), calls=%async_computation.11 | async-start | bytes 7962624 | tf_op jit(solution)/shard_map/all_gather | solution.py:1310
  99.4 8.0 %copy-start.13 = (s32[16,128]{1,0:T(8,128)S(1)}, s32[16,128]{1,0:T(8,128)}, u32[]{:S(2)}) copy-start(s32[16,128]{1,0:T(8,128)} %get-tuple-element.123) | copy-start | bytes 24580
  99.4 9.3 %copy-start.12 = (f32[32,256]{1,0:T(8,128)S(1)}, f32[32,256]{1,0:T(8,128)}, u32[]{:S(2)}) copy-start(f32[32,256]{1,0:T(8,128)} %get-tuple-element.117) | copy-start | bytes 98308
  99.4 38.7 %all-to-all-start = ((bf16[4,96,1152]{2,1,0:T(8,128)(2,1)}), bf16[4,96,1152]{2,1,0:T(8,128)(2,1)S(1)}, u32[]{:S(2)}, u32[]{:S(2)}) async-start(bf16[4,96,1152]{2,1,0:T(8,128)(2,1)} %param.31), calls=%async_computation | async-start | bytes 1769472 | tf_op jit(solution)/shard_map/all_to_all | solution.py:1269
  107.4 89.5 %all-gather.10.cloned.1.call-start = ((), (), s32[]{:S(2)}) async-start(), calls=%async_computation.12 | async-start | bytes 7962624 | tf_op jit(solution)/shard_map/all_gather | solution.py:1332
  121.9 17.2 %copy-start.15 = (s32[1,256,1]{1,2,0:T(1,128)S(1)}, s32[1,256,1]{1,2,0:T(1,128)}, u32[]{:S(2)}) copy-start(s32[1,256,1]{1,2,0:T(1,128)} %param.18) | copy-start | bytes 3076
  138.1 1.4 copy-start.4
  138.2 0.9 copy-start.2
  147.1 33.5 %all-to-all-start.1 = ((bf16[4,128,1152]{2,1,0:T(8,128)(2,1)}), bf16[4,128,1152]{2,1,0:T(8,128)(2,1)S(1)}, u32[]{:S(2)}, u32[]{:S(2)}) async-start(bf16[4,128,1152]{2,1,0:T(8,128)(2,1)} %bitcast.13), calls=%async_computation.1 | async-start | bytes 2359296 | tf_op jit(solution)/shard_map/all_to_all | solution.py:1269
  180.6 5.7 %copy-start.6 = (bf16[4,128,1152]{2,1,0:T(8,128)(2,1)}, bf16[4,128,1152]{2,1,0:T(8,128)(2,1)S(1)}, u32[]{:S(2)}) copy-start(bf16[4,128,1152]{2,1,0:T(8,128)(2,1)S(1)} %all-to-all-done.1.go_ref) | copy-start | bytes 3538948
  180.6 16.3 %all-to-all-start.2 = ((bf16[4,64,1152]{2,1,0:T(8,128)(2,1)}), bf16[4,64,1152]{2,1,0:T(8,128)(2,1)S(1)}, u32[]{:S(2)}, u32[]{:S(2)}) async-start(bf16[4,64,1152]{2,1,0:T(8,128)(2,1)} %bitcast.68), calls=%async_computation.2 | async-start | bytes 1179648 | tf_op jit(solution)/shard_map/all_to_all | solution.py:1269
  185.2 157.0 %reduce-scatter.3.cloned.1.call-start = ((), (), s32[]{:S(2)}) async-start(), calls=%async_computation.9 | async-start | bytes 15925248 | tf_op jit(solution)/shard_map/reduce_scatter | solution.py:1351
  196.9 0.8 copy-start.9
  236.8 1.1 copy-start.10
  254.3 5.5 %copy-start = (f32[256,1152]{1,0:T(8,128)S(1)}, f32[256,1152]{1,0:T(8,128)}, u32[]{:S(2)}) copy-start(f32[256,1152]{1,0:T(8,128)} %get-tuple-element.142.first_ref) | copy-start | bytes 3538948
  254.3 87.9 %all-to-all-start.4 = ((bf16[4,128,1152]{2,1,0:T(8,128)(2,1)}), bf16[4,128,1152]{2,1,0:T(8,128)(2,1)S(1)}, u32[]{:S(2)}, u32[]{:S(2)}) async-start(bf16[4,128,1152]{2,1,0:T(8,128)(2,1)} %get-tuple-element.163), calls=%async_computation.4 | async-start | bytes 2359296 | tf_op jit(solution)/shard_map/all_to_all | solution.py:1269
  259.5 125.0 %reduce-scatter.5.cloned.1.call-start = ((), (), s32[]{:S(2)}) async-start(), calls=%async_computation.10 | async-start | bytes 5971968 | tf_op jit(solution)/shard_map/reduce_scatter | solution.py:1374
  259.7 1.1 copy-start.16
  342.2 1.0 copy-start.1
  342.2 1.9 copy-start.5
  345.5 6.6 %copy-start.8 = (f32[1152,128]{1,0:T(8,128)S(1)}, f32[1152,128]{1,0:T(8,128)}, u32[]{:S(2)}) copy-start(f32[1152,128]{1,0:T(8,128)} %get-tuple-element.190) | copy-start | bytes 1769476
  345.5 42.6 %all-to-all-start.5 = ((bf16[4,96,1152]{2,1,0:T(8,128)(2,1)}), bf16[4,96,1152]{2,1,0:T(8,128)(2,1)S(1)}, u32[]{:S(2)}, u32[]{:S(2)}) async-start(bf16[4,96,1152]{2,1,0:T(8,128)(2,1)} %get-tuple-element.217), calls=%async_computation.7 | async-start | bytes 1769472 | tf_op jit(solution)/shard_map/all_to_all | solution.py:1269
  362.7 9.8 %collective-permute-start = (f32[8,2304]{1,0:T(8,128)}, f32[8,2304]{1,0:T(8,128)S(1)}, u32[]{:S(2)}, u32[]{:S(2)}) collective-permute-start(f32[8,2304]{1,0:T(8,128)} %get-tuple-element.176), channel_id=1, source_target_pairs={{1,0},{2,1},{3,2},{5,4},{6,5},{7,6},{9,8},{10,9},{11,10},{13,12},{... | collective-permute-start | bytes 221192 | tf_op jit(solution)/shard_map/ppermute | solution.py:1254
  372.5 0.6 copy-start.11
  373.1 10.6 %copy-start.14 = (f32[1152]{0:T(1024)S(1)}, f32[1152]{0:T(1024)}, u32[]{:S(2)}) copy-start(f32[1152]{0:T(1024)} %get-tuple-element.212) | copy-start | bytes 13828
  388.1 78.5 %copy-start.3 = (bf16[4,96,1152]{2,1,0:T(8,128)(2,1)}, bf16[4,96,1152]{2,1,0:T(8,128)(2,1)S(1)}, u32[]{:S(2)}) copy-start(bf16[4,96,1152]{2,1,0:T(8,128)(2,1)S(1)} %all-to-all-done.5.up_ref) | copy-start | bytes 2654212
  466.6 4.8 %copy-start.7 = (f32[144,1152]{1,0:T(8,128)S(1)}, f32[144,1152]{1,0:T(8,128)}, u32[]{:S(2)}) copy-start(f32[144,1152]{1,0:T(8,128)} %get-tuple-element.247) | copy-start | bytes 1990660
Sparse Core Ops, SparseCore 0:
  10.9 85.8 all-gather.5
  99.5 45.4 all-gather.7
  146.6 42.2 all-gather.9
  237.0 78.3 reduce-scatter.2
  342.4 37.0 reduce-scatter.4
